TPU v7x, 32 devices: a whole 2x2x4 slice. The times are simulated.
32 devices in a mesh: fsdp: 4 (over y, x), ctx: 8 (over z, core).
Axes of the slice: x: 2, y: 2, z: 4, core: 2. Of those that a mesh axis runs over, the one named last changes fastest.
Arguments:
- hidden_in: bfloat16 [8, 1024, 2048], P('fsdp', 'ctx'), may hold values from -6 to 6
- positions: int32 [8, 1024], P('fsdp', 'ctx'), may hold values from 0 to 1023, as said below
- cotangent: bfloat16 [8, 1024, 2048], P('fsdp', 'ctx'), may hold values from -6 to 6
- norm_gain: bfloat16 [2048], P('fsdp'), may hold values from 0.5 to 1.5
- w_query: bfloat16 [2048, 2048], P('fsdp'), may hold values from -0.125 to 0.125
- w_key: bfloat16 [2048, 256], P('fsdp'), may hold values from -0.125 to 0.125
- w_value: bfloat16 [2048, 256], P('fsdp'), may hold values from -0.125 to 0.125
- w_out: bfloat16 [2048, 2048], P('fsdp'), may hold values from -2 to 2
- ffn_gain: bfloat16 [2048], P('fsdp'), may hold values from 0.5 to 1.5
- w_gate: bfloat16 [2048, 5632], P('fsdp'), may hold values from -0.125 to 0.125
- w_up: bfloat16 [2048, 5632], P('fsdp'), may hold values from -0.125 to 0.125
- w_down: bfloat16 [5632, 2048], P('fsdp'), may hold values from -0.078125 to 0.078125
Outputs:
- output: bfloat16 [8, 1024, 2048], P('fsdp', 'ctx')
- grad_in: float32 [8, 1024, 2048], P('fsdp', 'ctx')
- grad_norm_gain: float32 [2048], P('fsdp')
- grad_query: float32 [2048, 2048], P('fsdp')
- grad_key: float32 [2048, 256], P('fsdp')
- grad_value: float32 [2048, 256], P('fsdp')
- grad_out: float32 [2048, 2048], P('fsdp')
- grad_ffn_gain: float32 [2048], P('fsdp')
- grad_gate: float32 [2048, 5632], P('fsdp')
- grad_up: float32 [2048, 5632], P('fsdp')
- grad_down: float32 [5632, 2048], P('fsdp')
Inputs may be any that keep to these rules, and one draw needn't show every extreme that they name: In each sequence, the 128 tokens that one device of ctx holds are consecutive positions in increasing order, starting at a multiple of 128; the devices of ctx hold different such runs, in an order drawn for each sequence.
All inputs are finite; a program needn't handle non-finite values.
Results may differ from a plain program's by a relative error of at most 0.023.
Values may be sent and summed in bfloat16 or wider, within the bound.
No kernel may reach another device: no remote copies, remote signals or barrier semaphores. Data moves between devices by JAX's collectives and lax.ppermute only.
A program may use at most 704 MiB of HBM per device.

v0:
```python
import jax
import jax.numpy as jnp
from jax import lax
from jax.sharding import PartitionSpec as P

H = 32
KVH = 4
HD = 64


NORM_EPS = 1e-05
MASKED = -1e30


def rms_scale(inputs):
    return lax.rsqrt(jnp.mean(inputs * inputs, -1, keepdims=True) + NORM_EPS)


def rope_table(positions):
    half_width = HD // 2
    spread = 10000.0 ** (-jnp.arange(half_width, dtype=jnp.float32) / half_width)
    turned = positions.astype(jnp.float32)[..., None] * spread
    return (jnp.cos(turned)[..., None, :], jnp.sin(turned)[..., None, :])


def rotate(inputs, cosine, sine_table):
    half_width = inputs.shape[-1] // 2
    first_half = inputs[..., :half_width]
    second_half = inputs[..., half_width:]
    return jnp.concatenate(
        [
            first_half * cosine - second_half * sine_table,
            first_half * sine_table + second_half * cosine,
        ],
        -1,
    )


def norm_back(grad_normed, inputs, row_scale, gain_row):
    scaled_grad = grad_normed * gain_row
    grad_gain = jnp.sum(grad_normed * inputs * row_scale, 0)
    grad_inputs = row_scale * scaled_grad - inputs * row_scale**3 * jnp.mean(
        scaled_grad * inputs, -1, keepdims=True
    )
    return (grad_inputs, grad_gain)


def item_scores(queries, key_rows, query_pos, key_pos):
    score_scale = queries.shape[-1] ** (-0.5)
    scores = (
        jnp.einsum("tgd,nd->gtn", queries, key_rows, preferred_element_type=jnp.float32)
        * score_scale
    )
    allowed = key_pos[None, None, :] <= query_pos[None, :, None]
    return jnp.where(allowed, scores, MASKED)


def attend_item(operands):
    queries, key_rows, values, query_pos, key_pos = operands
    scores = item_scores(queries, key_rows, query_pos, key_pos)
    row_top = jnp.max(scores, -1, keepdims=True)
    weights = jnp.exp(scores - row_top)
    row_total = jnp.sum(weights, -1, keepdims=True)
    shares = weights / row_total
    mixture = jnp.einsum(
        "gtn,nd->tgd", shares.astype(jnp.bfloat16), values, preferred_element_type=jnp.float32
    )
    return (mixture, (row_top + jnp.log(row_total))[..., 0])


def attend_back_item(operands):
    queries, key_rows, values, query_pos, key_pos, log_total, grad_mixture = operands
    score_scale = queries.shape[-1] ** (-0.5)
    scores = item_scores(queries, key_rows, query_pos, key_pos)
    shares = jnp.exp(scores - log_total[..., None])
    grad_shares = jnp.einsum(
        "tgd,nd->gtn", grad_mixture, values, preferred_element_type=jnp.float32
    )
    inner_sum = jnp.sum(shares * grad_shares, -1, keepdims=True)
    grad_scores = (shares * (grad_shares - inner_sum)).astype(jnp.bfloat16)
    grad_queries = (
        jnp.einsum("gtn,nd->tgd", grad_scores, key_rows, preferred_element_type=jnp.float32)
        * score_scale
    )
    grad_keys = (
        jnp.einsum("gtn,tgd->nd", grad_scores, queries, preferred_element_type=jnp.float32)
        * score_scale
    )
    grad_values = jnp.einsum(
        "gtn,tgd->nd", shares.astype(jnp.bfloat16), grad_mixture, preferred_element_type=jnp.float32
    )
    return (grad_queries, grad_keys, grad_values)


def to_items(array, seq_count, tok_count, group_size):
    shaped = array.reshape(seq_count, tok_count, KVH, group_size, HD).transpose(0, 2, 1, 3, 4)
    return shaped.reshape(seq_count * KVH, tok_count, group_size, HD)


def from_items(array, seq_count, tok_count, group_size):
    shaped = array.reshape(seq_count, KVH, tok_count, group_size, HD).transpose(0, 2, 1, 3, 4)
    return shaped.reshape(seq_count, tok_count, H, HD)


def on_device(
    hidden_in,
    positions,
    cotangent,
    norm_gain,
    w_query,
    w_key,
    w_value,
    w_out,
    ffn_gain,
    w_gate,
    w_up,
    w_down,
):
    seq_count, tok_count, model_width = hidden_in.shape
    row_count = seq_count * tok_count
    group_size = H // KVH
    gain_one, query_w, key_w, value_w, out_w = (
        lax.all_gather(norm_gain, "fsdp", axis=0, tiled=True),
        lax.all_gather(w_query, "fsdp", axis=0, tiled=True),
        lax.all_gather(w_key, "fsdp", axis=0, tiled=True),
        lax.all_gather(w_value, "fsdp", axis=0, tiled=True),
        lax.all_gather(w_out, "fsdp", axis=0, tiled=True),
    )
    inputs = hidden_in.astype(jnp.float32).reshape(row_count, model_width)
    scale_one = rms_scale(inputs)
    normed_one = (inputs * scale_one * gain_one.astype(jnp.float32)).astype(jnp.bfloat16)
    query_raw = jnp.dot(normed_one, query_w, preferred_element_type=jnp.float32).reshape(
        seq_count, tok_count, H, HD
    )
    key_raw = jnp.dot(normed_one, key_w, preferred_element_type=jnp.float32).reshape(
        seq_count, tok_count, KVH, HD
    )
    values_low = (
        jnp.dot(normed_one, value_w, preferred_element_type=jnp.float32)
        .astype(jnp.bfloat16)
        .reshape(seq_count, tok_count, KVH * HD)
    )
    cosine, sine_table = rope_table(positions)
    query_low = rotate(query_raw, cosine, sine_table).astype(jnp.bfloat16)
    keys_low = (
        rotate(key_raw, cosine, sine_table)
        .astype(jnp.bfloat16)
        .reshape(seq_count, tok_count, KVH * HD)
    )
    all_keys, all_values, all_pos = (
        lax.all_gather(keys_low, "ctx", axis=1, tiled=True),
        lax.all_gather(values_low, "ctx", axis=1, tiled=True),
        lax.all_gather(positions, "ctx", axis=1, tiled=True),
    )
    full_len = all_keys.shape[1]
    item_query = to_items(query_low, seq_count, tok_count, group_size)
    item_keys = (
        all_keys.reshape(seq_count, full_len, KVH, HD)
        .transpose(0, 2, 1, 3)
        .reshape(seq_count * KVH, full_len, HD)
    )
    item_values = (
        all_values.reshape(seq_count, full_len, KVH, HD)
        .transpose(0, 2, 1, 3)
        .reshape(seq_count * KVH, full_len, HD)
    )
    item_qpos = jnp.repeat(positions, KVH, axis=0)
    item_kpos = jnp.repeat(all_pos, KVH, axis=0)
    mixture_items, log_total = lax.map(
        attend_item, (item_query, item_keys, item_values, item_qpos, item_kpos)
    )
    attended = (
        from_items(mixture_items, seq_count, tok_count, group_size)
        .reshape(row_count, H * HD)
        .astype(jnp.bfloat16)
    )
    residual = inputs + jnp.dot(attended, out_w, preferred_element_type=jnp.float32)
    gain_two, gate_w, up_w, down_w = (
        lax.all_gather(ffn_gain, "fsdp", axis=0, tiled=True),
        lax.all_gather(w_gate, "fsdp", axis=0, tiled=True),
        lax.all_gather(w_up, "fsdp", axis=0, tiled=True),
        lax.all_gather(w_down, "fsdp", axis=0, tiled=True),
    )
    scale_two = rms_scale(residual)
    normed_two = (residual * scale_two * gain_two.astype(jnp.float32)).astype(jnp.bfloat16)
    gate_proj = jnp.dot(normed_two, gate_w, preferred_element_type=jnp.float32)
    up_proj = jnp.dot(normed_two, up_w, preferred_element_type=jnp.float32)
    sigmoid_gate = jax.nn.sigmoid(gate_proj)
    hidden_low = (gate_proj * sigmoid_gate * up_proj).astype(jnp.bfloat16)
    mixed_out = jnp.dot(hidden_low, down_w, preferred_element_type=jnp.float32)
    output = (residual + mixed_out).astype(jnp.bfloat16).reshape(seq_count, tok_count, model_width)
    gain_two, gate_w, up_w, down_w = (
        lax.all_gather(ffn_gain, "fsdp", axis=0, tiled=True),
        lax.all_gather(w_gate, "fsdp", axis=0, tiled=True),
        lax.all_gather(w_up, "fsdp", axis=0, tiled=True),
        lax.all_gather(w_down, "fsdp", axis=0, tiled=True),
    )
    grad_y = cotangent.astype(jnp.float32).reshape(row_count, model_width)
    grad_mixed = grad_y.astype(jnp.bfloat16)
    grad_down = jnp.dot(hidden_low.T, grad_mixed, preferred_element_type=jnp.float32)
    grad_hidden = jnp.dot(grad_mixed, down_w.T, preferred_element_type=jnp.float32)
    grad_up_in = (grad_hidden * gate_proj * sigmoid_gate).astype(jnp.bfloat16)
    grad_gate_in = (
        grad_hidden * up_proj * sigmoid_gate * (1.0 + gate_proj * (1.0 - sigmoid_gate))
    ).astype(jnp.bfloat16)
    grad_gate_w = jnp.dot(normed_two.T, grad_gate_in, preferred_element_type=jnp.float32)
    grad_up_w = jnp.dot(normed_two.T, grad_up_in, preferred_element_type=jnp.float32)
    grad_normed_two = jnp.dot(grad_gate_in, gate_w.T, preferred_element_type=jnp.float32) + jnp.dot(
        grad_up_in, up_w.T, preferred_element_type=jnp.float32
    )
    grad_res_norm, grad_gain_two = norm_back(
        grad_normed_two, residual, scale_two, gain_two.astype(jnp.float32)
    )
    grad_residual = grad_y + grad_res_norm
    part_gain_two, part_gate, part_up, part_down = (
        lax.psum_scatter(
            grad_gain_two.astype(jnp.bfloat16), "fsdp", scatter_dimension=0, tiled=True
        ).astype(jnp.float32),
        lax.psum_scatter(
            grad_gate_w.astype(jnp.bfloat16), "fsdp", scatter_dimension=0, tiled=True
        ).astype(jnp.float32),
        lax.psum_scatter(
            grad_up_w.astype(jnp.bfloat16), "fsdp", scatter_dimension=0, tiled=True
        ).astype(jnp.float32),
        lax.psum_scatter(
            grad_down.astype(jnp.bfloat16), "fsdp", scatter_dimension=0, tiled=True
        ).astype(jnp.float32),
    )
    summed_mlp = (
        lax.psum(part_gain_two.astype(jnp.bfloat16), "ctx").astype(jnp.float32),
        lax.psum(part_gate.astype(jnp.bfloat16), "ctx").astype(jnp.float32),
        lax.psum(part_up.astype(jnp.bfloat16), "ctx").astype(jnp.float32),
        lax.psum(part_down.astype(jnp.bfloat16), "ctx").astype(jnp.float32),
    )
    gain_one, query_w, key_w, value_w, out_w = (
        lax.all_gather(norm_gain, "fsdp", axis=0, tiled=True),
        lax.all_gather(w_query, "fsdp", axis=0, tiled=True),
        lax.all_gather(w_key, "fsdp", axis=0, tiled=True),
        lax.all_gather(w_value, "fsdp", axis=0, tiled=True),
        lax.all_gather(w_out, "fsdp", axis=0, tiled=True),
    )
    grad_proj = grad_residual.astype(jnp.bfloat16)
    grad_out_w = jnp.dot(attended.T, grad_proj, preferred_element_type=jnp.float32)
    grad_attended = jnp.dot(grad_proj, out_w.T, preferred_element_type=jnp.float32).astype(
        jnp.bfloat16
    )
    item_grad = to_items(grad_attended, seq_count, tok_count, group_size)
    grad_q_items, grad_k_items, grad_v_items = lax.map(
        attend_back_item,
        (item_query, item_keys, item_values, item_qpos, item_kpos, log_total, item_grad),
    )
    grad_keys_sum, grad_values_sum = (
        lax.psum_scatter(
            grad_k_items.reshape(seq_count, KVH, full_len, HD).astype(jnp.bfloat16),
            "ctx",
            scatter_dimension=2,
            tiled=True,
        ).astype(jnp.float32),
        lax.psum_scatter(
            grad_v_items.reshape(seq_count, KVH, full_len, HD).astype(jnp.bfloat16),
            "ctx",
            scatter_dimension=2,
            tiled=True,
        ).astype(jnp.float32),
    )
    grad_keys_low = (
        rotate(grad_keys_sum.transpose(0, 2, 1, 3), cosine, -sine_table)
        .astype(jnp.bfloat16)
        .reshape(row_count, KVH * HD)
    )
    grad_values_low = (
        grad_values_sum.transpose(0, 2, 1, 3).reshape(row_count, KVH * HD).astype(jnp.bfloat16)
    )
    grad_query_rot = from_items(grad_q_items, seq_count, tok_count, group_size)
    grad_query_low = (
        rotate(grad_query_rot, cosine, -sine_table).astype(jnp.bfloat16).reshape(row_count, H * HD)
    )
    grad_query_w = jnp.dot(normed_one.T, grad_query_low, preferred_element_type=jnp.float32)
    grad_key_w = jnp.dot(normed_one.T, grad_keys_low, preferred_element_type=jnp.float32)
    grad_value_w = jnp.dot(normed_one.T, grad_values_low, preferred_element_type=jnp.float32)
    grad_normed_one = (
        jnp.dot(grad_query_low, query_w.T, preferred_element_type=jnp.float32)
        + jnp.dot(grad_keys_low, key_w.T, preferred_element_type=jnp.float32)
        + jnp.dot(grad_values_low, value_w.T, preferred_element_type=jnp.float32)
    )
    grad_in_norm, grad_gain_one = norm_back(
        grad_normed_one, inputs, scale_one, gain_one.astype(jnp.float32)
    )
    grad_in = (grad_residual + grad_in_norm).reshape(seq_count, tok_count, model_width)
    part_gain_one, part_query, part_key, part_value, part_out = (
        lax.psum_scatter(
            grad_gain_one.astype(jnp.bfloat16), "fsdp", scatter_dimension=0, tiled=True
        ).astype(jnp.float32),
        lax.psum_scatter(
            grad_query_w.astype(jnp.bfloat16), "fsdp", scatter_dimension=0, tiled=True
        ).astype(jnp.float32),
        lax.psum_scatter(
            grad_key_w.astype(jnp.bfloat16), "fsdp", scatter_dimension=0, tiled=True
        ).astype(jnp.float32),
        lax.psum_scatter(
            grad_value_w.astype(jnp.bfloat16), "fsdp", scatter_dimension=0, tiled=True
        ).astype(jnp.float32),
        lax.psum_scatter(
            grad_out_w.astype(jnp.bfloat16), "fsdp", scatter_dimension=0, tiled=True
        ).astype(jnp.float32),
    )
    summed_attn = (
        lax.psum(part_gain_one.astype(jnp.bfloat16), "ctx").astype(jnp.float32),
        lax.psum(part_query.astype(jnp.bfloat16), "ctx").astype(jnp.float32),
        lax.psum(part_key.astype(jnp.bfloat16), "ctx").astype(jnp.float32),
        lax.psum(part_value.astype(jnp.bfloat16), "ctx").astype(jnp.float32),
        lax.psum(part_out.astype(jnp.bfloat16), "ctx").astype(jnp.float32),
    )
    return (
        output,
        grad_in,
        summed_attn[0],
        summed_attn[1],
        summed_attn[2],
        summed_attn[3],
        summed_attn[4],
        summed_mlp[0],
        summed_mlp[1],
        summed_mlp[2],
        summed_mlp[3],
    )


def solution(mesh):
    placed = (
        P("fsdp", "ctx", None),
        P("fsdp", "ctx"),
        P("fsdp", "ctx", None),
        P("fsdp"),
        P("fsdp", None),
        P("fsdp", None),
        P("fsdp", None),
        P("fsdp", None),
        P("fsdp"),
        P("fsdp", None),
        P("fsdp", None),
        P("fsdp", None),
    )
    return jax.shard_map(
        on_device,
        mesh=mesh,
        in_specs=placed,
        out_specs=(
            P("fsdp", "ctx", None),
            P("fsdp", "ctx", None),
            P("fsdp"),
            P("fsdp", None),
            P("fsdp", None),
            P("fsdp", None),
            P("fsdp", None),
            P("fsdp"),
            P("fsdp", None),
            P("fsdp", None),
            P("fsdp", None),
        ),
        check_vma=False,
    )
```

profile of v0, /device:TPU:0, one launch (start us, length us, event | category | flops | bytes accessed | tf_op | source)
XLA Modules:
  0.0 2655.7 jit_solution(8696935800204337764)
XLA Ops:
  22.2 17.0 all-gather.12.cloned.1.call-done
  42.9 24.8 all-gather.16.cloned.1.call-done
  102.7 19.3 all-gather.18.cloned.1.call-done
  128.0 83.2 %all-gather.20.cloned.1.call-done = bf16[2048,2048]{1,0:T(8,128)(2,1)} async-done(((bf16[512,2048]{1,0:T(8,128)(2,1)}), bf16[2048,2048]{1,0:T(8,128)(2,1)}) %all-gather.20.cloned.1.call-update) | async-done | bytes 8388624 | tf_op jit(solution)/shard_map/all_gather | solution.py:124
  233.5 37.1 %while.28 = (s32[]{:T(128)}, bf16[8,128,8,64]{1,3,2,0:T(8,128)(2,1)}, f32[8,8,128]{2,1,0:T(8,128)S(1)}, bf16[8,1024,64]{1,2,0:T(8,128)(2,1)}, s32[8,1024]{1,0:T(...) while((s32[]{:T(128)}, ...), condition=%wide.region_4.5_spmd.clone, body=%wide.region_1.4_spmd.sunk.clone | while | flops 281148416 | bytes 13811305 | solution.py:169
  274.6 25.9 all-gather.22.cloned.1.call-done
  307.0 205.9 %all-gather.24.cloned.1.call-done = bf16[2048,5632]{1,0:T(8,128)(2,1)} async-done(((bf16[512,5632]{1,0:T(8,128)(2,1)}), bf16[2048,5632]{1,0:T(8,128)(2,1)}) %all-gather.24.cloned.1.call-update) | async-done | bytes 23068688 | tf_op jit(solution)/shard_map/all_gather | solution.py:180
  512.9 14.3 fusion.104
  527.3 198.0 %all-gather.26.cloned.1.call-done = bf16[2048,5632]{1,0:T(8,128)(2,1)} async-done(((bf16[512,5632]{1,0:T(8,128)(2,1)}), bf16[2048,5632]{1,0:T(8,128)(2,1)}) %all-gather.26.cloned.1.call-update) | async-done | bytes 23068688 | tf_op jit(solution)/shard_map/all_gather | solution.py:181
  725.3 14.3 fusion.105
  739.6 198.0 %all-gather.28.cloned.1.call-done = bf16[5632,2048]{1,0:T(8,128)(2,1)} async-done(((bf16[1408,2048]{1,0:T(8,128)(2,1)}), bf16[5632,2048]{1,0:T(8,128)(2,1)}) %all-gather.28.cloned.1.call-update) | async-done | bytes 23068688 | tf_op jit(solution)/shard_map/all_gather | solution.py:182
  937.6 18.5 multiply_convert_fusion
  993.2 86.0 %while.29 = (s32[]{:T(128)}, f32[8,128,8,64]{1,3,2,0:T(8,128)}, bf16[8,1024,64]{1,2,0:T(8,128)(2,1)}, bf16[8,1024,64]{1,2,0:T(8,128)(2,1)S(1)}, bf16[8,1024,64]{...) while((s32[]{:T(128)}, f32[8,128,8,64]{1,3,2,0:T(8,128)}, ...), condition=%wide.region_9.10_spmd.clone, body=%wide.region_7.9_spmd.sunk.clone | while | flops 687078400 | bytes 33733248 | solution.py:248
  1084.3 103.4 %copy.119 = bf16[2,4,1024,64]{0,3,1,2:T(8,128)(2,1)} copy(bf16[2,4,1024,64]{2,3,1,0:T(8,128)(2,1)S(1)} %bitcast.391) | data formatting | bytes 2097152
  1187.7 97.3 %reshape.353 = bf16[1024,512]{1,0:T(8,128)(2,1)} reshape(bf16[1024,4,64,2]{3,2,1,0:T(8,128)(2,1)} %bitcast.65) | data formatting | bytes 2097152
  1288.3 29.4 %reduce-scatter.30.cloned.1.call-done = bf16[128,512]{1,0:T(8,128)(2,1)} async-done(((bf16[1024,512]{1,0:T(8,128)(2,1)}), bf16[128,512]{1,0:T(8,128)(2,1)}) %reduce-scatter.30.cloned.1.call-update) | async-done | bytes 131088
  1317.7 19.9 reshape.354
  1408.8 58.4 %reduce-scatter.14.cloned.1.call-done = bf16[512,2048]{1,0:T(8,128)(2,1)} async-done(((bf16[2048,2048]{1,0:T(8,128)(2,1)}), bf16[512,2048]{1,0:T(8,128)(2,1)}) %reduce-scatter.14.cloned.1.call-update) | async-done | bytes 2097168 | tf_op jit(solution)/shard_map/reduce_scatter | solution.py:294
  1467.1 90.2 %reduce-scatter.20.cloned.1.call-done = bf16[512,2048]{1,0:T(8,128)(2,1)} async-done(((bf16[2048,2048]{1,0:T(8,128)(2,1)}), bf16[512,2048]{1,0:T(8,128)(2,1)}) %reduce-scatter.20.cloned.1.call-update) | async-done | bytes 2097168 | tf_op jit(solution)/shard_map/reduce_scatter | solution.py:303
  1557.4 207.8 %reduce-scatter.22.cloned.1.call-done = bf16[512,5632]{1,0:T(8,128)(2,1)} async-done(((bf16[2048,5632]{1,0:T(8,128)(2,1)}), bf16[512,5632]{1,0:T(8,128)(2,1)}) %reduce-scatter.22.cloned.1.call-update) | async-done | bytes 5767184 | tf_op jit(solution)/shard_map/reduce_scatter | solution.py:219
  1765.2 208.1 %reduce-scatter.24.cloned.1.call-done = bf16[512,5632]{1,0:T(8,128)(2,1)} async-done(((bf16[2048,5632]{1,0:T(8,128)(2,1)}), bf16[512,5632]{1,0:T(8,128)(2,1)}) %reduce-scatter.24.cloned.1.call-update) | async-done | bytes 5767184 | tf_op jit(solution)/shard_map/reduce_scatter | solution.py:222
  1973.3 207.8 %reduce-scatter.26.cloned.1.call-done = bf16[1408,2048]{1,0:T(8,128)(2,1)} async-done(((bf16[5632,2048]{1,0:T(8,128)(2,1)}), bf16[1408,2048]{1,0:T(8,128)(2,1)}) %reduce-scatter.26.cloned.1.call-update) | async-done | bytes 5767184 | tf_op jit(solution)/shard_map/reduce_scatter | solution.py:225
  2215.5 15.6 all-reduce.2
  2235.7 385.2 %all-reduce.7.cloned.1.call-done = (bf16[512,2048]{1,0:T(8,128)(2,1)}, bf16[512,256]{1,0:T(8,128)(2,1)}, bf16[512,256]{1,0:T(8,128)(2,1)}, bf16[512,2048]{1,0:T(...) async-done(((bf16[512,2048]{1,0:T(8,128)(2,1)}, bf16[512,256]{1,0:T(8,128)(2,1)}, bf16[512,256]{1,0:T(8,128)(2,1)}, ...) | async-done | bytes 22020112 | tf_op jit(solution)/shard_map/psum | solution.py:309
  (362 shorter events, 396.3 us)
Async XLA Ops:
  7.2 32.0 %all-gather.12.cloned.1.call-start = ((), (), s32[]{:S(2)}) async-start(), calls=%async_computation.9 | async-start | bytes 1310720 | tf_op jit(solution)/shard_map/all_gather | solution.py:126
  7.9 59.8 %all-gather.16.cloned.1.call-start = ((), (), s32[]{:S(2)}) async-start(), calls=%async_computation.11 | async-start | bytes 1310720 | tf_op jit(solution)/shard_map/all_gather | solution.py:125
  8.7 87.0 %all-gather.14.cloned.1.call-start = ((), (), s32[]{:S(2)}) async-start(), calls=%async_computation.10 | async-start | bytes 1179648 | tf_op jit(solution)/shard_map/all_gather | solution.py:152
  41.7 80.3 %all-gather.18.cloned.1.call-start = ((), (), s32[]{:S(2)}) async-start(), calls=%async_computation.12 | async-start | bytes 1179648 | tf_op jit(solution)/shard_map/all_gather | solution.py:151
  42.6 186.3 %copy-start.24 = (f32[2,128,32]{1,2,0:T(8,128)}, f32[2,128,32]{1,2,0:T(8,128)S(1)}, u32[]{:S(2)}) copy-start(f32[2,128,32]{1,2,0:T(8,128)S(1)} %get-tuple-element.275) | copy-start | bytes 98308
  42.9 180.6 %copy-start.2 = (bf16[2,128,2048]{2,1,0:T(8,128)(2,1)}, bf16[2,128,2048]{2,1,0:T(8,128)(2,1)S(1)}, u32[]{:S(2)}) copy-start(bf16[2,128,2048]{2,1,0:T(8,128)(2,1)S(1)} %fusion.64) | copy-start | bytes 3145732
  70.6 140.7 %all-gather.20.cloned.1.call-start = ((), (), s32[]{:S(2)}) async-start(), calls=%async_computation.13 | async-start | bytes 10485760 | tf_op jit(solution)/shard_map/all_gather | solution.py:124
  71.2 229.4 %all-gather.22.cloned.1.call-start = ((), (), s32[]{:S(2)}) async-start(), calls=%async_computation.14 | async-start | bytes 10485760 | tf_op jit(solution)/shard_map/all_gather | solution.py:127
  71.7 441.2 %all-gather.24.cloned.1.call-start = ((), (), s32[]{:S(2)}) async-start(), calls=%async_computation.15 | async-start | bytes 28835840 | tf_op jit(solution)/shard_map/all_gather | solution.py:180
  72.5 652.8 %all-gather.26.cloned.1.call-start = ((), (), s32[]{:S(2)}) async-start(), calls=%async_computation.16 | async-start | bytes 28835840 | tf_op jit(solution)/shard_map/all_gather | solution.py:181
  73.2 864.4 %all-gather.28.cloned.1.call-start = ((), (), s32[]{:S(2)}) async-start(), calls=%async_computation.17 | async-start | bytes 28835840 | tf_op jit(solution)/shard_map/all_gather | solution.py:182
  74.0 1211.2 %reduce-scatter.28.cloned.1.call-start = ((), (), s32[]{:S(2)}) async-start(), calls=%async_computation.25 | async-start | bytes 1179648
  306.7 675.9 %copy-start.4 = (f32[256,2048]{1,0:T(8,128)}, f32[256,2048]{1,0:T(8,128)S(1)}, u32[]{:S(2)}) copy-start(f32[256,2048]{1,0:T(8,128)S(1)} %get-tuple-element.281) | copy-start | bytes 6291460
  307.0 418.3 %copy-start.9 = (bf16[256,2048]{1,0:T(8,128)(2,1)}, bf16[256,2048]{1,0:T(8,128)(2,1)S(1)}, u32[]{:S(2)}) copy-start(bf16[256,2048]{1,0:T(8,128)(2,1)S(1)} %multiply_convert_fusion.3) | copy-start | bytes 3145732
  1084.3 233.5 %reduce-scatter.30.cloned.1.call-start = ((), (), s32[]{:S(2)}) async-start(), calls=%async_computation.26 | async-start | bytes 1179648
  1187.7 98.8 %copy-start.26 = (f32[2,128,32]{1,2,0:T(8,128)S(1)}, f32[2,128,32]{1,2,0:T(8,128)}, u32[]{:S(2)}) copy-start(f32[2,128,32]{1,2,0:T(8,128)} %get-tuple-element.273) | copy-start | bytes 98308
  1285.1 123.7 %reduce-scatter.16.cloned.1.call-start = ((), (), s32[]{:S(2)}) async-start(), calls=%async_computation.19 | async-start | bytes 1310720 | tf_op jit(solution)/shard_map/reduce_scatter | solution.py:297
  1288.3 120.5 %reduce-scatter.18.cloned.1.call-start = ((), (), s32[]{:S(2)}) async-start(), calls=%async_computation.20 | async-start | bytes 1310720 | tf_op jit(solution)/shard_map/reduce_scatter | solution.py:300
  1350.3 116.9 %reduce-scatter.14.cloned.1.call-start = ((), (), s32[]{:S(2)}) async-start(), calls=%async_computation.18 | async-start | bytes 10485760 | tf_op jit(solution)/shard_map/reduce_scatter | solution.py:294
  1358.9 198.4 %reduce-scatter.20.cloned.1.call-start = ((), (), s32[]{:S(2)}) async-start(), calls=%async_computation.21 | async-start | bytes 10485760 | tf_op jit(solution)/shard_map/reduce_scatter | solution.py:303
  1366.6 398.6 %reduce-scatter.22.cloned.1.call-start = ((), (), s32[]{:S(2)}) async-start(), calls=%async_computation.22 | async-start | bytes 28835840 | tf_op jit(solution)/shard_map/reduce_scatter | solution.py:219
  1380.8 592.5 %reduce-scatter.24.cloned.1.call-start = ((), (), s32[]{:S(2)}) async-start(), calls=%async_computation.23 | async-start | bytes 28835840 | tf_op jit(solution)/shard_map/reduce_scatter | solution.py:222
  1394.1 787.0 %reduce-scatter.26.cloned.1.call-start = ((), (), s32[]{:S(2)}) async-start(), calls=%async_computation.24 | async-start | bytes 28835840 | tf_op jit(solution)/shard_map/reduce_scatter | solution.py:225
  1408.7 1212.3 %all-reduce.7.cloned.1.call-start = ((), (), s32[]{:S(2)}) async-start(), calls=%async_computation.27 | async-start | bytes 44040192 | tf_op jit(solution)/shard_map/psum | solution.py:309
  (38 other events, 363.0 us)
Sparse Core Ops, SparseCore 0:
  9.9 29.3 all-gather.11
  41.1 26.6 all-gather.15
  69.9 24.9 all-gather.13
  96.9 24.9 all-gather.17
  123.6 87.5 all-gather.19
  212.9 87.5 all-gather.21
  302.4 210.4 all-gather.23
  514.8 210.4 all-gather.25
  727.1 210.4 all-gather.27
  1084.4 32.4 reduce-scatter.27
  1285.2 32.4 reduce-scatter.29
  1320.5 25.8 reduce-scatter.15
  1350.4 26.7 reduce-scatter.17
  1380.7 86.3 reduce-scatter.13
  1470.9 86.4 reduce-scatter.19
  1560.3 204.8 reduce-scatter.21
  1768.4 204.8 reduce-scatter.23
  1976.3 204.8 reduce-scatter.25
  2184.9 435.9 all-reduce.6
where the time goes:
time: 2660 us
  waiting for transfers between devices  1960 us (74%)
  local copies, waits for them, and re-layouts  286 us (11%)
  matrix products  271 us (10%)
  other arithmetic  62 us (2%)
  blocking collectives  54.4 us (2%)
    psum x1, waiting for transfers between devices, on_device(): lax.psum(part_query.astype(jnp.bfloat16), 'ctx').astype(jnp.float32)  385 us
    unnamed x99, local copies, waits for them, and re-layouts  250 us
    reduce_scatter x1, waiting for transfers between devices, on_device(): lax.psum_scatter(grad_up_w.astype(jnp.bfloat16), 'fsdp', scatter_dimensio...  208 us
    reduce_scatter x1, waiting for transfers between devices, on_device(): lax.psum_scatter(grad_gate_w.astype(jnp.bfloat16), 'fsdp', scatter_dimens...  208 us
    reduce_scatter x1, waiting for transfers between devices, on_device(): lax.psum_scatter(grad_down.astype(jnp.bfloat16), 'fsdp', scatter_dimensio...  208 us
    all_gather x1, waiting for transfers between devices, on_device(): lax.all_gather(w_gate, 'fsdp', axis=0, tiled=True)  206 us
    all_gather x1, waiting for transfers between devices, on_device(): lax.all_gather(w_down, 'fsdp', axis=0, tiled=True)  198 us
    all_gather x1, waiting for transfers between devices, on_device(): lax.all_gather(w_up, 'fsdp', axis=0, tiled=True)  198 us
  transfers between devices with their start and end apart: 19, of which 15 were waited for; matrix products, arithmetic and copies ran while one was open for 17% of the time, Pallas kernels for 0%

commit v1 on v0

v1 whole, which is shorter than its diff:
```python
import jax
import jax.numpy as jnp
from jax import lax
from jax.sharding import PartitionSpec as P

H = 32
KVH = 4
HD = 64


NORM_EPS = 1e-05
MASKED = -1e30


def rms_scale(inputs):
    return lax.rsqrt(jnp.mean(inputs * inputs, -1, keepdims=True) + NORM_EPS)


def rope_table(positions):
    half_width = HD // 2
    spread = 10000.0 ** (-jnp.arange(half_width, dtype=jnp.float32) / half_width)
    turned = positions.astype(jnp.float32)[..., None] * spread
    return (jnp.cos(turned)[..., None, :], jnp.sin(turned)[..., None, :])


def rotate(inputs, cosine, sine_table):
    half_width = inputs.shape[-1] // 2
    first_half = inputs[..., :half_width]
    second_half = inputs[..., half_width:]
    return jnp.concatenate(
        [
            first_half * cosine - second_half * sine_table,
            first_half * sine_table + second_half * cosine,
        ],
        -1,
    )


def norm_back(grad_normed, inputs, row_scale, gain_row):
    scaled_grad = grad_normed * gain_row
    grad_gain = jnp.sum(grad_normed * inputs * row_scale, 0)
    grad_inputs = row_scale * scaled_grad - inputs * row_scale**3 * jnp.mean(
        scaled_grad * inputs, -1, keepdims=True
    )
    return (grad_inputs, grad_gain)


def item_scores(queries, key_rows, query_pos, key_pos):
    score_scale = queries.shape[-1] ** (-0.5)
    scores = (
        jnp.einsum("tgd,nd->gtn", queries, key_rows, preferred_element_type=jnp.float32)
        * score_scale
    )
    allowed = key_pos[None, None, :] <= query_pos[None, :, None]
    return jnp.where(allowed, scores, MASKED)


def attend_item(operands):
    queries, key_rows, values, query_pos, key_pos = operands
    scores = item_scores(queries, key_rows, query_pos, key_pos)
    row_top = jnp.max(scores, -1, keepdims=True)
    weights = jnp.exp(scores - row_top)
    row_total = jnp.sum(weights, -1, keepdims=True)
    shares = weights / row_total
    mixture = jnp.einsum(
        "gtn,nd->tgd", shares.astype(jnp.bfloat16), values, preferred_element_type=jnp.float32
    )
    return (mixture, (row_top + jnp.log(row_total))[..., 0])


def attend_back_item(operands):
    queries, key_rows, values, query_pos, key_pos, log_total, grad_mixture = operands
    score_scale = queries.shape[-1] ** (-0.5)
    scores = item_scores(queries, key_rows, query_pos, key_pos)
    shares = jnp.exp(scores - log_total[..., None])
    grad_shares = jnp.einsum(
        "tgd,nd->gtn", grad_mixture, values, preferred_element_type=jnp.float32
    )
    inner_sum = jnp.sum(shares * grad_shares, -1, keepdims=True)
    grad_scores = (shares * (grad_shares - inner_sum)).astype(jnp.bfloat16)
    grad_queries = (
        jnp.einsum("gtn,nd->tgd", grad_scores, key_rows, preferred_element_type=jnp.float32)
        * score_scale
    )
    grad_keys = (
        jnp.einsum("gtn,tgd->nd", grad_scores, queries, preferred_element_type=jnp.float32)
        * score_scale
    )
    grad_values = jnp.einsum(
        "gtn,tgd->nd", shares.astype(jnp.bfloat16), grad_mixture, preferred_element_type=jnp.float32
    )
    return (grad_queries, grad_keys, grad_values)


def to_items(array, seq_count, tok_count, group_size):
    shaped = array.reshape(seq_count, tok_count, KVH, group_size, HD).transpose(0, 2, 1, 3, 4)
    return shaped.reshape(seq_count * KVH, tok_count, group_size, HD)


def from_items(array, seq_count, tok_count, group_size):
    shaped = array.reshape(seq_count, KVH, tok_count, group_size, HD).transpose(0, 2, 1, 3, 4)
    return shaped.reshape(seq_count, tok_count, H, HD)


def at(array, start, size, axis=0):
    return lax.dynamic_slice_in_dim(array, start, size, axis)


def on_device(
    hidden_in,
    positions,
    cotangent,
    norm_gain,
    w_query,
    w_key,
    w_value,
    w_out,
    ffn_gain,
    w_gate,
    w_up,
    w_down,
):
    bf, f32 = jnp.bfloat16, jnp.float32
    seq_count, tok_count, model_width = hidden_in.shape
    row_count = seq_count * tok_count
    group_size = H // KVH
    parts = lax.axis_size("fsdp")
    runs = lax.axis_size("ctx")
    levels = runs // 2
    mine = lax.axis_index("fsdp")
    run = lax.axis_index("ctx")
    core = lax.rem(run, 2)
    level = run // 2
    shard = model_width // parts
    ff_part = w_down.shape[0]

    def hop(array, bit):
        return lax.ppermute(array, "fsdp", [(i, i ^ bit) for i in range(parts)])

    def swap_core(array):
        return lax.ppermute(array, "ctx", [(i, i ^ 1) for i in range(runs)])

    def level_send(array, pairs):
        return lax.ppermute(
            array, "ctx", [(2 * a + k, 2 * b + k) for a, b in pairs for k in range(2)]
        )

    def spread(local):
        if parts != 4:
            return [hop(local, bit) for bit in range(1, parts)]
        half = local.shape[0] // 2
        from_x, from_y = hop(local, 1), hop(local, 2)
        return [from_x, from_y, hop(from_x[:half], 2), hop(from_y[half:], 1)]

    def gather_rows(local):
        rows, cols = local.shape
        half = rows // 2
        own = at(local, core * half, half)
        got = jnp.concatenate(spread(own), 0)
        other = swap_core(got)
        whole = jnp.zeros((parts, 2, half, cols), local.dtype)
        whole = lax.dynamic_update_slice(
            whole, local.reshape(1, 2, half, cols), (mine, 0, 0, 0)
        )
        for step in range(1, parts):
            for source, side in ((got, core), (other, 1 - core)):
                piece = source[(step - 1) * half : step * half].reshape(1, 1, half, cols)
                whole = lax.dynamic_update_slice(whole, piece, (mine ^ step, side, 0, 0))
        return whole.reshape(parts * rows, cols)

    def gather_columns(locals_, cols):
        rows = locals_[0].shape[0]
        half = rows // 2

        def block(index, start, size):
            return jnp.concatenate(
                [
                    lax.dynamic_slice(a, (start, index * cols), (size, cols))
                    for a in locals_
                ],
                1,
            )

        width = cols * len(locals_)
        got = jnp.concatenate(
            [hop(block(mine ^ bit, core * half, half), bit) for bit in range(1, parts)],
            0,
        )
        other = swap_core(got)
        whole = jnp.zeros((parts, 2, half, width), locals_[0].dtype)
        whole = lax.dynamic_update_slice(
            whole, block(mine, 0, rows).reshape(1, 2, half, width), (mine, 0, 0, 0)
        )
        for step in range(1, parts):
            for source, side in ((got, core), (other, 1 - core)):
                piece = source[(step - 1) * half : step * half].reshape(1, 1, half, width)
                whole = lax.dynamic_update_slice(whole, piece, (mine ^ step, side, 0, 0))
        return whole.reshape(parts * rows, width)

    def gather_tokens(local):
        return jnp.concatenate([local] + spread(local), 0)

    def sum_blocks(blocks):
        if parts != 4:
            return sum(
                [hop(blocks[bit], bit).astype(f32) for bit in range(1, parts)],
                blocks[0].astype(f32),
            )
        half = blocks[0].shape[0] // 2
        low_part = hop(blocks[3][half:], 1)
        top_part = hop(blocks[3][:half], 2)
        add = lambda a, b: (a.astype(f32) + b.astype(f32)).astype(bf)
        to_x = jnp.concatenate([add(blocks[1][:half], top_part), blocks[1][half:]], 0)
        to_y = jnp.concatenate([blocks[2][:half], add(blocks[2][half:], low_part)], 0)
        from_x, from_y = hop(to_x, 1), hop(to_y, 2)
        return blocks[0].astype(f32) + from_x.astype(f32) + from_y.astype(f32)

    def sum_levels(local):
        add = lambda a, b: (a.astype(f32) + b.astype(f32)).astype(bf)
        middle = levels // 2
        last = levels - 1
        total = local
        for step in range(middle - 1):
            total = add(
                total, level_send(total, [(step, step + 1), (last - step, last - step - 1)])
            )
        total = add(total, level_send(total, [(middle - 1, middle), (middle, middle - 1)]))
        for step in reversed(range(middle - 1)):
            got = level_send(total, [(step + 1, step), (last - step - 1, last - step)])
            total = jnp.where((level == step) | (level == last - step), got, total)
        return total

    def both_halves(local, axis=0):
        other = swap_core(local)
        first = jnp.where(core == 0, local, other)
        second = jnp.where(core == 0, other, local)
        return jnp.concatenate([first, second], axis).astype(f32)

    def pair_sum(array, axis):
        size = array.shape[axis] // 2
        got = swap_core(at(array, (1 - core) * size, size, axis))
        kept = at(array, core * size, size, axis)
        return (kept.astype(f32) + got.astype(f32)).astype(bf)

    def reduce_rows(partial):
        cols = partial.shape[1]
        half = shard // 2
        split = pair_sum(partial.reshape(parts, shard, cols), 1)
        blocks = [at(split, mine ^ step, 1).reshape(half, cols) for step in range(parts)]
        return both_halves(sum_levels(sum_blocks(blocks).astype(bf)))

    def reduce_columns(partial):
        cols = partial.shape[1]
        half = shard // 2
        split = pair_sum(partial.reshape(parts, shard, cols), 1)
        blocks = [at(split, mine ^ step, 1).reshape(half, cols) for step in range(parts)]
        got = [blocks[0]] + [hop(blocks[step], step) for step in range(1, parts)]
        whole = jnp.zeros((parts, half, cols), bf)
        for step in range(parts):
            whole = lax.dynamic_update_slice(whole, got[step][None], (mine ^ step, 0, 0))
        return whole

    dot = lambda a, b: jnp.dot(a, b, preferred_element_type=f32)

    gains = lax.all_gather(jnp.stack([norm_gain, ffn_gain], 0), "fsdp", axis=1, tiled=True)
    gain_one, gain_two = gains[0].astype(f32), gains[1].astype(f32)
    key_value_w = gather_rows(jnp.concatenate([w_key, w_value], 1))
    query_w = gather_rows(w_query)
    out_w = gather_rows(w_out)
    wide_w = gather_columns([w_gate, w_up], ff_part)
    grad_y_low = cotangent.reshape(row_count, model_width)
    all_dm = gather_tokens(grad_y_low)

    inputs = hidden_in.astype(f32).reshape(row_count, model_width)
    scale_one = rms_scale(inputs)
    normed_one = (inputs * scale_one * gain_one).astype(bf)
    key_value = dot(normed_one, key_value_w)
    cosine, sine_table = rope_table(positions)
    keys_low = rotate(
        key_value[:, : KVH * HD].reshape(seq_count, tok_count, KVH, HD), cosine, sine_table
    ).astype(bf)
    packed = jnp.concatenate(
        [
            keys_low.reshape(seq_count, tok_count, KVH * HD),
            key_value[:, KVH * HD :].astype(bf).reshape(seq_count, tok_count, KVH * HD),
        ],
        -1,
    )
    all_packed = lax.all_gather(packed, "ctx", axis=1, tiled=True)
    all_keys, all_values = all_packed[..., : KVH * HD], all_packed[..., KVH * HD :]
    all_pos = lax.all_gather(positions, "ctx", axis=1, tiled=True)
    query_low = rotate(
        dot(normed_one, query_w).reshape(seq_count, tok_count, H, HD), cosine, sine_table
    ).astype(bf)
    full_len = all_keys.shape[1]
    item_query = to_items(query_low, seq_count, tok_count, group_size)
    item_keys = (
        all_keys.reshape(seq_count, full_len, KVH, HD)
        .transpose(0, 2, 1, 3)
        .reshape(seq_count * KVH, full_len, HD)
    )
    item_values = (
        all_values.reshape(seq_count, full_len, KVH, HD)
        .transpose(0, 2, 1, 3)
        .reshape(seq_count * KVH, full_len, HD)
    )
    item_qpos = jnp.repeat(positions, KVH, axis=0)
    item_kpos = jnp.repeat(all_pos, KVH, axis=0)
    mixture_items, log_total = lax.map(
        attend_item, (item_query, item_keys, item_values, item_qpos, item_kpos)
    )
    attended = (
        from_items(mixture_items, seq_count, tok_count, group_size)
        .reshape(row_count, H * HD)
        .astype(bf)
    )
    residual = inputs + dot(attended, out_w)
    scale_two = rms_scale(residual)
    normed_two = (residual * scale_two * gain_two).astype(bf)
    all_normed = gather_tokens(normed_two)

    gate_w, up_w = wide_w[:, :ff_part], wide_w[:, ff_part:]
    gate_proj, up_proj = dot(all_normed, gate_w), dot(all_normed, up_w)
    sigmoid_gate = jax.nn.sigmoid(gate_proj)
    hidden_low = (gate_proj * sigmoid_gate * up_proj).astype(bf)
    grad_hidden = dot(all_dm, w_down.T)
    grad_down_part = dot(hidden_low.T, all_dm).astype(bf)
    grad_down = both_halves(sum_levels(pair_sum(grad_down_part, 0)))
    grad_up_in = (grad_hidden * gate_proj * sigmoid_gate).astype(bf)
    grad_gate_in = (
        grad_hidden * up_proj * sigmoid_gate * (1.0 + gate_proj * (1.0 - sigmoid_gate))
    ).astype(bf)
    grad_wide_in = jnp.concatenate([grad_gate_in, grad_up_in], 1)
    grad_normed_part = dot(grad_wide_in, wide_w.T).astype(bf)
    split_rows = lambda a: [a[i * row_count : (i + 1) * row_count] for i in range(parts)]
    grad_normed_two = sum_blocks(split_rows(grad_normed_part))
    grad_wide_part = dot(all_normed.T, grad_wide_in).astype(bf)
    wide_blocks = reduce_columns(grad_wide_part)
    wide_sum = sum_levels(wide_blocks)
    half_rows = lambda a: both_halves(
        a.transpose(1, 0, 2).reshape(shard // 2, parts * ff_part)
    )
    grad_gate_w = half_rows(wide_sum[:, :, :ff_part])
    grad_up_w = half_rows(wide_sum[:, :, ff_part:])

    grad_y = grad_y_low.astype(f32)
    grad_res_norm, grad_gain_two = norm_back(grad_normed_two, residual, scale_two, gain_two)
    grad_residual = grad_y + grad_res_norm
    grad_proj = grad_residual.astype(bf)
    grad_out_w = reduce_rows(dot(attended.T, grad_proj).astype(bf))
    grad_attended = dot(grad_proj, out_w.T).astype(bf)
    mixed_part = dot(hidden_low, w_down).astype(bf)
    output = (
        (residual + sum_blocks(split_rows(mixed_part)))
        .astype(bf)
        .reshape(seq_count, tok_count, model_width)
    )

    item_grad = to_items(grad_attended, seq_count, tok_count, group_size)
    grad_q_items, grad_k_items, grad_v_items = lax.map(
        attend_back_item,
        (item_query, item_keys, item_values, item_qpos, item_kpos, log_total, item_grad),
    )
    by_run = lambda a: a.reshape(seq_count, KVH, levels, 2, tok_count, HD)
    grad_kv = jnp.stack([by_run(grad_k_items), by_run(grad_v_items)], 0).astype(bf)
    grad_kv = grad_kv.transpose(3, 4, 0, 1, 2, 5, 6)
    kept = at(grad_kv, core, 1, 1)[:, 0].astype(f32)
    got = swap_core(at(grad_kv, 1 - core, 1, 1)[:, 0])
    by_level = kept + got.astype(f32)
    own_kv = at(by_level, level, 1)[0]
    for step in range(1, levels):
        sent = at(by_level, lax.rem(level + step, levels), 1)[0].astype(bf)
        own_kv = own_kv + level_send(
            sent, [(i, (i + step) % levels) for i in range(levels)]
        ).astype(f32)
    grad_keys_low = (
        rotate(own_kv[0].transpose(0, 2, 1, 3), cosine, -sine_table)
        .astype(bf)
        .reshape(row_count, KVH * HD)
    )
    grad_values_low = own_kv[1].transpose(0, 2, 1, 3).reshape(row_count, KVH * HD).astype(bf)
    grad_query_rot = from_items(grad_q_items, seq_count, tok_count, group_size)
    grad_query_low = (
        rotate(grad_query_rot, cosine, -sine_table).astype(bf).reshape(row_count, H * HD)
    )
    grad_kv_low = jnp.concatenate([grad_keys_low, grad_values_low], 1)
    grad_query_w = reduce_rows(dot(normed_one.T, grad_query_low).astype(bf))
    grad_kv_w = reduce_rows(dot(normed_one.T, grad_kv_low).astype(bf))
    grad_normed_one = dot(grad_query_low, query_w.T) + dot(grad_kv_low, key_value_w.T)
    grad_in_norm, grad_gain_one = norm_back(grad_normed_one, inputs, scale_one, gain_one)
    grad_in = (grad_residual + grad_in_norm).reshape(seq_count, tok_count, model_width)
    gain_sum = lax.psum(jnp.stack([grad_gain_one, grad_gain_two], 0), ("fsdp", "ctx"))
    gain_own = at(gain_sum, mine * shard, shard, 1)
    return (
        output,
        grad_in,
        gain_own[0],
        grad_query_w,
        grad_kv_w[:, : KVH * HD],
        grad_kv_w[:, KVH * HD :],
        grad_out_w,
        gain_own[1],
        grad_gate_w,
        grad_up_w,
        grad_down,
    )


def solution(mesh):
    placed = (
        P("fsdp", "ctx", None),
        P("fsdp", "ctx"),
        P("fsdp", "ctx", None),
        P("fsdp"),
        P("fsdp", None),
        P("fsdp", None),
        P("fsdp", None),
        P("fsdp", None),
        P("fsdp"),
        P("fsdp", None),
        P("fsdp", None),
        P("fsdp", None),
    )
    return jax.shard_map(
        on_device,
        mesh=mesh,
        in_specs=placed,
        out_specs=(
            P("fsdp", "ctx", None),
            P("fsdp", "ctx", None),
            P("fsdp"),
            P("fsdp", None),
            P("fsdp", None),
            P("fsdp", None),
            P("fsdp", None),
            P("fsdp"),
            P("fsdp", None),
            P("fsdp", None),
            P("fsdp", None),
        ),
        check_vma=False,
    )
```

time: 2660 us -> 1540 us (0.58)
  waiting for transfers between devices: 1960 us -> 480 us
  blocking collectives: 54.4 us -> 192 us
  other arithmetic: 62 us -> 161 us
  starting transfers between devices: 0.76 us -> 85.2 us
  local copies, waits for them, and re-layouts: 286 us -> 350 us
  matrix products: 271 us -> 233 us
    reduce_scatter x7 -> x0, waiting for transfers between devices: 772 us -> none  [the longest x1 208 us: on_device(): lax.psum_scatter(grad_up_w.astype(jnp.bfloat16), 'fsdp', scatter_dimensio...]
    all_gather x9 -> x1, waiting for transfers between devices: 772 us -> 0.01 us  [on_device(): all_packed = lax.all_gather(packed, 'ctx', axis=1, tiled=True)]
    ppermute x0 -> x80, waiting for transfers between devices: none -> 480 us  [the longest x18 245 us: level_send(): lax.ppermute(array, 'ctx', [(2 * a + k, 2 * b + k) for a, b in pairs for...]
    psum x1 -> x0, waiting for transfers between devices: 385 us -> none  [on_device(): lax.psum(part_query.astype(jnp.bfloat16), 'ctx').astype(jnp.float32)]
    unnamed x99 -> x152, local copies, waits for them, and re-layouts: 250 us -> 22.5 us
    dynamic_update_slice x0 -> x28, local copies, waits for them, and re-layouts: none -> 183 us  [the longest x4 152 us: reduce_columns(): lax.dynamic_update_slice(whole, got[step][None], (mine ^ step, 0, 0))]
    psum x1, blocking collectives: 15.6 us -> 138 us  [on_device(): lax.psum(jnp.stack([grad_gain_one, grad_gain_two], 0), ('fsdp', 'ctx'))]
    ppermute x0 -> x80, starting transfers between devices: none -> 85.2 us  [the longest x46 47.5 us: hop(): return lax.ppermute(array, 'fsdp', [(i, i ^ bit) for i in range(parts)])]
  transfers between devices with their start and end apart: 19 -> 81, of which waited for: 15 -> 32; matrix products, arithmetic and copies ran while one was open for 17% -> 43% of each run, Pallas kernels for 0% -> 0%
where the time goes in v1:
time: 1540 us; the launch traced here: 1520 us
  waiting for transfers between devices  480 us (31%)
  local copies, waits for them, and re-layouts  350 us (23%)
  matrix products  233 us (15%)
  blocking collectives  192 us (12%)
  other arithmetic  161 us (10%)
  starting transfers between devices  85.2 us (6%)
  between operations  16 us (1%)
    ppermute x18, waiting for transfers between devices, level_send(): lax.ppermute(array, 'ctx', [(2 * a + k, 2 * b + k) for a, b in pairs for...  245 us
    ppermute x46, waiting for transfers between devices, hop(): return lax.ppermute(array, 'fsdp', [(i, i ^ bit) for i in range(parts)])  235 us
    dynamic_update_slice x4, local copies, waits for them, and re-layouts, reduce_columns(): lax.dynamic_update_slice(whole, got[step][None], (mine ^ step, 0, 0))  152 us
    psum x1, blocking collectives, on_device(): lax.psum(jnp.stack([grad_gain_one, grad_gain_two], 0), ('fsdp', 'ctx'))  138 us
    dot_general x16, matrix products, on_device(): dot = lambda a, b: jnp.dot(a, b, preferred_element_type=f32)  125 us
    ppermute x46, starting transfers between devices, hop(): return lax.ppermute(array, 'fsdp', [(i, i ^ bit) for i in range(parts)])  47.5 us
    all_gather x1, blocking collectives, on_device(): lax.all_gather(jnp.stack([norm_gain, ffn_gain], 0), 'fsdp', axis=1, tiled...  42.7 us
    ppermute x18, starting transfers between devices, level_send(): lax.ppermute(array, 'ctx', [(2 * a + k, 2 * b + k) for a, b in pairs for...  35.1 us
  transfers between devices with their start and end apart: 81, of which 32 were waited for; matrix products, arithmetic and copies ran while one was open for 43% of the time, Pallas kernels for 0%

profile of v1, /device:TPU:0, one launch (start us, length us, event | category | flops | bytes accessed | tf_op | source)
XLA Modules:
  0.0 1518.1 jit_solution(17145342394278491452)
XLA Ops:
  24.8 42.7 %all_gather.9 = bf16[2,2048]{1,0:T(2,128)(2,1)S(1)} all-gather(bf16[2,512]{1,0:T(2,128)(2,1)S(1)} %pad_maximum_fusion.29), channel_id=1, replica_groups=mesh['fsdp'=4,'ctx'=8] {'fsdp'}, dimensions={1}, use_global_device_ids=true | all-gather | bytes 10240 | tf_op jit(solution)/shard_map/all_gather | solution.py:265
  130.6 14.6 collective-permute-done.6
  149.0 18.7 %collective-permute-done.28 = bf16[256,2048]{1,0:T(8,128)(2,1)S(1)} collective-permute-done((bf16[256,2048]{1,0:T(8,128)(2,1)}, bf16[256,2048]{1,0:T(8,128)(2,1)S(1)}, u32[]{:S(2)}, u32[]{:S(2)}) %collective-permute-start.28) | collective-permute-done | bytes 1048608 | tf_op jit(solution)/shard_map/ppermute | solution.py:138
  182.8 23.7 %collective-permute-done.21 = bf16[256,2816]{1,0:T(8,128)(2,1)} collective-permute-done((bf16[256,2816]{1,0:T(8,128)(2,1)}, bf16[256,2816]{1,0:T(8,128)(2,1)}, u32[]{:S(2)}, u32[]{:S(2)}) %collective-permute-start.21) | collective-permute-done | bytes 1441824 | tf_op jit(solution)/shard_map/ppermute | solution.py:138
  207.1 22.5 %collective-permute-done.20 = bf16[256,2816]{1,0:T(8,128)(2,1)} collective-permute-done((bf16[256,2816]{1,0:T(8,128)(2,1)}, bf16[256,2816]{1,0:T(8,128)(2,1)}, u32[]{:S(2)}, u32[]{:S(2)}) %collective-permute-start.20) | collective-permute-done | bytes 1441824 | tf_op jit(solution)/shard_map/ppermute | solution.py:138
  262.4 12.0 fusion.137
  280.2 12.4 copy.73
  321.5 47.7 %while.28 = (s32[]{:T(128)}, bf16[8,128,8,64]{1,3,2,0:T(8,128)(2,1)}, f32[8,8,128]{2,1,0:T(8,128)}, bf16[8,1024,64]{1,2,0:T(8,128)(2,1)}, s32[8,1024]{1,0:T(8,12...) while((s32[]{:T(128)}, ...), condition=%wide.region_4.5_spmd.clone, body=%wide.region_1.4_spmd.sunk.clone | while | flops 281148416 | bytes 13811305 | solution.py:309
  390.8 12.0 collective-permute-done.15
  429.9 14.7 multiply_convert_fusion.1
  444.6 18.2 %convolution_convert_fusion.4 = bf16[1024,2048]{1,0:T(8,128)(2,1)S(1)} fusion(bf16[2048,2816]{1,0:T(8,128)(2,1)} %bitcast.73, bf16[1024,1408]{1,0:T(8,128)(2,1)} %get-tuple-element.206, bf16[1024,1408]{1,0:T(8,128)(2,1)} %get-tuple-element.204), kind=kOutput, calls=%fused_computation.98 | convolution fusion | flops 11824791552 | bytes 21495808 | tf_op jit(solution)/shard_map/dot_general | solution.py:263
  462.9 17.6 %convolution_convert_fusion = bf16[2048,2816]{1,0:T(8,128)(2,1)} fusion(bf16[1024,2048]{1,0:T(8,128)(2,1)} %copy-done.40, bf16[1024,1408]{1,0:T(8,128)(2,1)} %get-tuple-element.206, bf16[1024,1408]{1,0:T(8,128)(2,1)S(1)} %copy-done.55), kind=kOutput, calls=%fused_computation.75 | convolution fusion | flops 11828461568 | bytes 21495808 | tf_op jit(solution)/shard_map/dot_general | solution.py:263
  532.6 15.3 %collective-permute-done.26 = bf16[256,2048]{1,0:T(8,128)(2,1)S(1)} collective-permute-done((bf16[256,2048]{1,0:T(8,128)(2,1)}, bf16[256,2048]{1,0:T(8,128)(2,1)S(1)}, u32[]{:S(2)}, u32[]{:S(2)}) %collective-permute-start.26) | collective-permute-done | bytes 1048608 | tf_op jit(solution)/shard_map/ppermute | solution.py:138
  564.8 102.2 %while.29 = (s32[]{:T(128)}, f32[8,128,8,64]{1,3,2,0:T(8,128)}, bf16[8,1024,64]{1,2,0:T(8,128)(2,1)}, bf16[8,1024,64]{1,2,0:T(8,128)(2,1)}, bf16[8,1024,64]{1,2,...) while((s32[]{:T(128)}, f32[8,128,8,64]{1,3,2,0:T(8,128)}, ...), condition=%wide.region_9.10_spmd.clone, body=%wide.region_7.9_spmd.sunk.clone | while | flops 687078400 | bytes 33733248 | solution.py:360
  714.1 12.6 collective-permute-done.37
  741.9 26.3 %collective-permute-done.68 = bf16[256,2816]{1,0:T(8,128)(2,1)} collective-permute-done((bf16[256,2816]{1,0:T(8,128)(2,1)}, bf16[256,2816]{1,0:T(8,128)(2,1)}, u32[]{:S(2)}, u32[]{:S(2)}) %collective-permute-start.68) | collective-permute-done | bytes 1441824 | tf_op jit(solution)/shard_map/ppermute | solution.py:138
  778.6 48.4 %dynamic_update_slice.143 = bf16[4,256,2816]{2,0,1:T(4,128)(2,1)} dynamic-update-slice(bf16[4,256,2816]{2,0,1:T(4,128)(2,1)} %copy.88, bf16[1,256,2816]{2,0,1:T(2,128)(2,1)} %copy.89, s32[]{:T(128)S(6)} %select_n.252, s32[]{:T(128)} %constant.103.clone.1, s32[]{:T(128)} %constant.103.clone.1) | dynamic-update-slice | bytes 2883588 | tf_op jit(solution)/shard_map/dynamic_update_slice | solution.py:260
  827.0 48.4 %dynamic_update_slice.144 = bf16[4,256,2816]{2,0,1:T(4,128)(2,1)} dynamic-update-slice(bf16[4,256,2816]{2,0,1:T(4,128)(2,1)} %dynamic_update_slice.143, bf16[1,256,2816]{2,0,1:T(2,128)(2,1)} %copy.90, s32[]{:T(128)S(6)} %select_n.255, s32[]{:T(128)} %constant.103.clone.1, s32[]{:T(128)} %constant.103.clone.1) | dynamic-update-slice | bytes 2883588 | tf_op jit(solution)/shard_map/dynamic_update_slice | solution.py:260
  875.4 48.5 %dynamic_update_slice.145 = bf16[4,256,2816]{2,0,1:T(4,128)(2,1)} dynamic-update-slice(bf16[4,256,2816]{2,0,1:T(4,128)(2,1)} %dynamic_update_slice.144, bf16[1,256,2816]{2,0,1:T(2,128)(2,1)} %copy.91, s32[]{:T(128)S(6)} %select_n.256, s32[]{:T(128)} %constant.103.clone.1, s32[]{:T(128)} %constant.103.clone.1) | dynamic-update-slice | bytes 2883588 | tf_op jit(solution)/shard_map/dynamic_update_slice | solution.py:260
  973.6 78.5 %collective-permute-done.70 = bf16[4,256,2816]{2,0,1:T(4,128)(2,1)} collective-permute-done((bf16[4,256,2816]{2,0,1:T(4,128)(2,1)}, bf16[4,256,2816]{2,0,1:T(4,128)(2,1)}, u32[]{:S(2)}, u32[]{:S(2)}) %collective-permute-start.70) | collective-permute-done | bytes 5767200 | tf_op jit(solution)/shard_map/ppermute | solution.py:144
  1065.0 47.1 %collective-permute-done.53 = bf16[256,512]{1,0:T(8,128)(2,1)S(1)} collective-permute-done((bf16[256,512]{1,0:T(8,128)(2,1)S(1)}, bf16[256,512]{1,0:T(8,128)(2,1)S(1)}, u32[]{:S(2)}, u32[]{:S(2)}) %collective-permute-start.53) | collective-permute-done | bytes 262176 | tf_op jit(solution)/shard_map/ppermute | solution.py:144
  1203.5 137.7 %psum.7 = f32[2,2048]{1,0:T(2,128)S(1)} all-reduce(f32[2,2048]{1,0:T(2,128)S(1)} %pad_maximum_fusion.28), channel_id=1, replica_groups=mesh['fsdp'=4,'ctx'=8] {'fsdp','ctx'}, use_global_device_ids=true, to_apply=%region_13.14 | all-reduce | flops 4096 | bytes 32768 | tf_op jit(solution)/shard_map/psum | solution.py:392
  1357.9 87.9 %collective-permute-done.46 = bf16[256,2048]{1,0:T(8,128)(2,1)S(1)} collective-permute-done((bf16[256,2048]{1,0:T(8,128)(2,1)S(1)}, bf16[256,2048]{1,0:T(8,128)(2,1)S(1)}, u32[]{:S(2)}, u32[]{:S(2)}) %collective-permute-start.46) | collective-permute-done | bytes 1048608 | tf_op jit(solution)/shard_map/ppermute | solution.py:144
  1446.9 18.8 %collective-permute-done.64 = bf16[256,2048]{1,0:T(8,128)(2,1)S(1)} collective-permute-done((bf16[256,2048]{1,0:T(8,128)(2,1)S(1)}, bf16[256,2048]{1,0:T(8,128)(2,1)S(1)}, u32[]{:S(2)}, u32[]{:S(2)}) %collective-permute-start.64) | collective-permute-done | bytes 1048608 | tf_op jit(solution)/shard_map/ppermute | solution.py:144
  (657 shorter events, 722.6 us)
Async XLA Ops:
  7.2 301.2 %all-gather.2.cloned.1.call-start = ((), (), s32[]{:S(2)}) async-start(), calls=%async_computation | async-start | bytes 2359296 | tf_op jit(solution)/shard_map/all_gather | solution.py:289
  9.7 109.9 %collective-permute-start.10 = (bf16[256,2048]{1,0:T(8,128)(2,1)}, bf16[256,2048]{1,0:T(8,128)(2,1)S(1)}, u32[]{:S(2)}, u32[]{:S(2)}) collective-permute-start(bf16[256,2048]{1,0:T(8,128)(2,1)} %constant_dynamic-slice_fusion.12), channel_id=1, source_target_pairs={{0,8},{8,0},{16,24},{24,16},{1,9},{9,1},{17,25},{25,17},{2,10},{10... | collective-permute-start | bytes 3145736 | tf_op jit(solution)/shard_map/ppermute | solution.py:138
  12.6 116.7 %collective-permute-start.11 = (bf16[256,2048]{1,0:T(8,128)(2,1)}, bf16[256,2048]{1,0:T(8,128)(2,1)S(1)}, u32[]{:S(2)}, u32[]{:S(2)}) collective-permute-start(bf16[256,2048]{1,0:T(8,128)(2,1)} %constant_dynamic-slice_fusion.12), channel_id=1, source_target_pairs={{0,16},{8,24},{16,0},{24,8},{1,17},{9,25},{17,1},{25,9},{2,18},{10... | collective-permute-start | bytes 3145736 | tf_op jit(solution)/shard_map/ppermute | solution.py:138
  17.6 81.2 %collective-permute-start = (bf16[256,512]{1,0:T(8,128)(2,1)}, bf16[256,512]{1,0:T(8,128)(2,1)}, u32[]{:S(2)}, u32[]{:S(2)}) collective-permute-start(bf16[256,512]{1,0:T(8,128)(2,1)} %constant_dynamic-slice_fusion.14), channel_id=1, source_target_pairs={{0,8},{8,0},{16,24},{24,16},{1,9},{9,1},{17,25},{25,17},{2,10},{10... | collective-permute-start | bytes 786440 | tf_op jit(solution)/shard_map/ppermute | solution.py:138
  18.1 78.5 %collective-permute-start.1 = (bf16[256,512]{1,0:T(8,128)(2,1)}, bf16[256,512]{1,0:T(8,128)(2,1)S(1)}, u32[]{:S(2)}, u32[]{:S(2)}) collective-permute-start(bf16[256,512]{1,0:T(8,128)(2,1)} %constant_dynamic-slice_fusion.14), channel_id=1, source_target_pairs={{0,16},{8,24},{16,0},{24,8},{1,17},{9,25},{17,1},{25,9},{2,18},{10... | collective-permute-start | bytes 786440 | tf_op jit(solution)/shard_map/ppermute | solution.py:138
  18.1 106.1 %collective-permute-start.27 = (bf16[256,2048]{1,0:T(8,128)(2,1)}, bf16[256,2048]{1,0:T(8,128)(2,1)}, u32[]{:S(2)}, u32[]{:S(2)}) collective-permute-start(bf16[256,2048]{1,0:T(8,128)(2,1)} %bitcast.578), channel_id=1, source_target_pairs={{0,8},{8,0},{16,24},{24,16},{1,9},{9,1},{17,25},{25,17},{2,10},{10... | collective-permute-start | bytes 3145736 | tf_op jit(solution)/shard_map/ppermute | solution.py:138
  147.6 82.0 %collective-permute-start.20 = (bf16[256,2816]{1,0:T(8,128)(2,1)}, bf16[256,2816]{1,0:T(8,128)(2,1)}, u32[]{:S(2)}, u32[]{:S(2)}) collective-permute-start(bf16[256,2816]{1,0:T(8,128)(2,1)} %pad_maximum_fusion.8), channel_id=1, source_target_pairs={{0,16},{8,24},{16,0},{24,8},{1,17},{9,25},{17,1},{25,9},{2,18},{10... | collective-permute-start | bytes 4325384 | tf_op jit(solution)/shard_map/ppermute | solution.py:138
  240.9 139.7 %collective-permute-start.22 = (bf16[768,2816]{1,0:T(8,128)(2,1)}, bf16[768,2816]{1,0:T(8,128)(2,1)}, u32[]{:S(2)}, u32[]{:S(2)}) collective-permute-start(bf16[768,2816]{1,0:T(8,128)(2,1)} %pad_maximum_fusion.1), channel_id=1, source_target_pairs={{0,1},{1,0},{2,3},{3,2},{4,5},{5,4},{6,7},{7,6},{8,9},{9,8},{10,11... | collective-permute-start | bytes 12976136 | tf_op jit(solution)/shard_map/ppermute | solution.py:141
  518.7 172.6 %collective-permute-start.66 = (bf16[4,256,2816]{2,1,0:T(8,128)(2,1)}, bf16[4,256,2816]{2,1,0:T(8,128)(2,1)}, u32[]{:S(2)}, u32[]{:S(2)}) collective-permute-start(bf16[4,256,2816]{2,1,0:T(8,128)(2,1)} %constant_dynamic-slice_fusion.6), channel_id=1, source_target_pairs={{0,1},{1,0},{2,3},{3,2},{4,5},{5,4},{6,7},{7,6},{8,9},{9,8},{10,11... | collective-permute-start | bytes 17301512 | tf_op jit(solution)/shard_map/ppermute | solution.py:141
  726.8 236.1 %collective-permute-start.75 = (bf16[704,2048]{1,0:T(8,128)(2,1)}, bf16[704,2048]{1,0:T(8,128)(2,1)}, u32[]{:S(2)}, u32[]{:S(2)}) collective-permute-start(bf16[704,2048]{1,0:T(8,128)(2,1)} %constant_dynamic-slice_fusion.5), channel_id=1, source_target_pairs={{0,1},{1,0},{2,3},{3,2},{4,5},{5,4},{6,7},{7,6},{8,9},{9,8},{10,11... | collective-permute-start | bytes 8650760 | tf_op jit(solution)/shard_map/ppermute | solution.py:141
  923.9 128.2 %collective-permute-start.70 = (bf16[4,256,2816]{2,0,1:T(4,128)(2,1)}, bf16[4,256,2816]{2,0,1:T(4,128)(2,1)}, u32[]{:S(2)}, u32[]{:S(2)}) collective-permute-start(bf16[4,256,2816]{2,0,1:T(4,128)(2,1)} %dynamic_update_slice.145), channel_id=1, source_target_pairs={{0,2},{1,3},{6,4},{7,5},{8,10},{9,11},{14,12},{15,13},{16,18},{17,... | collective-permute-start | bytes 17301512 | tf_op jit(solution)/shard_map/ppermute | solution.py:144
  943.0 169.9 %collective-permute-start.39 = (bf16[4,256,2048]{2,1,0:T(8,128)(2,1)}, bf16[4,256,2048]{2,1,0:T(8,128)(2,1)}, u32[]{:S(2)}, u32[]{:S(2)}) collective-permute-start(bf16[4,256,2048]{2,1,0:T(8,128)(2,1)} %constant_dynamic-slice_fusion.9), channel_id=1, source_target_pairs={{0,1},{1,0},{2,3},{3,2},{4,5},{5,4},{6,7},{7,6},{8,9},{9,8},{10,11... | collective-permute-start | bytes 12582920 | tf_op jit(solution)/shard_map/ppermute | solution.py:141
  950.5 171.4 %collective-permute-start.57 = (bf16[4,256,2048]{2,1,0:T(8,128)(2,1)}, bf16[4,256,2048]{2,1,0:T(8,128)(2,1)}, u32[]{:S(2)}, u32[]{:S(2)}) collective-permute-start(bf16[4,256,2048]{2,1,0:T(8,128)(2,1)} %constant_dynamic-slice_fusion.7), channel_id=1, source_target_pairs={{0,1},{1,0},{2,3},{3,2},{4,5},{5,4},{6,7},{7,6},{8,9},{9,8},{10,11... | collective-permute-start | bytes 12582920 | tf_op jit(solution)/shard_map/ppermute | solution.py:141
  969.1 182.2 %collective-permute-start.76 = (bf16[704,2048]{1,0:T(8,128)(2,1)S(1)}, bf16[704,2048]{1,0:T(8,128)(2,1)}, u32[]{:S(2)}, u32[]{:S(2)}) collective-permute-start(bf16[704,2048]{1,0:T(8,128)(2,1)S(1)} %add_convert_fusion.7), channel_id=1, source_target_pairs={{0,2},{1,3},{6,4},{7,5},{8,10},{9,11},{14,12},{15,13},{16,18},{17,... | collective-permute-start | bytes 8650760 | tf_op jit(solution)/shard_map/ppermute | solution.py:144
  972.1 140.1 %collective-permute-start.53 = (bf16[256,512]{1,0:T(8,128)(2,1)S(1)}, bf16[256,512]{1,0:T(8,128)(2,1)S(1)}, u32[]{:S(2)}, u32[]{:S(2)}) collective-permute-start(bf16[256,512]{1,0:T(8,128)(2,1)S(1)} %fusion.107), channel_id=1, source_target_pairs={{0,2},{1,3},{6,4},{7,5},{8,10},{9,11},{14,12},{15,13},{16,18},{17,... | collective-permute-start | bytes 786440 | tf_op jit(solution)/shard_map/ppermute | solution.py:144
  1061.9 130.4 %collective-permute-start.71 = (bf16[4,256,2816]{2,0,1:T(4,128)(2,1)}, bf16[4,256,2816]{2,0,1:T(4,128)(2,1)}, u32[]{:S(2)}, u32[]{:S(2)}) collective-permute-start(bf16[4,256,2816]{2,0,1:T(4,128)(2,1)} %add_convert_fusion.1), channel_id=1, source_target_pairs={{2,4},{3,5},{4,2},{5,3},{10,12},{11,13},{12,10},{13,11},{18,20},{1... | collective-permute-start | bytes 17301512 | tf_op jit(solution)/shard_map/ppermute | solution.py:144
  1168.7 173.1 %collective-permute-start.54 = (bf16[256,512]{1,0:T(8,128)(2,1)S(1)}, bf16[256,512]{1,0:T(8,128)(2,1)}, u32[]{:S(2)}, u32[]{:S(2)}) collective-permute-start(bf16[256,512]{1,0:T(8,128)(2,1)S(1)} %copy-done.31), channel_id=1, source_target_pairs={{2,4},{3,5},{4,2},{5,3},{10,12},{11,13},{12,10},{13,11},{18,20},{1... | collective-permute-start | bytes 786440 | tf_op jit(solution)/shard_map/ppermute | solution.py:144
  1172.4 175.3 %collective-permute-start.77 = (bf16[704,2048]{1,0:T(8,128)(2,1)}, bf16[704,2048]{1,0:T(8,128)(2,1)}, u32[]{:S(2)}, u32[]{:S(2)}) collective-permute-start(bf16[704,2048]{1,0:T(8,128)(2,1)} %add_convert_fusion.6), channel_id=1, source_target_pairs={{2,4},{3,5},{4,2},{5,3},{10,12},{11,13},{12,10},{13,11},{18,20},{1... | collective-permute-start | bytes 8650760 | tf_op jit(solution)/shard_map/ppermute | solution.py:144
  1183.1 161.0 %collective-permute-start.44 = (bf16[256,2048]{1,0:T(8,128)(2,1)S(1)}, bf16[256,2048]{1,0:T(8,128)(2,1)S(1)}, u32[]{:S(2)}, u32[]{:S(2)}) collective-permute-start(bf16[256,2048]{1,0:T(8,128)(2,1)S(1)} %fusion.68), channel_id=1, source_target_pairs={{0,2},{1,3},{6,4},{7,5},{8,10},{9,11},{14,12},{15,13},{16,18},{17,... | collective-permute-start | bytes 3145736 | tf_op jit(solution)/shard_map/ppermute | solution.py:144
  1188.2 157.0 %collective-permute-start.62 = (bf16[256,2048]{1,0:T(8,128)(2,1)S(1)}, bf16[256,2048]{1,0:T(8,128)(2,1)}, u32[]{:S(2)}, u32[]{:S(2)}) collective-permute-start(bf16[256,2048]{1,0:T(8,128)(2,1)S(1)} %fusion.66), channel_id=1, source_target_pairs={{0,2},{1,3},{6,4},{7,5},{8,10},{9,11},{14,12},{15,13},{16,18},{17,... | collective-permute-start | bytes 3145736 | tf_op jit(solution)/shard_map/ppermute | solution.py:144
  1202.1 264.6 %collective-permute-start.72 = (bf16[4,256,2816]{2,0,1:T(4,128)(2,1)}, bf16[4,256,2816]{2,0,1:T(4,128)(2,1)}, u32[]{:S(2)}, u32[]{:S(2)}) collective-permute-start(bf16[4,256,2816]{2,0,1:T(4,128)(2,1)} %add_convert_fusion), channel_id=1, source_target_pairs={{2,0},{3,1},{4,6},{5,7},{10,8},{11,9},{12,14},{13,15},{18,16},{19,... | collective-permute-start | bytes 17301512 | tf_op jit(solution)/shard_map/ppermute | solution.py:144
  1351.5 114.3 %collective-permute-start.78 = (bf16[704,2048]{1,0:T(8,128)(2,1)S(1)}, bf16[704,2048]{1,0:T(8,128)(2,1)S(1)}, u32[]{:S(2)}, u32[]{:S(2)}) collective-permute-start(bf16[704,2048]{1,0:T(8,128)(2,1)S(1)} %add_convert_fusion.5), channel_id=1, source_target_pairs={{2,0},{3,1},{4,6},{5,7},{10,8},{11,9},{12,14},{13,15},{18,16},{19,... | collective-permute-start | bytes 8650760 | tf_op jit(solution)/shard_map/ppermute | solution.py:144
  1353.5 92.3 %collective-permute-start.46 = (bf16[256,2048]{1,0:T(8,128)(2,1)S(1)}, bf16[256,2048]{1,0:T(8,128)(2,1)S(1)}, u32[]{:S(2)}, u32[]{:S(2)}) collective-permute-start(bf16[256,2048]{1,0:T(8,128)(2,1)S(1)} %add_convert_fusion.11), channel_id=1, source_target_pairs={{2,0},{3,1},{4,6},{5,7},{10,8},{11,9},{12,14},{13,15},{18,16},{19,... | collective-permute-start | bytes 3145736 | tf_op jit(solution)/shard_map/ppermute | solution.py:144
  1355.2 110.5 %collective-permute-start.64 = (bf16[256,2048]{1,0:T(8,128)(2,1)S(1)}, bf16[256,2048]{1,0:T(8,128)(2,1)S(1)}, u32[]{:S(2)}, u32[]{:S(2)}) collective-permute-start(bf16[256,2048]{1,0:T(8,128)(2,1)S(1)} %add_convert_fusion.8), channel_id=1, source_target_pairs={{2,0},{3,1},{4,6},{5,7},{10,8},{11,9},{12,14},{13,15},{18,16},{19,... | collective-permute-start | bytes 3145736 | tf_op jit(solution)/shard_map/ppermute | solution.py:144
  (127 other events, 2909.4 us)
Sparse Core Ops, SparseCore 0:
  182.3 28.0 all-gather.1

commit v2 on v0

v2 whole, which is shorter than its diff:
```python
import functools

import jax
import jax.numpy as jnp
from jax import lax
from jax.experimental import pallas as pl
from jax.experimental.pallas import tpu as pltpu
from jax.sharding import PartitionSpec as P

H = 32
KVH = 4
HD = 64
GROUP = H // KVH
KW = KVH * HD


NORM_EPS = 1e-05
MASKED = -1e30
BF = jnp.bfloat16
F32 = jnp.float32
ROOM = 60 * 1024 * 1024
EXTRA = 16


def rms_scale(inputs):
    return lax.rsqrt(jnp.mean(inputs * inputs, -1, keepdims=True) + NORM_EPS)


def norm_back(grad_normed, inputs, row_scale, gain_row):
    scaled_grad = grad_normed * gain_row
    grad_gain = jnp.sum(grad_normed * inputs * row_scale, 0)
    grad_inputs = row_scale * scaled_grad - inputs * row_scale**3 * jnp.mean(
        scaled_grad * inputs, -1, keepdims=True
    )
    return (grad_inputs, grad_gain)


def at(array, start, size, axis=0):
    return lax.dynamic_slice_in_dim(array, start, size, axis)


def dot(a, b):
    return jnp.dot(a, b, preferred_element_type=F32)


def dot_cols(a, b):
    return lax.dot_general(a, b, (((1,), (1,)), ((), ())), preferred_element_type=F32)


def dot_rows(a, b):
    return lax.dot_general(a, b, (((0,), (0,)), ((), ())), preferred_element_type=F32)


def swap_halves(value):
    lane = lax.broadcasted_iota(jnp.int32, value.shape, 1)
    size = value.shape[1]
    ahead = pltpu.roll(value, size - HD // 2, 1)
    behind = pltpu.roll(value, HD // 2, 1)
    return jnp.where(lane % HD < HD // 2, ahead, behind)


def spin(value, cosine, sine):
    return value * cosine + swap_halves(value) * sine


def call(
    body, outs, args, scratch=(), flops=0, nbytes=0, grid=None, in_specs=None, out_specs=None,
    after=(), prefetch=False,
):
    whole = pl.BlockSpec(memory_space=pltpu.VMEM)
    many = isinstance(outs, (list, tuple))
    in_specs = list(in_specs or [whole] * len(args))
    count = len(args)
    args = [*args, *after]
    in_specs += [pl.BlockSpec(memory_space=pl.ANY)] * len(after)

    def run(*refs):
        return body(*refs[:count], *refs[count + len(after) :])

    options = pltpu.CompilerParams(vmem_limit_bytes=ROOM)
    cost = pl.CostEstimate(flops=flops, bytes_accessed=nbytes, transcendentals=0)
    if prefetch:
        return pl.pallas_call(
            run,
            out_shape=outs,
            grid_spec=pltpu.PrefetchScalarGridSpec(
                num_scalar_prefetch=1, grid=grid, in_specs=in_specs, out_specs=out_specs
            ),
            compiler_params=options,
            cost_estimate=cost,
        )(*args)
    return pl.pallas_call(
        run,
        out_shape=outs,
        in_specs=in_specs,
        out_specs=out_specs or ([whole] * len(outs) if many else whole),
        scratch_shapes=list(scratch),
        grid=grid or (),
        compiler_params=options,
        cost_estimate=cost,
    )(*args)


def shape(dims, kind):
    return jax.ShapeDtypeStruct(tuple(dims), kind)


class Pieces:
    def __init__(self, own, sources, blocks, cell, width, levels=0):
        self.levels = levels
        self.own, self.sources, self.blocks = list(own), list(sources), tuple(blocks)
        self.cell, self.width = cell, width
        self.part_rows = own[0].shape[0]
        self.count = len(self.own) + len(self.sources)
        self.copies = len(self.own) + len(self.blocks)

    def args(self):
        return self.own + self.sources

    def spot(self, where, step, flip):
        side = where[2] ^ flip
        if self.levels:
            side = lax.rem(where[3] + self.levels - step, self.levels) * 2 + side
        return pl.multiple_of(side * self.cell, self.cell)

    def moves(self, where, refs, bit, first, size):
        own, sources = refs[: len(self.own)], refs[len(self.own) :]
        step = self.width // len(self.own)
        moves = []
        if bit == 0:
            for number, source in enumerate(own):
                column = first
                if len(own) > 1:
                    column = pl.multiple_of(where[0] * step + first, 128)
                moves.append((source.at[:, pl.ds(column, size)], 0, self.part_rows, number))
        for source, row, step_, flip, flag in self.blocks:
            if flag != bit:
                continue
            spot = self.spot(where, step_, flip)
            for number in range(len(own)):
                place = sources[source].at[pl.ds(row, self.cell), pl.ds(number * step + first, size)]
                moves.append((place, spot, self.cell, number))
        return moves

    def whole_moves(self, where, refs, bit):
        own, sources = refs[: len(self.own)], refs[len(self.own) :]
        step = self.width // len(self.own)
        moves = []
        if bit == 0:
            for number, source in enumerate(own):
                column = pl.multiple_of(where[0] * step, 128) if len(own) > 1 else 0
                moves.append(
                    (source.at[:, pl.ds(column, step)], 0, self.part_rows, number * step, step)
                )
        for source, row, step_, flip, flag in self.blocks:
            if flag == bit:
                spot = self.spot(where, step_, flip)
                moves.append(
                    (sources[source].at[pl.ds(row, self.cell), :], spot, self.cell, 0, self.width)
                )
        return moves


def fetch_parts(pieces, where, refs, held, sems, parts):
    groups, number = [], 0
    for bit in range(parts):
        group = []
        for source, row, rows, column, cols in pieces.whole_moves(where, refs, bit):
            target = held.at[bit, pl.ds(row, rows), pl.ds(column, cols)]
            copy = pltpu.make_async_copy(source, target, sems.at[number])
            copy.start()
            group.append(copy)
            number += 1
        groups.append(group)
    return groups


SMEM = pl.BlockSpec(memory_space=pltpu.SMEM)
VMEM = pl.BlockSpec(memory_space=pltpu.VMEM)
HBM = pl.BlockSpec(memory_space=pl.ANY)


def forward_body(pieces, parts, where, left_ref, *refs):
    (out_ref, held, sems), refs = refs[-3:], refs[:-3]
    groups = fetch_parts(pieces, where, refs, held, sems, parts)
    rows = pieces.part_rows
    chunk = min(512, pieces.width)
    for bit in range(parts):
        for copy in groups[bit]:
            copy.wait()
        first = pl.multiple_of((where[0] ^ bit) * rows, 128)
        left = left_ref[:, pl.ds(first, rows)]

        def step(number, carry, bit=bit, left=left):
            cols = pl.ds(pl.multiple_of(number * chunk, chunk), chunk)
            part = dot(left, held[bit, :, cols])
            out_ref[:, cols] = part if bit == 0 else out_ref[:, cols] + part
            return carry

        lax.fori_loop(0, pieces.width // chunk, step, 0)


def forward_mm(where, left, pieces, parts, after=()):
    rows, depth = left.shape
    return call(
        functools.partial(forward_body, pieces, parts),
        shape((rows, pieces.width), F32),
        [where, left, *pieces.args()],
        [
            pltpu.VMEM((parts, pieces.part_rows, pieces.width), BF),
            pltpu.SemaphoreType.DMA((pieces.copies,)),
        ],
        flops=2 * rows * depth * pieces.width,
        nbytes=2 * (rows * depth + depth * pieces.width + 2 * rows * pieces.width),
        in_specs=[SMEM, VMEM] + [HBM] * pieces.count,
        after=after,
    )


def back_body(pieces, parts, blocks, where, left_ref, *refs):
    outs, (held, sems), refs = refs[-2 - blocks : -2], refs[-2:], refs[: -2 - blocks]
    groups = fetch_parts(pieces, where, refs, held, sems, parts)
    rows = pieces.part_rows
    chunk = min(256, rows)
    tall = outs[0].shape[0]
    for bit in range(parts):
        for copy in groups[bit]:
            copy.wait()

        def step(number, carry, bit=bit):
            spot = pl.ds(pl.multiple_of(number * chunk, chunk), chunk)
            weight = held[bit, spot, :]
            first = pl.multiple_of((where[0] ^ bit) * rows + number * chunk, 128)
            for block, out_ref in enumerate(outs):
                left = left_ref[block * tall : (block + 1) * tall, :]
                out_ref[:, pl.ds(first, chunk)] = dot_cols(left, weight).astype(out_ref.dtype)
            return carry

        lax.fori_loop(0, rows // chunk, step, 0)


def back_mm(where, left, pieces, parts, kind, blocks=1, after=()):
    rows, depth = left.shape
    width = parts * pieces.part_rows
    return call(
        functools.partial(back_body, pieces, parts, blocks),
        [shape((rows // blocks, width), kind)] * blocks,
        [where, left, *pieces.args()],
        [
            pltpu.VMEM((parts, pieces.part_rows, pieces.width), BF),
            pltpu.SemaphoreType.DMA((pieces.copies,)),
        ],
        flops=2 * rows * depth * width,
        nbytes=2 * (rows * depth + depth * width + rows * width),
        in_specs=[SMEM, VMEM] + [HBM] * pieces.count,
        after=after,
    )


def spans_of(width):
    groups = [(first, min(512, width - first)) for first in range(0, width, 512)]
    return [
        (first, size, [(at_, min(256, size - at_)) for at_ in range(0, size, 256)])
        for first, size in groups
    ]


def feed_body(pieces, parts, counts, where, *refs):
    tokens, refs = refs[: counts[0]], refs[counts[0] :]
    grads, refs = refs[: counts[1]], refs[counts[1] :]
    down_ref, refs = refs[0], refs[1:]
    weights, refs = refs[: pieces.count], refs[pieces.count :]
    hid_ref, wide_ref, normed, grad, wide_w, down_w, sems = refs
    cols = pieces.width // 2
    number = 0

    def go(source, target):
        nonlocal number
        copy = pltpu.make_async_copy(source, target, sems.at[number])
        copy.start()
        number += 1
        return copy

    def stack(sources, target):
        row, copies = 0, []
        for source in sources:
            rows = source.shape[0]
            copies.append(go(source, target.at[pl.ds(row, rows), :]))
            row += rows
        return copies

    first_copies = stack(tokens, normed)
    groups = []
    for first, size, _ in spans_of(cols):
        group = []
        for bit in range(parts):
            base = pl.multiple_of((where[0] ^ bit) * pieces.part_rows, pieces.cell)
            for source, row, rows, side in pieces.moves(where, weights, bit, first, size):
                spot = pl.multiple_of(base + row, pieces.cell)
                target = wide_w.at[pl.ds(spot, rows), pl.ds(side * cols + first, size)]
                group.append(go(source, target))
        group.append(go(down_ref.at[pl.ds(first, size), :], down_w.at[pl.ds(first, size), :]))
        groups.append(group)
        if first == 0:
            first_copies += stack(grads, grad)
    for copy in first_copies:
        copy.wait()
    total = normed.shape[0]
    tall = min(512, total)
    for (first, size, pieces_), group in zip(spans_of(cols), groups):
        for copy in group:
            copy.wait()
        for offset, width in pieces_:
            left = first + offset
            gate_cols = slice(left, left + width)
            up_cols = slice(cols + left, cols + left + width)

            def step(block, carry, gate_cols=gate_cols, up_cols=up_cols):
                rows = pl.ds(pl.multiple_of(block * tall, tall), tall)
                gate = dot(normed[rows, :], wide_w[:, gate_cols])
                up = dot(normed[rows, :], wide_w[:, up_cols])
                back = dot_cols(grad[rows, :], down_w[gate_cols, :])
                sig = 1.0 / (1.0 + jnp.exp(-gate))
                silu = gate * sig
                hid_ref[rows, gate_cols] = (silu * up).astype(BF)
                wide_ref[rows, up_cols] = (back * silu).astype(BF)
                slope = sig * (1.0 + gate * (1.0 - sig))
                wide_ref[rows, gate_cols] = (back * up * slope).astype(BF)
                return carry

            lax.fori_loop(0, total // tall, step, 0)


def feed(where, tokens, grads, down, pieces, parts):
    rows = sum(a.shape[0] for a in tokens)
    depth = tokens[0].shape[1]
    cols = pieces.width // 2
    copies = len(tokens) + len(grads)
    copies += len(spans_of(cols)) * (2 * pieces.copies + 1)
    return call(
        functools.partial(feed_body, pieces, parts, (len(tokens), len(grads))),
        [
            shape((rows, cols), BF),
            shape((rows, 2 * cols), BF),
            shape((rows, depth), BF),
            shape((rows, depth), BF),
        ],
        [where, *tokens, *grads, down, *pieces.args()],
        [
            pltpu.VMEM((depth, 2 * cols), BF),
            pltpu.VMEM((cols, depth), BF),
            pltpu.SemaphoreType.DMA((copies,)),
        ],
        flops=6 * rows * depth * cols,
        nbytes=6 * depth * cols + 4 * rows * depth + 6 * rows * cols,
        in_specs=[SMEM] + [HBM] * (len(tokens) + len(grads) + 1 + pieces.count),
    )


def grad_body(more, where, left_ref, right_ref, *refs):
    total = dot_rows(left_ref[...], right_ref[...])
    if more:
        total = total.astype(BF).astype(F32) + refs[0][...].astype(F32)
    refs[-1][...] = total.astype(BF)


def grad_mm(where, left, right, side, parts, got=None, after=()):
    rows, depth = left.shape
    width = right.shape[1]
    half = depth // parts // 2
    more = got is not None
    column = lambda b, w: (0, (w[0] ^ b) * 2 + (w[2] ^ side))
    block = pl.BlockSpec((half, width), lambda b, w: (b, 0))
    return call(
        functools.partial(grad_body, more),
        shape((parts * half, width), BF),
        [where, left, right] + [got] * more,
        flops=2 * rows * parts * half * width,
        nbytes=2 * (rows * parts * half + rows * width + parts * half * width),
        grid=(parts,),
        in_specs=[
            pl.BlockSpec((rows, half), column),
            pl.BlockSpec((rows, width), lambda b, w: (0, 0)),
        ]
        + [block] * more,
        out_specs=block,
        after=after,
        prefetch=True,
    )


def grad_columns(where, left, right, side, got=None, after=()):
    rows, depth = left.shape
    width = right.shape[1] // 2
    steps = 2
    more = got is not None
    column = lambda n, w: (0, (w[2] ^ side) * steps + n)
    block = pl.BlockSpec((depth, width // steps), lambda n, w: (0, n))
    return call(
        functools.partial(grad_body, more),
        shape((depth, width), BF),
        [where, left, right] + [got] * more,
        flops=2 * rows * depth * width,
        nbytes=2 * (rows * depth + rows * width + depth * width),
        grid=(steps,),
        in_specs=[
            pl.BlockSpec((rows, depth), lambda n, w: (0, 0)),
            pl.BlockSpec((rows, width // steps), column),
        ]
        + [block] * more,
        out_specs=block,
        after=after,
        prefetch=True,
    )


def mix_body(left_ref, right_ref, out_ref):
    out_ref[...] = dot(left_ref[...], right_ref[...]).astype(BF)


def mix(left, right, blocks, after=()):
    rows, depth = left.shape
    width = right.shape[1]
    return call(
        mix_body,
        shape((rows, width), BF),
        [left, right],
        flops=2 * rows * depth * width,
        nbytes=2 * (rows * depth + depth * width + rows * width),
        grid=(blocks,),
        in_specs=[
            pl.BlockSpec((rows // blocks, depth), lambda n: (n, 0)),
            pl.BlockSpec((depth, width), lambda n: (0, 0)),
        ],
        out_specs=pl.BlockSpec((rows // blocks, width), lambda n: (n, 0)),
        after=after,
    )


def key_value_body(pieces, parts, where, x_ref, gain_ref, cos_ref, sin_ref, tag_ref, *refs):
    (normed_ref, out_ref, held, sems), refs = refs[-4:], refs[:-4]
    groups = fetch_parts(pieces, where, refs, held, sems, parts)
    x = x_ref[...].astype(F32)
    normed_ref[...] = (x * rms_scale(x) * gain_ref[0:1, :]).astype(BF)
    rows = x.shape[0]
    both = 0.0
    for bit in range(parts):
        for copy in groups[bit]:
            copy.wait()
        first = pl.multiple_of((where[0] ^ bit) * pieces.part_rows, 128)
        both = both + dot(normed_ref[:, pl.ds(first, pieces.part_rows)], held[bit])
    cosine = jnp.concatenate([cos_ref[...]] * (KW // 128), 1)
    sine = jnp.concatenate([sin_ref[...]] * (KW // 128), 1)
    keys = spin(both[:, :KW], cosine, sine)
    out_ref[:rows, :KW] = keys.astype(BF)
    out_ref[:rows, KW:] = both[:, KW:].astype(BF)
    out_ref[rows:, :] = tag_ref[...]


def seq_keys(kv_refs, seq, head, tok):
    rows = pl.ds(seq * tok, tok)
    found = []
    for first in (head * HD, KW + head * HD):
        sides = [ref[:, rows, first : first + HD].reshape(-1, HD) for ref in kv_refs]
        found.append(jnp.concatenate(sides, 0))
    return found


def fill_bias(kv_refs, tag_ref, bias_ref, seq, tok, rows):
    levels = kv_refs[0].shape[0]
    row = lax.broadcasted_iota(jnp.int32, (EXTRA, 128), 0)

    def start_of(block):
        return jnp.sum(jnp.where(row == seq, block.astype(F32), 0.0), 0, keepdims=True)

    own = start_of(tag_ref[:, 0:128])
    ahead = (
        lax.broadcasted_iota(jnp.int32, (tok, 128), 0)
        - lax.broadcasted_iota(jnp.int32, (tok, 128), 1)
    ).astype(F32)
    for run in range(2 * levels):
        tags = kv_refs[run // levels][run % levels, rows : rows + EXTRA, 0:128]
        lead = (start_of(tags) - own) * float(tok)
        block = jnp.where(ahead + lead <= 0.0, 0.0, MASKED)
        bias_ref[run * tok : (run + 1) * tok, :] = jnp.concatenate([block, block], 1)


def stack_heads(two):
    return jnp.concatenate([two[:, :HD], two[:, HD:]], 0)


def lay_heads(stacked):
    tok = stacked.shape[0] // 2
    return jnp.concatenate([stacked[:tok], stacked[tok:]], 1)


def attend_body(seq, q_ref, kept_ref, other_ref, tag_ref, cos_ref, sin_ref, rot_ref, out_ref, log_ref, bias_ref):
    tok = q_ref.shape[0]
    kv_refs = (kept_ref, other_ref)
    rows = kept_ref.shape[1] - EXTRA
    fill_bias(kv_refs, tag_ref, bias_ref, seq, tok, rows)
    for head in range(KVH):
        keys, values = seq_keys(kv_refs, seq, head, tok)
        values_t = values.astype(F32).T.astype(BF)

        def pair(number, carry, head=head, keys=keys, values_t=values_t):
            first = head * GROUP + 2 * number
            lanes = pl.ds(pl.multiple_of(first * HD, 128), 128)
            turned = spin(q_ref[:, lanes], cos_ref[...], sin_ref[...]).astype(BF)
            turned = turned * jnp.asarray(HD**-0.5, BF)
            rot_ref[:, lanes] = turned
            scores = dot_cols(keys, stack_heads(turned)) + bias_ref[...]
            top = jnp.max(scores, 0, keepdims=True)
            weights = jnp.exp(scores - top)
            total = jnp.sum(weights, 0, keepdims=True)
            shares = (weights * (1.0 / total)).astype(BF)
            mixed = dot(values_t, shares).T
            out_ref[:, lanes] = lay_heads(mixed).astype(BF)
            logs = top + jnp.log(total)
            log_ref[0, pl.ds(first, 1), :] = logs[:, :tok]
            log_ref[0, pl.ds(first + 1, 1), :] = logs[:, tok:]
            return carry

        lax.fori_loop(0, GROUP // 2, pair, 0)


def attend(seq, query_raw, kv, tag, cosine, sine, tok, after=()):
    width = query_raw.shape[1]
    runs = 2 * kv[0].shape[0]
    block = pl.BlockSpec((tok, width), lambda s: (seq, 0))
    table = pl.BlockSpec((tok, 128), lambda s: (seq, 0))
    fixed = lambda dims: pl.BlockSpec(dims, lambda s: (0,) * len(dims))
    return call(
        functools.partial(attend_body, seq),
        [shape((tok, width), BF), shape((tok, width), BF), shape((1, H, tok), F32)],
        [query_raw, *kv, tag, cosine, sine],
        [pltpu.VMEM((runs * tok, 2 * tok), F32)],
        flops=16 * H * tok * runs * tok * HD,
        nbytes=tok * width * 8,
        grid=(1,),
        in_specs=[block, fixed(kv[0].shape), fixed(kv[0].shape), fixed(tag.shape), table, table],
        out_specs=[fixed((tok, width)), fixed((tok, width)), fixed((1, H, tok))],
        after=after,
    )


def attend_back_body(
    seq, heads, rot_ref, kept_ref, other_ref, tag_ref, log_ref, grad_ref, cos_ref, sin_ref, dq_ref,
    dkept_ref, dother_ref, bias_ref, dk_ref, dv_ref,
):
    tok = rot_ref.shape[0]
    kv_refs = (kept_ref, other_ref)
    rows = kept_ref.shape[1] - EXTRA
    levels = kept_ref.shape[0]
    fill_bias(kv_refs, tag_ref, bias_ref, seq, tok, rows)
    for head in heads:
        keys, values = seq_keys(kv_refs, seq, head, tok)
        keys_t = keys.astype(F32).T.astype(BF)
        dk_ref[...] = jnp.zeros_like(dk_ref)
        dv_ref[...] = jnp.zeros_like(dv_ref)

        def pair(number, carry, head=head, keys=keys, values=values, keys_t=keys_t):
            first = head * GROUP + 2 * number
            lanes = pl.ds(pl.multiple_of((first - heads[0] * GROUP) * HD, 128), 128)
            queries = stack_heads(rot_ref[:, lanes])
            grads = stack_heads(grad_ref[:, lanes])
            logs = jnp.concatenate(
                [log_ref[0, pl.ds(first, 1), :], log_ref[0, pl.ds(first + 1, 1), :]], 1
            )
            shares = jnp.exp(dot_cols(keys, queries) + bias_ref[...] - logs)
            grad_shares = dot_cols(values, grads)
            inner = jnp.sum(shares * grad_shares, 0, keepdims=True)
            grad_scores = (shares * (grad_shares - inner)).astype(BF)
            dk_ref[...] += dot(grad_scores, queries)
            dv_ref[...] += dot(shares.astype(BF), grads)
            grad_q = (dot(keys_t, grad_scores) * HD**-0.5).T
            grad_q = spin(lay_heads(grad_q), cos_ref[...], -sin_ref[...])
            dq_ref[:, lanes] = grad_q.astype(BF)
            return carry

        lax.fori_loop(0, GROUP // 2, pair, 0)
        low, high = (head - heads[0]) * HD, (head - heads[0] + 1) * HD
        step = len(heads) * HD
        for side, out_ref in enumerate((dkept_ref, dother_ref)):
            span = slice(side * levels * tok, (side + 1) * levels * tok)
            out_ref[:, :, low:high] = dk_ref[span, :].astype(BF).reshape(levels, tok, HD)
            out_ref[:, :, step + low : step + high] = (
                dv_ref[span, :].astype(BF).reshape(levels, tok, HD)
            )


def attend_back(seq, heads, rot, kv, tag, logs, grad, cosine, sine, tok, after=()):
    width = len(heads) * GROUP * HD
    lane = heads[0] // len(heads)
    runs = 2 * kv[0].shape[0]
    table = pl.BlockSpec((tok, 128), lambda s: (seq, 0))
    fixed = lambda dims: pl.BlockSpec(dims, lambda s: (0,) * len(dims))
    moved = (runs // 2, tok, 2 * len(heads) * HD)
    return call(
        functools.partial(attend_back_body, seq, heads),
        [shape((tok, width), BF)] + [shape(moved, BF)] * 2,
        [rot, *kv, tag, logs, grad, cosine, sine],
        [
            pltpu.VMEM((runs * tok, 2 * tok), F32),
            pltpu.VMEM((runs * tok, HD), F32),
            pltpu.VMEM((runs * tok, HD), F32),
        ],
        flops=10 * len(heads) * GROUP * tok * runs * tok * HD,
        nbytes=tok * width * 8,
        grid=(1,),
        in_specs=[
            pl.BlockSpec((tok, width), lambda s: (0, lane)),
            fixed(kv[0].shape),
            fixed(kv[0].shape),
            fixed(tag.shape),
            fixed((1, H, tok)),
            pl.BlockSpec((tok, width), lambda s: (seq, lane)),
            table,
            table,
        ],
        out_specs=[fixed((tok, width))] + [fixed(moved)] * 2,
        after=after,
    )


def kv_back_body(*refs):
    parts, (cos_ref, sin_ref, out_ref) = refs[:-3], refs[-3:]
    total = parts[0][...].astype(F32)
    for part in parts[1:]:
        total = total + part[...].astype(F32)
    cosine = jnp.concatenate([cos_ref[...]] * (KW // 128), 1)
    sine = jnp.concatenate([sin_ref[...]] * (KW // 128), 1)
    out_ref[:, :KW] = spin(total[:, :KW], cosine, -sine).astype(BF)
    out_ref[:, KW:] = total[:, KW:].astype(BF)


def place_body(plan, count, outs, where, *refs):
    pieces, targets = refs[:count], refs[count : count + outs]
    held, wide, in_sems, out_sems = refs[count + outs :]
    mine, core = where[0], where[2]
    reads, writes = [], []
    for number, (piece, first, column, rows, cols, target, place) in enumerate(plan):
        slot = number % 2
        top, left = place(mine, core)
        reads.append(
            pltpu.make_async_copy(
                pieces[piece].at[pl.ds(first, rows), pl.ds(column, cols)],
                held.at[slot, pl.ds(0, rows), pl.ds(0, cols)],
                in_sems.at[slot],
            )
        )
        writes.append(
            pltpu.make_async_copy(
                wide.at[slot, pl.ds(0, rows), pl.ds(0, cols)],
                targets[target].at[pl.ds(top, rows), pl.ds(left, cols)],
                out_sems.at[slot],
            )
        )
    reads[0].start()
    for number, (_, _, _, rows, cols, _, _) in enumerate(plan):
        slot = number % 2
        if number + 1 < len(plan):
            reads[number + 1].start()
        reads[number].wait()
        if number >= 2:
            writes[number - 2].wait()
        wide[slot, :rows, :cols] = held[slot, :rows, :cols].astype(F32)
        writes[number].start()
    for copy in writes[-2:]:
        copy.wait()


def place(where, pieces, plan, outs):
    hbm = pl.BlockSpec(memory_space=pl.ANY)
    rows = max(step[3] for step in plan)
    cols = max(step[4] for step in plan)
    moved = sum(step[3] * step[4] for step in plan)
    return call(
        functools.partial(place_body, plan, len(pieces), len(outs)),
        [shape(dims, F32) for dims in outs],
        [where, *pieces],
        [
            pltpu.VMEM((2, rows, cols), BF),
            pltpu.VMEM((2, rows, cols), F32),
            pltpu.SemaphoreType.DMA((2,)),
            pltpu.SemaphoreType.DMA((2,)),
        ],
        nbytes=6 * moved,
        in_specs=[pl.BlockSpec(memory_space=pltpu.SMEM)] + [hbm] * len(pieces),
        out_specs=[hbm] * len(outs),
    )


def on_device(
    hidden_in,
    positions,
    cotangent,
    norm_gain,
    w_query,
    w_key,
    w_value,
    w_out,
    ffn_gain,
    w_gate,
    w_up,
    w_down,
):
    seq_count, tok_count, model_width = hidden_in.shape
    row_count = seq_count * tok_count
    parts = lax.axis_size("fsdp")
    runs = lax.axis_size("ctx")
    levels = runs // 2
    mine = lax.axis_index("fsdp").astype(jnp.int32)
    run = lax.axis_index("ctx").astype(jnp.int32)
    core = lax.rem(run, 2)
    level = run // 2
    quarter = lax.rem(run, 4)
    where = jnp.stack([mine, quarter, core, level])
    shard = model_width // parts
    half = shard // 2
    ff_part = w_down.shape[0]
    aligned = ff_part % 128 == 0

    def hop(array, bit):
        return lax.ppermute(array, "fsdp", [(i, i ^ bit) for i in range(parts)])

    def swap_run(array, bit):
        return lax.ppermute(array, "ctx", [(i, i ^ bit) for i in range(runs)])

    def level_send(array, pairs):
        return lax.ppermute(
            array, "ctx", [(2 * a + k, 2 * b + k) for a, b in pairs for k in range(2)]
        )

    def tie(values, *after):
        many = isinstance(values, (list, tuple))
        flat = list(values) if many else [values]
        tied = lax.optimization_barrier((*flat, *after))[: len(flat)]
        return list(tied) if many else tied[0]

    def add(a, b):
        return (a.astype(F32) + b.astype(F32)).astype(BF)

    def spread(local):
        if parts != 4:
            return [hop(local, bit) for bit in range(1, parts)]
        middle = local.shape[0] // 2
        from_x, from_y = hop(local, 1), hop(local, 2)
        return [from_x, from_y, hop(from_x[:middle], 2), hop(from_y[middle:], 1)]

    def halves(own, pieces, others, width):
        cell = own[0].shape[0] // 2
        blocks = [(bit - 1, 0, 0, 0, bit) for bit in range(1, parts)]
        bit = 1
        for number, other in enumerate(others):
            for row in range(0, other.shape[0], cell):
                blocks.append((parts - 1 + number, row, 0, 1, bit))
                bit += 1
        return Pieces(own, pieces + list(others), blocks, cell, width)

    def hops(local):
        return [hop(local, bit) for bit in range(1, parts)]

    def turn(array):
        return level_send(array, [(i, (i + 1) % levels) for i in range(levels)])

    def columns_of(sources, index, cols):
        cell = sources[0].shape[0] // runs
        return jnp.concatenate(
            [lax.dynamic_slice(a, (run * cell, index * cols), (cell, cols)) for a in sources],
            1,
        )

    def lay_rows(pieces):
        rows, cell, width = pieces.part_rows, pieces.cell, pieces.width
        step = width // len(pieces.own)
        local = jnp.concatenate([at(a, mine * step, step, 1) for a in pieces.own], 1)
        whole = jnp.zeros((parts * rows, width), BF)
        whole = lax.dynamic_update_slice(whole, local, (mine * rows, 0))
        for source, first, back, flip, bit in pieces.blocks:
            side = lax.rem(level + levels - back, levels) * 2 + (core ^ flip)
            spot = (mine ^ bit) * rows + side * cell
            piece = pieces.sources[source][first : first + cell]
            whole = lax.dynamic_update_slice(whole, piece, (spot, 0))
        return whole

    def sum_first(blocks):
        if parts != 4:
            return [hop(blocks[bit], bit) for bit in range(1, parts)]
        middle = blocks[0].shape[0] // 2
        return [hop(blocks[3][middle:], 1), hop(blocks[3][:middle], 2)]

    def sum_second(blocks, got):
        if parts != 4:
            return got
        middle = blocks[0].shape[0] // 2
        to_x = jnp.concatenate([add(blocks[1][:middle], got[1]), blocks[1][middle:]], 0)
        to_y = jnp.concatenate([blocks[2][:middle], add(blocks[2][middle:], got[0])], 0)
        return [hop(to_x, 1), hop(to_y, 2)]

    def sum_last(blocks, got):
        return sum([a.astype(F32) for a in got], blocks[0].astype(F32))

    def far_of(pieces):
        if parts != 4:
            return []
        half_ = pieces[0].shape[0] // 2
        return [hop(pieces[0][:half_], 2), hop(pieces[1][half_:], 1)]

    def near_of(local):
        return [hop(local, bit) for bit in ((1, 2) if parts == 4 else range(1, parts))]

    middle_level = levels // 2
    last_level = levels - 1
    ups = [[(s, s + 1), (last_level - s, last_level - s - 1)] for s in range(middle_level - 1)]
    over = [(middle_level - 1, middle_level), (middle_level, middle_level - 1)]
    downs = [[(b, a) for a, b in pairs] for pairs in reversed(ups)]

    class Climb:
        def __init__(self, value):
            self.value, self.stage = value, 0

        def start(self):
            self.moving = level_send(self.value, (ups + [over] + downs)[self.stage])
            return self.moving

        def take(self, got):
            if self.stage < middle_level:
                self.value = add(self.value, got)
            else:
                s = 2 * middle_level - 2 - self.stage
                ends = (level == s) | (level == last_level - s)
                self.value = jnp.where(ends, got, self.value)
            self.stage += 1

        @property
        def done(self):
            return self.stage == 2 * middle_level - 1

    def complete(climb):
        while not climb.done:
            climb.take(climb.start())
        return climb

    def both_ways(new, old):
        if levels != 4 or new.value.shape != old.value.shape:
            return [new.start(), old.start()]
        inner = (level == 1) | (level == 2)
        sent = jnp.where(inner, old.value, new.value)
        return [level_send(sent, [(0, 1), (1, 0), (2, 3), (3, 2)])]

    def take_both(new, old, got):
        if len(got) == 2:
            new.take(got[0])
            old.take(got[1])
            return
        inner = (level == 1) | (level == 2)
        new.value = jnp.where(inner, add(new.value, got[0]), new.value)
        old.value = jnp.where(inner, old.value, got[0])
        new.stage += 1
        old.stage += 1

    def advance(climbs):
        return [c.start() for c in climbs]

    def take(climbs, results):
        for climb, got in zip(climbs, results):
            climb.take(got)

    gains = jnp.stack([norm_gain, ffn_gain] + [jnp.zeros_like(norm_gain)] * (EXTRA - 2), 0)
    own_kv = jnp.concatenate([w_key, w_value], 1)
    wide = own_kv.shape[1] // shard
    tag_rows = jnp.concatenate([gains] * wide, 1)
    sent_kv = jnp.concatenate([at(own_kv, core * half, half), tag_rows], 0)
    got_kv = [hop(sent_kv, bit) for bit in range(1, parts)]
    own_query = at(w_query, core * half, half)
    near_query = [hop(own_query, bit) for bit in range(1, min(3, parts))]
    got_kv = tie(got_kv)
    kv_pieces = [a[:half] for a in got_kv]
    other_kv = swap_run(jnp.concatenate(kv_pieces, 0), 1)
    rest_query = [hop(tie(own_query, *got_kv), bit) for bit in range(3, parts)]
    key_value_w = halves([own_kv], kv_pieces, [other_kv], own_kv.shape[1])
    gain_cells = [gains] + [a[half:, :shard] for a in got_kv]
    all_gains = jnp.zeros((EXTRA, model_width), BF)
    for bit in range(parts):
        all_gains = lax.dynamic_update_slice(
            all_gains, gain_cells[bit], (0, (mine ^ bit) * shard)
        )
    all_gains = all_gains.astype(F32)
    gain_one, gain_two = all_gains[0], all_gains[1]

    spread_of = 10000.0 ** (-jnp.arange(HD // 2, dtype=F32) / (HD // 2))
    turned = positions.astype(F32).reshape(row_count, 1) * spread_of
    cosine = jnp.concatenate([jnp.cos(turned)] * 4, 1)
    sine = jnp.concatenate([-jnp.sin(turned), jnp.sin(turned)] * 2, 1)
    starts = (positions[:, :1] // tok_count).astype(BF)
    tag = jnp.concatenate(
        [
            jnp.broadcast_to(starts, (seq_count, 2 * KW)),
            jnp.zeros((EXTRA - seq_count, 2 * KW), BF),
        ],
        0,
    )

    x_low = hidden_in.reshape(row_count, model_width)
    normed_one, packed = call(
        functools.partial(key_value_body, key_value_w, parts),
        [shape((row_count, model_width), BF), shape((row_count + EXTRA, 2 * KW), BF)],
        [where, x_low, all_gains, cosine, sine, tag, *key_value_w.args()],
        [
            pltpu.VMEM((parts, shard, 2 * KW), BF),
            pltpu.SemaphoreType.DMA((key_value_w.copies,)),
        ],
        flops=4 * row_count * model_width * KW,
        nbytes=row_count * model_width * 4 + model_width * KW * 4,
        in_specs=[SMEM] + [VMEM] * 5 + [HBM] * key_value_w.count,
    )
    turns = [packed]
    while len(turns) < levels:
        turns.append(turn(turns[-1]))
    got_query = tie(near_query + rest_query, turns[-1])
    kept_kv = jnp.stack(turns, 0)
    kv = [kept_kv, swap_run(kept_kv, 1)]
    other_query = swap_run(jnp.concatenate(got_query, 0), 1)
    sent_wide = [columns_of([w_gate, w_up], mine ^ bit, ff_part) for bit in range(1, parts)]
    sent_wide = tie(sent_wide, *got_query)
    wide_hops = [hop(a, bit + 1) for bit, a in enumerate(sent_wide)]
    query_w = halves([w_query], got_query, [other_query], w_query.shape[1])
    query_raw = forward_mm(where, normed_one, query_w, parts)

    wide_hops = tie(wide_hops, query_raw)
    rings = [jnp.concatenate(wide_hops, 0)]
    moving = turn(rings[0])
    near_out = near_of(at(tie(w_out, *wide_hops), core * half, half))
    forward = [
        attend(0, query_raw, kv, tag, cosine, sine, tok_count, after=[rings[0]])
    ]
    moving, *near_out = tie([moving, *near_out], forward[0][1])
    rings.append(moving)
    moving = turn(rings[1])
    far_out = far_of(near_out)
    grad_y_low = cotangent.reshape(row_count, model_width)
    near_dm = near_of(tie(grad_y_low, *near_out))
    for seq in range(1, seq_count):
        forward.append(
            attend(
                seq, query_raw, kv, tag, cosine, sine, tok_count, after=[rings[-1], *near_out]
            )
        )
    rot, attended, logs = [list(a) for a in zip(*forward)]
    moving, *far_out = tie([moving, *far_out], attended[-1])
    rings.append(moving)
    far_out = [jnp.concatenate(far_out, 0)] if parts == 4 else far_out
    got_out = near_out + far_out
    other_out = [swap_run(jnp.concatenate(got_out, 0), 1)]
    while len(rings) < levels - 1:
        rings.append(turn(rings[-1]))
    moving = turn(rings[-1])
    out_w = halves([w_out], got_out, other_out, w_out.shape[1])
    attended = jnp.concatenate(attended, 0)
    inputs = x_low.astype(F32)
    residual = inputs + forward_mm(where, attended, out_w, parts)
    scale_two = rms_scale(residual)
    normed_two = (residual * scale_two * gain_two).astype(BF)
    near_normed = near_of(normed_two)
    far_dm = far_of(tie(near_dm, residual))
    far_normed = far_of(near_normed)
    rings.append(moving)
    other_wide = swap_run(jnp.concatenate(rings, 0), 1)
    all_normed = [normed_two] + near_normed + far_normed
    all_dm = [grad_y_low] + near_dm + far_dm
    cell = shard // runs
    blocks = []
    for back in range(levels):
        for bit in range(1, parts):
            blocks.append((back, (bit - 1) * cell, back, 0, bit))
            blocks.append((levels, (back * (parts - 1) + bit - 1) * cell, back, 1, bit))
    wide_w = Pieces([w_gate, w_up], rings + [other_wide], blocks, cell, 2 * ff_part, levels)

    if aligned:
        hidden_low, grad_wide_in, stacked, stacked_dm = feed(
            where, all_normed, all_dm, w_down, wide_w, parts
        )
    else:
        laid = lay_rows(wide_w)
        stacked, stacked_dm = jnp.concatenate(all_normed, 0), jnp.concatenate(all_dm, 0)
        gate_proj, up_proj = dot(stacked, laid[:, :ff_part]), dot(stacked, laid[:, ff_part:])
        sigmoid_gate = jax.nn.sigmoid(gate_proj)
        hidden_low = (gate_proj * sigmoid_gate * up_proj).astype(BF)
        grad_hidden = dot_cols(stacked_dm, w_down)
        grad_up_in = (grad_hidden * gate_proj * sigmoid_gate).astype(BF)
        slope = sigmoid_gate * (1.0 + gate_proj * (1.0 - sigmoid_gate))
        grad_wide_in = jnp.concatenate(
            [(grad_hidden * up_proj * slope).astype(BF), grad_up_in], 1
        )

    def blocks_of(total):
        return [total[b * half : (b + 1) * half] for b in range(parts)]

    def split(both, *counts):
        out = []
        for count in counts:
            out.append(both[:count])
            both = both[count:]
        return [*out, both]

    def values(climbs):
        return [c.value for c in climbs]

    down_rows = ff_part // 2
    middle = model_width // 2

    def both_rows(done, first, cols, target, row=0):
        return [
            (done[0], first, cols, target, lambda m, k: (k * half + row, 0)),
            (done[1], first, cols, target, lambda m, k: ((1 - k) * half + row, 0)),
        ]

    def put(steps, outs):
        pieces, plan = [], []
        for piece, column, cols, target, spot in steps:
            if not any(piece is p for p in pieces):
                pieces.append(piece)
            index = [piece is p for p in pieces].index(True)
            rows = piece.shape[0]
            plan.append((index, 0, column, rows, cols, target, spot))
        return place(where, pieces, plan, outs)

    full = (shard, parts * ff_part)

    def place_wide(wide_done):
        if not aligned:
            outs = [jnp.zeros(full, F32), jnp.zeros(full, F32)]
            for bit in range(parts):
                for side in range(2):
                    spot = ((core ^ side) * half, (mine ^ bit) * ff_part)
                    piece = wide_done[bit][side].astype(F32)
                    for number in range(2):
                        part = piece[:, number * ff_part : (number + 1) * ff_part]
                        outs[number] = lax.dynamic_update_slice(outs[number], part, spot)
            return outs
        steps = []
        for bit in range(parts):
            for side in range(2):
                for target in range(2):

                    def spot(m, k, bit=bit, side=side):
                        row = pl.multiple_of((k ^ side) * half, half)
                        return row, pl.multiple_of((m ^ bit) * ff_part, 128)

                    steps.append(
                        (wide_done[bit][side], target * ff_part, ff_part, target, spot)
                    )
        return put(steps, [full, full])

    def place_down(down_done):
        if not aligned:
            out = jnp.zeros((ff_part, model_width), F32)
            for number in range(2):
                for side in range(2):
                    spot = (number * down_rows, (core ^ side) * middle)
                    piece = down_done[number][side].astype(F32)
                    out = lax.dynamic_update_slice(out, piece, spot)
            return out
        steps = []
        for number in range(2):
            for side in range(2):

                def spot(m, k, number=number, side=side):
                    return number * down_rows, pl.multiple_of((k ^ side) * middle, 128)

                steps.append((down_done[number][side], 0, middle, 0, spot))
        return put(steps, [(ff_part, model_width)])[0]

    def sync(*groups):
        flat = [a for group in groups for a in group]
        flat = list(lax.optimization_barrier(tuple(flat)))
        out = []
        for group in groups:
            out.append(flat[: len(group)])
            flat = flat[len(group) :]
        return out

    def sync_climbs(climbs, *groups):
        held, *rest = sync(values(climbs), *groups)
        for climb, value in zip(climbs, held):
            climb.value = value
        return rest

    down_sent = dot_rows(hidden_low, at(stacked_dm, (1 - core) * middle, middle, 1)).astype(BF)
    (down_sent,), (hidden_low,) = sync([down_sent], [hidden_low])
    down_got = swap_run(down_sent, 1)
    down_kept = dot_rows(hidden_low, at(stacked_dm, core * middle, middle, 1)).astype(BF)
    down_pair = add(down_kept, down_got)
    down = [Climb(down_pair[i * down_rows : (i + 1) * down_rows]) for i in range(2)]

    moving = advance(down[:1])
    if aligned:
        back_blocks = back_mm(
            where, grad_wide_in, wide_w, parts, BF, parts, after=values(down)
        )
    else:
        back_rows = dot_cols(grad_wide_in, laid).astype(BF)
        back_blocks = [back_rows[i * row_count : (i + 1) * row_count] for i in range(parts)]
    back_got = sum_first(back_blocks)
    wide_sent = grad_mm(where, stacked, grad_wide_in, 1, parts, after=back_blocks[:1])
    take(down[:1], moving)
    (wide_sent,), back_got = sync_climbs(down, [wide_sent], back_got)

    moving = advance(down)
    wide_got = swap_run(wide_sent, 1)
    back_got = sum_second(back_blocks, back_got)
    mixed = mix(hidden_low, w_down, parts, after=[wide_sent, *values(down)])
    wide_pair = grad_mm(
        where, stacked, grad_wide_in, 0, parts, got=wide_got, after=[mixed]
    )
    take(down, moving)
    (wide_pair,), back_got, (mixed,) = sync_climbs(down, [wide_pair], back_got, [mixed])
    wide_blocks = blocks_of(wide_pair)
    mixed_blocks = [mixed[i * row_count : (i + 1) * row_count] for i in range(parts)]

    climbs = [Climb(wide_blocks[0])]
    moving = advance(down + climbs)
    near_wide = [hop(a, bit + 1) for bit, a in enumerate(wide_blocks[1:3])]
    grad_normed_two = sum_last(back_blocks, back_got)
    grad_y = grad_y_low.astype(F32)
    grad_res_norm, grad_gain_two = norm_back(grad_normed_two, residual, scale_two, gain_two)
    grad_residual = grad_y + grad_res_norm
    grad_proj = grad_residual.astype(BF)
    (grad_attended,) = back_mm(where, grad_proj, out_w, parts, BF, after=values(down))
    backward = []

    def pull(seq, number, after=()):
        heads = range(number * KVH // 2, (number + 1) * KVH // 2)
        after = list(after) + [a[0] for a in backward[-1:]]
        backward.append(
            attend_back(
                seq, heads, rot[seq], kv, tag, logs[seq], grad_attended, cosine, sine,
                tok_count, after=after,
            )
        )

    def sync_pulled(climbs, *groups):
        pulled, *rest = sync_climbs(climbs, backward[-1], *groups)
        backward[-1] = pulled
        return rest

    pull(0, 0, values(down))
    take(down + climbs, moving)
    (near_wide,) = sync_pulled(down + climbs, near_wide)

    climbs += [Climb(a) for a in near_wide]
    moving = advance(down[1:] + climbs[:2])
    rest_wide = [hop(wide_blocks[b], b) for b in range(3, parts)]
    pull(0, 1, values(down + climbs))
    pull(1, 0)
    take(down[1:] + climbs[:2], moving)
    (rest_wide,) = sync_pulled(down + climbs, rest_wide)

    climbs += [Climb(a) for a in rest_wide]
    moving = advance(climbs[1:2])
    merged = both_ways(climbs[2], climbs[0])
    swap_down = [swap_run(complete(c).value, 1) for c in down]
    pull(1, 1, values(climbs))
    for seq in range(2, seq_count):
        for number in range(2):
            pull(seq, number)

    def lay(index):
        rows = [
            [backward[2 * seq + number][index] for number in range(2)]
            for seq in range(seq_count)
        ]
        if index == 0:
            return jnp.concatenate([jnp.concatenate(r, 1) for r in rows], 0)
        step = KW // 2
        keys = jnp.concatenate([jnp.concatenate([a[..., :step] for a in r], 2) for r in rows], 1)
        rest = jnp.concatenate([jnp.concatenate([a[..., step:] for a in r], 2) for r in rows], 1)
        return jnp.concatenate([keys, rest], 2)

    out_sent = grad_mm(where, attended, grad_proj, 1, parts, after=[backward[-1][0]])
    grad_query_low = lay(0)
    query_sent = grad_mm(where, normed_one, grad_query_low, 1, parts, after=[out_sent])
    take(climbs[1:2], moving)
    take_both(climbs[2], climbs[0], merged)
    (out_sent, query_sent), swap_down = sync_pulled(
        climbs, [out_sent, query_sent], swap_down
    )

    moving = advance(climbs[2:3])
    merged = both_ways(climbs[3], climbs[1])
    other_dkv = swap_run(lay(2), 1)
    out_got = swap_run(out_sent, 1)
    by_level = add(lay(1), other_dkv)
    ring_kv = by_level[levels - 1]
    for step in reversed(range(1, levels)):
        ring_kv = level_send(ring_kv, [(i, (i - 1) % levels) for i in range(levels)])
        if step > 1:
            ring_kv = add(ring_kv, by_level[step - 1])
    out_pair = grad_mm(
        where, attended, grad_proj, 0, parts, got=out_got, after=[by_level, *values(climbs)]
    )
    (out_pair,), (query_sent,) = sync([out_pair], [query_sent])
    query_got = swap_run(query_sent, 1)
    (grad_normed_one,) = back_mm(where, grad_query_low, query_w, parts, F32, after=[out_pair])
    query_pair = grad_mm(
        where, normed_one, grad_query_low, 0, parts, got=query_got, after=[grad_normed_one]
    )
    take(climbs[2:3], moving)
    take_both(climbs[3], climbs[1], merged)
    (ring_kv,), (out_pair, query_pair) = sync_climbs(climbs, [ring_kv], [out_pair, query_pair])
    out_blocks, query_blocks = blocks_of(out_pair), blocks_of(query_pair)

    moving = advance(climbs[2:])
    out_got = sum_first(out_blocks)
    grad_kv_low = call(
        kv_back_body,
        shape((row_count, 2 * KW), BF),
        [by_level[0], ring_kv, cosine, sine],
        nbytes=row_count * KW * 4 * (levels + 1),
        after=values(climbs),
    )
    kv_sent = grad_mm(where, normed_one, grad_kv_low, 1, parts)
    out_got, (kv_sent,) = sync(out_got, [kv_sent])
    out_got = sum_second(out_blocks, out_got)
    kv_got = swap_run(kv_sent, 1)
    (grad_normed_kv,) = back_mm(where, grad_kv_low, key_value_w, parts, F32, after=[kv_sent])
    kv_pair = grad_mm(
        where, normed_one, grad_kv_low, 0, parts, got=kv_got, after=[grad_normed_kv]
    )
    grad_normed_one = grad_normed_one + grad_normed_kv
    scale_one = rms_scale(inputs)
    grad_in_norm, grad_gain_one = norm_back(grad_normed_one, inputs, scale_one, gain_one)
    grad_in = (grad_residual + grad_in_norm).reshape(seq_count, tok_count, model_width)
    gain_rows = jnp.stack([grad_gain_one, grad_gain_two], 0).astype(BF)
    gain_rows = gain_rows.reshape(2, parts, 2, half)
    gain_rows = jnp.concatenate(
        [lax.dynamic_slice(gain_rows, (0, mine ^ b, 0, 0), (2, 1, 2, half)) for b in range(parts)],
        1,
    )
    gain_sent = at(gain_rows, 1 - core, 1, 2).reshape(2, parts * half)
    gain_kept = at(gain_rows, core, 1, 2).reshape(2, parts * half)
    gain_cols = add(gain_kept, swap_run(gain_sent, 1)).T
    gain_cols = jnp.concatenate([gain_cols, jnp.zeros((parts * half, 126), BF)], 1)
    kv_blocks = blocks_of(jnp.concatenate([kv_pair, gain_cols], 1))
    take(climbs[2:], moving)
    out_got, kv_blocks, (grad_in,) = sync_climbs(climbs, out_got, kv_blocks, [grad_in])

    out_climb = Climb(sum_last(out_blocks, out_got).astype(BF))
    moving = advance([climbs[3], out_climb])
    query_mid = sum_first(query_blocks)
    swap_wide = [swap_run(complete(c).value, 1) for c in climbs[:2]]
    query_mid, swap_wide = sync(query_mid, swap_wide)
    query_end = sum_second(query_blocks, query_mid)
    kv_mid = sum_first(kv_blocks)
    take([climbs[3], out_climb], moving)
    query_end, kv_mid = sync_climbs([climbs[3], out_climb], query_end, kv_mid)

    query_climb = Climb(sum_last(query_blocks, query_end).astype(BF))
    moving = advance([out_climb, query_climb])
    kv_end = sum_second(kv_blocks, kv_mid)
    swap_wide += [swap_run(complete(c).value, 1) for c in climbs[2:]]
    down_done = [[c.value, s] for c, s in zip(down, swap_down)]
    grad_down = place_down(down_done)
    take([out_climb, query_climb], moving)
    kv_end, swap_wide, (grad_down,) = sync_climbs(
        [out_climb, query_climb], kv_end, swap_wide, [grad_down]
    )

    kv_climb = Climb(sum_last(kv_blocks, kv_end).astype(BF))
    moving = advance([kv_climb, out_climb, query_climb])
    mixed_mid = sum_first(mixed_blocks)
    wide_done = [[c.value, s] for c, s in zip(climbs, swap_wide)]
    grad_gate_w, grad_up_w = place_wide(wide_done)
    take([kv_climb, out_climb, query_climb], moving)
    mixed_mid, (grad_gate_w, grad_up_w) = sync_climbs(
        [kv_climb, out_climb, query_climb], mixed_mid, [grad_gate_w, grad_up_w]
    )

    moving = advance([query_climb, kv_climb])
    mixed_end = sum_second(mixed_blocks, mixed_mid)
    out_done = [complete(out_climb).value, swap_run(out_climb.value, 1)]
    (grad_out_w,) = put(both_rows(out_done, 0, model_width, 0), [(shard, model_width)])
    take([query_climb, kv_climb], moving)
    mixed_end, (grad_out_w,) = sync_climbs([query_climb, kv_climb], mixed_end, [grad_out_w])
    mixed_sum = sum_last(mixed_blocks, mixed_end)
    output = (residual + mixed_sum).astype(BF).reshape(seq_count, tok_count, model_width)
    query_done, kv_done = [
        [c.value, swap_run(c.value, 1)] for c in [complete(c) for c in (query_climb, kv_climb)]
    ]
    grad_query_w, grad_key_w, grad_value_w, gain_out = put(
        both_rows(query_done, 0, model_width, 0)
        + both_rows(kv_done, 0, KW, 1)
        + both_rows(kv_done, KW, KW, 2)
        + both_rows(kv_done, 2 * KW, 128, 3),
        [(shard, model_width), (shard, KW), (shard, KW), (shard, 128)],
    )
    return (
        output,
        grad_in,
        gain_out[:, 0],
        grad_query_w,
        grad_key_w,
        grad_value_w,
        grad_out_w,
        gain_out[:, 1],
        grad_gate_w,
        grad_up_w,
        grad_down,
    )


def solution(mesh):
    placed = (
        P("fsdp", "ctx", None),
        P("fsdp", "ctx"),
        P("fsdp", "ctx", None),
        P("fsdp"),
        P("fsdp", None),
        P("fsdp", None),
        P("fsdp", None),
        P("fsdp", None),
        P("fsdp"),
        P("fsdp", None),
        P("fsdp", None),
        P("fsdp", None),
    )
    return jax.shard_map(
        on_device,
        mesh=mesh,
        in_specs=placed,
        out_specs=(
            P("fsdp", "ctx", None),
            P("fsdp", "ctx", None),
            P("fsdp"),
            P("fsdp", None),
            P("fsdp", None),
            P("fsdp", None),
            P("fsdp", None),
            P("fsdp"),
            P("fsdp", None),
            P("fsdp", None),
            P("fsdp", None),
        ),
        check_vma=False,
    )
```

time: 2660 us -> 908 us (0.34)
  waiting for transfers between devices: 1960 us -> 259 us
  Pallas kernels: 0 us -> 309 us
  matrix products: 271 us -> 13.7 us
  local copies, waits for them, and re-layouts: 286 us -> 56 us
  starting transfers between devices: 0.76 us -> 138 us
  other arithmetic: 62 us -> 119 us
  blocking collectives: 54.4 us -> 0 us
    reduce_scatter x7 -> x0, waiting for transfers between devices: 772 us -> none  [the longest x1 208 us: on_device(): lax.psum_scatter(grad_up_w.astype(jnp.bfloat16), 'fsdp', scatter_dimensio...]
    all_gather x9 -> x0, waiting for transfers between devices: 772 us -> none  [the longest x1 206 us: on_device(): lax.all_gather(w_gate, 'fsdp', axis=0, tiled=True)]
    psum x1 -> x0, waiting for transfers between devices: 385 us -> none  [on_device(): lax.psum(part_query.astype(jnp.bfloat16), 'ctx').astype(jnp.float32)]
    pallas_call x0 -> x28, Pallas kernels: none -> 309 us  [the longest x20 250 us: call(): pl.pallas_call(run, out_shape=outs, in_specs=in_specs, out_specs=out_spec...]
    ppermute x0 -> x99, waiting for transfers between devices: none -> 259 us  [the longest x34 150 us: level_send(): lax.ppermute(array, 'ctx', [(2 * a + k, 2 * b + k) for a, b in pairs for...]
    dot_general x77 -> x2, matrix products: 271 us -> 13.7 us  [dot_rows(): lax.dot_general(a, b, (((0,), (0,)), ((), ())), preferred_element_type=F32)]
    unnamed x99 -> x155, local copies, waits for them, and re-layouts: 250 us -> 11.1 us
    ppermute x0 -> x99, starting transfers between devices: none -> 138 us  [the longest x34 83.4 us: level_send(): lax.ppermute(array, 'ctx', [(2 * a + k, 2 * b + k) for a, b in pairs for...]
  transfers between devices with their start and end apart: 19 -> 99, of which waited for: 15 -> 33; matrix products, arithmetic and copies ran while one was open for 17% -> 16% of each run, Pallas kernels for 0% -> 29%
where the time goes in v2:
time: 908 us; the launch traced here: 897 us
  Pallas kernels  309 us (34%)
  waiting for transfers between devices  259 us (29%)
  starting transfers between devices  138 us (15%)
  other arithmetic  119 us (13%)
  local copies, waits for them, and re-layouts  56 us (6%)
  matrix products  13.7 us (2%)
    pallas_call x20, Pallas kernels, call(): pl.pallas_call(run, out_shape=outs, in_specs=in_specs, out_specs=out_spec...  250 us
    ppermute x34, waiting for transfers between devices, level_send(): lax.ppermute(array, 'ctx', [(2 * a + k, 2 * b + k) for a, b in pairs for...  150 us
    ppermute x44, waiting for transfers between devices, hop(): return lax.ppermute(array, 'fsdp', [(i, i ^ bit) for i in range(parts)])  95.3 us
    ppermute x34, starting transfers between devices, level_send(): lax.ppermute(array, 'ctx', [(2 * a + k, 2 * b + k) for a, b in pairs for...  83.4 us
    pallas_call x8, Pallas kernels, call(): pl.pallas_call(run, out_shape=outs, grid_spec=pltpu.PrefetchScalarGridSpe...  58.3 us
    ppermute x44, starting transfers between devices, hop(): return lax.ppermute(array, 'fsdp', [(i, i ^ bit) for i in range(parts)])  51.5 us
    convert_element_type x27, other arithmetic, add(): return (a.astype(F32) + b.astype(F32)).astype(BF)  49.1 us
  transfers between devices with their start and end apart: 99, of which 33 were waited for; matrix products, arithmetic and copies ran while one was open for 16% of the time, Pallas kernels for 29%

profile of v2, /device:TPU:0, one launch (start us, length us, event | category | flops | bytes accessed | tf_op | source)
XLA Modules:
  0.0 897.1 jit_solution(16711670448965307793)
XLA Ops:
  48.4 9.8 %collective-permute-done.8 = bf16[272,512]{1,0:T(8,128)(2,1)S(1)} collective-permute-done((bf16[272,512]{1,0:T(8,128)(2,1)S(1)}, bf16[272,512]{1,0:T(8,128)(2,1)S(1)}, u32[]{:S(2)}, u32[]{:S(2)}) %collective-permute-start.8) | collective-permute-done | bytes 278560 | tf_op jit(solution)/shard_map/ppermute | solution.py:731
  58.2 10.2 %collective-permute-done.5.refs_4_ = bf16[256,2048]{1,0:T(8,128)(2,1)S(1)} collective-permute-done((bf16[256,2048]{1,0:T(8,128)(2,1)}, bf16[256,2048]{1,0:T(8,128)(2,1)S(1)}, u32[]{:S(2)}, u32[]{:S(2)}) %collective-permute-start.5) | collective-permute-done | bytes 1048608 | tf_op jit(solution)/shard_map/ppermute | solution.py:725
  100.6 22.5 %shard_map.205 = (bf16[128,2048]{1,0:T(8,128)(2,1)}, bf16[128,2048]{1,0:T(8,128)(2,1)}, f32[1,32,128]{2,1,0:T(8,128)}) custom-call(f32[256,2048]{1,0:T(8,128)} %shard_map.204.refs_0_, bf16[4,272,512]{2,1,0:T(8,128)(2,1)} %copy-done.5, bf16[4,272,512]{2,1,0:T(8,128)(2,1)} %collective-permute-done.11.refs_2_, bf16[16,512]{1,0:T(8,128)(2,1)} %concatenate.144.refs_5_.refs_3_, ...), custom_call_target="tpu_custom_call" | custom-call | flops 4294967296 | bytes 2097152 | tf_op jit(solution)/shard_map/pallas_call | solution.py:92
  129.8 22.5 %shard_map.206 = (bf16[128,2048]{1,0:T(8,128)(2,1)}, bf16[128,2048]{1,0:T(8,128)(2,1)}, f32[1,32,128]{2,1,0:T(8,128)}) custom-call(f32[256,2048]{1,0:T(8,128)} %shard_map.204.refs_0_, bf16[4,272,512]{2,1,0:T(8,128)(2,1)} %copy-done.5, bf16[4,272,512]{2,1,0:T(8,128)(2,1)} %collective-permute-done.11.refs_2_, bf16[16,512]{1,0:T(8,128)(2,1)} %concatenate.144.refs_5_.refs_3_, ...), custom_call_target="tpu_custom_call" | custom-call | flops 4294967296 | bytes 2097152 | tf_op jit(solution)/shard_map/pallas_call | solution.py:92
  159.5 23.1 %collective-permute-done.30.refs_17_.refs_7_ = bf16[192,2816]{1,0:T(8,128)(2,1)S(1)} collective-permute-done((bf16[192,2816]{1,0:T(8,128)(2,1)S(1)}, bf16[192,2816]{1,0:T(8,128)(2,1)S(1)}, u32[]{:S(2)}, u32[]{:S(2)}) %collective-permute-start.30) | collective-permute-done | bytes 1081376 | tf_op jit(solution)/shard_map/ppermute | solution.py:731
  217.4 15.0 %collective-permute-done.22.refs_2_ = bf16[256,2048]{1,0:T(8,128)(2,1)S(1)} collective-permute-done((bf16[256,2048]{1,0:T(8,128)(2,1)S(1)}, bf16[256,2048]{1,0:T(8,128)(2,1)S(1)}, u32[]{:S(2)}, u32[]{:S(2)}) %collective-permute-start.22) | collective-permute-done | bytes 1048608 | tf_op jit(solution)/shard_map/ppermute | solution.py:725
  244.9 10.5 %collective-permute-done.24.refs_4_ = bf16[128,2048]{1,0:T(8,128)(2,1)} collective-permute-done((bf16[128,2048]{1,0:T(8,128)(2,1)}, bf16[128,2048]{1,0:T(8,128)(2,1)}, u32[]{:S(2)}, u32[]{:S(2)}) %collective-permute-start.24) | collective-permute-done | bytes 524320 | tf_op jit(solution)/shard_map/ppermute | solution.py:725
  255.5 34.3 %shard_map.208 = (bf16[1024,1408]{1,0:T(8,128)(2,1)}, bf16[1024,2816]{1,0:T(8,128)(2,1)}, bf16[1024,2048]{1,0:T(8,128)(2,1)}, bf16[1024,2048]{1,0:T(8,128)(2,1)}) custom-call(s32[4]{0:T(128)} %pad_add_fusion.refs_0_, bf16[256,2048]{1,0:T(8,128)(2,1)} %copy-done.46, bf16[256,2048]{1,0:T(8,128)(2,1)} %copy-done.59, bf16[256,2048]{1,0:T(8,128)(2,1)} %copy-done.60, ...), custom_call_target="tpu_custom_call" | custom-call | flops 17716740096 | bytes 34340864 | tf_op jit(solution)/shard_map/pallas_call | solution.py:92
  314.6 19.7 %shard_map.209 = (bf16[256,2048]{1,0:T(8,128)(2,1)}, bf16[256,2048]{1,0:T(8,128)(2,1)}, bf16[256,2048]{1,0:T(8,128)(2,1)}, bf16[256,2048]{1,0:T(8,128)(2,1)}) custom-call(s32[4]{0:T(128)} %pad_add_fusion.refs_0_, bf16[1024,2816]{1,0:T(8,128)(2,1)} %get-tuple-element.194.refs_1_.refs_2_, bf16[512,5632]{1,0:T(8,128)(2,1)} %refs_2_.7, ...), custom_call_target="tpu_custom_call" | custom-call | flops 11811160064 | bytes 21495808 | tf_op jit(solution)/shard_map/pallas_call | solution.py:92
  338.8 11.5 %shard_map.210.refs_2_ = bf16[1024,2816]{1,0:T(8,128)(2,1)} custom-call(s32[4]{0:T(128)} %pad_add_fusion.refs_0_, bf16[1024,2048]{1,0:T(8,128)(2,1)} %get-tuple-element.193.refs_1_, bf16[1024,2816]{1,0:T(8,128)(2,1)} %get-tuple-element.194.refs_1_.refs_2_, bf16[256,2048]{1,0:T(8,128)(2,1)} %get-tuple-element.195.refs_3_), custom_call_target="tpu_custom_call" | custom-call | flops 5905580032 | bytes 13631488 | tf_op jit(solution)/shard_map/pallas_call | solution.py:83
  366.6 11.1 %shard_map.211.refs_4_ = bf16[1024,2048]{1,0:T(8,128)(2,1)} custom-call(bf16[1024,1408]{1,0:T(8,128)(2,1)} %get-tuple-element.191.refs_0_, bf16[1408,2048]{1,0:T(8,128)(2,1)} %refs_1_.1, bf16[1024,2816]{1,0:T(8,128)(2,1)} %shard_map.210.refs_2_, bf16[704,1024]{1,0:T(8,128)(2,1)} %add_convert_fusion.12.refs_3_, ...), custom_call_target="tpu_custom_call" | custom-call | flops 5905580032 | bytes 12845056 | tf_op jit(solution)/shard_map/pallas_call | solution.py:92
  377.7 11.9 %collective-permute-done.37 = bf16[704,1024]{1,0:T(8,128)(2,1)} collective-permute-done((bf16[704,1024]{1,0:T(8,128)(2,1)}, bf16[704,1024]{1,0:T(8,128)(2,1)}, u32[]{:S(2)}, u32[]{:S(2)}) %collective-permute-start.37) | collective-permute-done | bytes 1441824 | tf_op jit(solution)/shard_map/ppermute | solution.py:731
  396.6 12.4 %shard_map.212 = bf16[1024,2816]{1,0:T(8,128)(2,1)} custom-call(s32[4]{0:T(128)} %pad_add_fusion.refs_0_, bf16[1024,2048]{1,0:T(8,128)(2,1)} %get-tuple-element.193.refs_1_, bf16[1024,2816]{1,0:T(8,128)(2,1)} %get-tuple-element.194.refs_1_.refs_2_, bf16[1024,2816]{1,0:T(8,128)(2,1)} %collective-permute-done.38.refs_3_, bf16[1024,2048]{1,0:T(8,128)(2,1)} %shard_map.211.refs_4_), custom_call_target="tpu_custom_call" | custom-call | flops 5905580032 | bytes 13631488 | tf_op jit(solution)/shard_map/pallas_call | solution.py:83
  441.1 15.2 %shard_map.214 = (bf16[128,1024]{1,0:T(8,128)(2,1)}, bf16[4,128,256]{2,1,0:T(8,128)(2,1)}, bf16[4,128,256]{2,1,0:T(8,128)(2,1)}) custom-call(bf16[128,2048]{1,0:T(8,128)(2,1)} %get-tuple-element.208.refs_0_, bf16[4,272,512]{2,1,0:T(8,128)(2,1)} %copy-done.5, bf16[4,272,512]{2,1,0:T(8,128)(2,1)} %collective-permute-done.11.refs_2_, ...), custom_call_target="tpu_custom_call" | custom-call | flops 1342177280 | bytes 1048576 | tf_op jit(solution)/shard_map/pallas_call | solution.py:92
  478.0 15.2 %shard_map.215 = (bf16[128,1024]{1,0:T(8,128)(2,1)}, bf16[4,128,256]{2,1,0:T(8,128)(2,1)}, bf16[4,128,256]{2,1,0:T(8,128)(2,1)}) custom-call(bf16[128,2048]{1,0:T(8,128)(2,1)} %get-tuple-element.208.refs_0_, bf16[4,272,512]{2,1,0:T(8,128)(2,1)} %copy-done.5, bf16[4,272,512]{2,1,0:T(8,128)(2,1)} %collective-permute-done.11.refs_2_, ...), custom_call_target="tpu_custom_call" | custom-call | flops 1342177280 | bytes 1048576 | tf_op jit(solution)/shard_map/pallas_call | solution.py:92
  493.2 15.2 %shard_map.216 = (bf16[128,1024]{1,0:T(8,128)(2,1)}, bf16[4,128,256]{2,1,0:T(8,128)(2,1)}, bf16[4,128,256]{2,1,0:T(8,128)(2,1)}) custom-call(bf16[128,2048]{1,0:T(8,128)(2,1)} %get-tuple-element.220.refs_0_, bf16[4,272,512]{2,1,0:T(8,128)(2,1)} %copy-done.5, bf16[4,272,512]{2,1,0:T(8,128)(2,1)} %collective-permute-done.11.refs_2_, ...), custom_call_target="tpu_custom_call" | custom-call | flops 1342177280 | bytes 1048576 | tf_op jit(solution)/shard_map/pallas_call | solution.py:92
  521.6 15.2 %shard_map.217 = (bf16[128,1024]{1,0:T(8,128)(2,1)}, bf16[4,128,256]{2,1,0:T(8,128)(2,1)}, bf16[4,128,256]{2,1,0:T(8,128)(2,1)}) custom-call(bf16[128,2048]{1,0:T(8,128)(2,1)} %get-tuple-element.220.refs_0_, bf16[4,272,512]{2,1,0:T(8,128)(2,1)} %copy-done.5, bf16[4,272,512]{2,1,0:T(8,128)(2,1)} %collective-permute-done.11.refs_2_, ...), custom_call_target="tpu_custom_call" | custom-call | flops 1342177280 | bytes 1048576 | tf_op jit(solution)/shard_map/pallas_call | solution.py:92
  584.1 33.7 %collective-permute-done.57 = bf16[256,512]{1,0:T(8,128)(2,1)S(1)} collective-permute-done((bf16[256,512]{1,0:T(8,128)(2,1)S(1)}, bf16[256,512]{1,0:T(8,128)(2,1)S(1)}, u32[]{:S(2)}, u32[]{:S(2)}) %collective-permute-start.57) | collective-permute-done | bytes 262176 | tf_op jit(solution)/shard_map/ppermute | solution.py:731
  730.9 11.7 %collective-permute-done.71 = bf16[256,2048]{1,0:T(8,128)(2,1)S(1)} collective-permute-done((bf16[256,2048]{1,0:T(8,128)(2,1)S(1)}, bf16[256,2048]{1,0:T(8,128)(2,1)S(1)}, u32[]{:S(2)}, u32[]{:S(2)}) %collective-permute-start.71) | collective-permute-done | bytes 1048608 | tf_op jit(solution)/shard_map/ppermute | solution.py:731
  744.0 15.9 %collective-permute-done.70 = bf16[256,2816]{1,0:T(8,128)(2,1)S(1)} collective-permute-done((bf16[256,2816]{1,0:T(8,128)(2,1)S(1)}, bf16[256,2816]{1,0:T(8,128)(2,1)S(1)}, u32[]{:S(2)}, u32[]{:S(2)}) %collective-permute-start.70) | collective-permute-done | bytes 1441824 | tf_op jit(solution)/shard_map/ppermute | solution.py:731
  802.6 12.3 %collective-permute-start.86 = (bf16[256,640]{1,0:T(8,128)(2,1)S(1)}, bf16[256,640]{1,0:T(8,128)(2,1)S(1)}, u32[]{:S(2)}, u32[]{:S(2)}) collective-permute-start(bf16[256,640]{1,0:T(8,128)(2,1)S(1)} %add_convert_fusion.31), channel_id=1, source_target_pairs={{0,2},{1,3},{6,4},{7,5},{8,10},{9,11},{14,12},{15,13},{16,18},{17,... | collective-permute-start | bytes 983048 | tf_op jit(solution)/shard_map/ppermute | solution.py:731
  818.3 15.1 %shard_map.228 = (f32[512,5632]{1,0:T(8,128)}, f32[512,5632]{1,0:T(8,128)}) custom-call(s32[4]{0:T(128)} %pad_add_fusion.refs_0_, bf16[256,2816]{1,0:T(8,128)(2,1)} %get-tuple-element.267.refs_5_.refs_4_.refs_1_, bf16[256,2816]{1,0:T(8,128)(2,1)} %copy-done.37, bf16[256,2816]{1,0:T(8,128)(2,1)} %get-tuple-element.268.refs_5_.refs_3_, ...), custom_call_target="tpu_custom_call" | custom-call | bytes 34603008 | tf_op jit(solution)/shard_map/pallas_call | solution.py:92
  849.3 15.2 %collective-permute-done.91 = bf16[256,2048]{1,0:T(8,128)(2,1)} collective-permute-done((bf16[256,2048]{1,0:T(8,128)(2,1)S(1)}, bf16[256,2048]{1,0:T(8,128)(2,1)}, u32[]{:S(2)}, u32[]{:S(2)}) %collective-permute-start.91) | collective-permute-done | bytes 1048608 | tf_op jit(solution)/shard_map/ppermute | solution.py:731
  871.4 12.2 %collective-permute-done.97 = bf16[256,640]{1,0:T(8,128)(2,1)S(1)} collective-permute-done((bf16[256,640]{1,0:T(8,128)(2,1)S(1)}, bf16[256,640]{1,0:T(8,128)(2,1)S(1)}, u32[]{:S(2)}, u32[]{:S(2)}) %collective-permute-start.97) | collective-permute-done | bytes 327712 | tf_op jit(solution)/shard_map/ppermute | solution.py:731
  (504 shorter events, 502.8 us)
Async XLA Ops:
  11.8 46.5 %collective-permute-start.4 = (bf16[256,2048]{1,0:T(8,128)(2,1)}, bf16[256,2048]{1,0:T(8,128)(2,1)S(1)}, u32[]{:S(2)}, u32[]{:S(2)}) collective-permute-start(bf16[256,2048]{1,0:T(8,128)(2,1)} %constant_dynamic-slice_fusion.6), channel_id=1, source_target_pairs={{0,8},{8,0},{16,24},{24,16},{1,9},{9,1},{17,25},{25,17},{2,10},{10... | collective-permute-start | bytes 3145736 | tf_op jit(solution)/shard_map/ppermute | solution.py:725
  13.7 54.7 %collective-permute-start.5 = (bf16[256,2048]{1,0:T(8,128)(2,1)}, bf16[256,2048]{1,0:T(8,128)(2,1)S(1)}, u32[]{:S(2)}, u32[]{:S(2)}) collective-permute-start(bf16[256,2048]{1,0:T(8,128)(2,1)} %constant_dynamic-slice_fusion.6), channel_id=1, source_target_pairs={{0,16},{8,24},{16,0},{24,8},{1,17},{9,25},{17,1},{25,9},{2,18},{10... | collective-permute-start | bytes 3145736 | tf_op jit(solution)/shard_map/ppermute | solution.py:725
  28.0 40.4 %collective-permute-start.6 = (bf16[256,2048]{1,0:T(8,128)(2,1)}, bf16[256,2048]{1,0:T(8,128)(2,1)}, u32[]{:S(2)}, u32[]{:S(2)}) collective-permute-start(bf16[256,2048]{1,0:T(8,128)(2,1)} %constant_dynamic-slice_fusion.6), channel_id=1, source_target_pairs={{0,24},{8,16},{16,8},{24,0},{1,25},{9,17},{17,9},{25,1},{2,26},{10... | collective-permute-start | bytes 3145736 | tf_op jit(solution)/shard_map/ppermute | solution.py:725
  183.7 71.8 %collective-permute-start.31 = (bf16[768,2816]{1,0:T(8,128)(2,1)}, bf16[768,2816]{1,0:T(8,128)(2,1)}, u32[]{:S(2)}, u32[]{:S(2)}) collective-permute-start(bf16[768,2816]{1,0:T(8,128)(2,1)} %constant_dynamic-update-slice_fusion.9), channel_id=1, source_target_pairs={{0,1},{1,0},{2,3},{3,2},{4,5},{5,4},{6,7},{7,6},{8,9},{9,8},{10,11... | collective-permute-start | bytes 12976136 | tf_op jit(solution)/shard_map/ppermute | solution.py:728
  311.7 38.6 %collective-permute-start.33 = (bf16[704,1024]{1,0:T(8,128)(2,1)}, bf16[704,1024]{1,0:T(8,128)(2,1)}, u32[]{:S(2)}, u32[]{:S(2)}) collective-permute-start(bf16[704,1024]{1,0:T(8,128)(2,1)} %get-tuple-element.352.refs_9_), channel_id=1, source_target_pairs={{0,2},{1,3},{6,4},{7,5},{8,10},{9,11},{14,12},{15,13},{16,18},{17,... | collective-permute-start | bytes 4325384 | tf_op jit(solution)/shard_map/ppermute | solution.py:731
  353.8 42.8 %collective-permute-start.38 = (bf16[1024,2816]{1,0:T(8,128)(2,1)}, bf16[1024,2816]{1,0:T(8,128)(2,1)}, u32[]{:S(2)}, u32[]{:S(2)}) collective-permute-start(bf16[1024,2816]{1,0:T(8,128)(2,1)} %shard_map.210.refs_2_), channel_id=1, source_target_pairs={{0,1},{1,0},{2,3},{3,2},{4,5},{5,4},{6,7},{7,6},{8,9},{9,8},{10,11... | collective-permute-start | bytes 17301512 | tf_op jit(solution)/shard_map/ppermute | solution.py:728
  360.9 48.1 %collective-permute-start.40 = (bf16[256,2048]{1,0:T(8,128)(2,1)}, bf16[256,2048]{1,0:T(8,128)(2,1)}, u32[]{:S(2)}, u32[]{:S(2)}) collective-permute-start(bf16[256,2048]{1,0:T(8,128)(2,1)} %pad_maximum_fusion.4), channel_id=1, source_target_pairs={{0,16},{8,24},{16,0},{24,8},{1,17},{9,25},{17,1},{25,9},{2,18},{10... | collective-permute-start | bytes 3145736 | tf_op jit(solution)/shard_map/ppermute | solution.py:725
  365.6 43.4 %collective-permute-start.39 = (bf16[256,2048]{1,0:T(8,128)(2,1)}, bf16[256,2048]{1,0:T(8,128)(2,1)}, u32[]{:S(2)}, u32[]{:S(2)}) collective-permute-start(bf16[256,2048]{1,0:T(8,128)(2,1)} %pad_maximum_fusion.3), channel_id=1, source_target_pairs={{0,8},{8,0},{16,24},{24,16},{1,9},{9,1},{17,25},{25,17},{2,10},{10... | collective-permute-start | bytes 3145736 | tf_op jit(solution)/shard_map/ppermute | solution.py:725
  414.4 41.9 %collective-permute-start.42 = (bf16[704,1024]{1,0:T(8,128)(2,1)}, bf16[704,1024]{1,0:T(8,128)(2,1)}, u32[]{:S(2)}, u32[]{:S(2)}) collective-permute-start(bf16[704,1024]{1,0:T(8,128)(2,1)} %add_convert_fusion.10.refs_8_.refs_9_), channel_id=1, source_target_pairs={{2,4},{3,5},{4,2},{5,3},{10,12},{11,13},{12,10},{13,11},{18,20},{1... | collective-permute-start | bytes 4325384 | tf_op jit(solution)/shard_map/ppermute | solution.py:731
  416.2 43.6 %collective-permute-start.41 = (bf16[704,1024]{1,0:T(8,128)(2,1)}, bf16[704,1024]{1,0:T(8,128)(2,1)}, u32[]{:S(2)}, u32[]{:S(2)}) collective-permute-start(bf16[704,1024]{1,0:T(8,128)(2,1)} %add_convert_fusion.11.refs_7_.refs_8_), channel_id=1, source_target_pairs={{2,0},{3,1},{4,6},{5,7},{10,8},{11,9},{12,14},{13,15},{18,16},{19,... | collective-permute-start | bytes 4325384 | tf_op jit(solution)/shard_map/ppermute | solution.py:731
  420.2 42.3 %collective-permute-start.43 = (bf16[256,2816]{1,0:T(8,128)(2,1)}, bf16[256,2816]{1,0:T(8,128)(2,1)}, u32[]{:S(2)}, u32[]{:S(2)}) collective-permute-start(bf16[256,2816]{1,0:T(8,128)(2,1)} %get-tuple-element.326), channel_id=1, source_target_pairs={{0,2},{1,3},{6,4},{7,5},{8,10},{9,11},{14,12},{15,13},{16,18},{17,... | collective-permute-start | bytes 4325384 | tf_op jit(solution)/shard_map/ppermute | solution.py:731
  427.2 38.5 %collective-permute-start.44 = (bf16[256,2816]{1,0:T(8,128)(2,1)}, bf16[256,2816]{1,0:T(8,128)(2,1)}, u32[]{:S(2)}, u32[]{:S(2)}) collective-permute-start(bf16[256,2816]{1,0:T(8,128)(2,1)} %get-tuple-element.325), channel_id=1, source_target_pairs={{0,8},{8,0},{16,24},{24,16},{1,9},{9,1},{17,25},{25,17},{2,10},{10... | collective-permute-start | bytes 4325384 | tf_op jit(solution)/shard_map/ppermute | solution.py:725
  427.8 37.9 %collective-permute-start.45 = (bf16[256,2816]{1,0:T(8,128)(2,1)}, bf16[256,2816]{1,0:T(8,128)(2,1)}, u32[]{:S(2)}, u32[]{:S(2)}) collective-permute-start(bf16[256,2816]{1,0:T(8,128)(2,1)} %get-tuple-element.324), channel_id=1, source_target_pairs={{0,16},{8,24},{16,0},{24,8},{1,17},{9,25},{17,1},{25,9},{2,18},{10... | collective-permute-start | bytes 4325384 | tf_op jit(solution)/shard_map/ppermute | solution.py:725
  465.7 42.7 %collective-permute-start.46 = (bf16[704,1024]{1,0:T(8,128)(2,1)}, bf16[704,1024]{1,0:T(8,128)(2,1)}, u32[]{:S(2)}, u32[]{:S(2)}) collective-permute-start(bf16[704,1024]{1,0:T(8,128)(2,1)} %add_convert_fusion.9.refs_9_), channel_id=1, source_target_pairs={{2,0},{3,1},{4,6},{5,7},{10,8},{11,9},{12,14},{13,15},{18,16},{19,... | collective-permute-start | bytes 4325384 | tf_op jit(solution)/shard_map/ppermute | solution.py:731
  467.0 44.0 %collective-permute-start.48 = (bf16[256,2816]{1,0:T(8,128)(2,1)}, bf16[256,2816]{1,0:T(8,128)(2,1)}, u32[]{:S(2)}, u32[]{:S(2)}) collective-permute-start(bf16[256,2816]{1,0:T(8,128)(2,1)} %collective-permute-done.44.refs_11_), channel_id=1, source_target_pairs={{0,2},{1,3},{6,4},{7,5},{8,10},{9,11},{14,12},{15,13},{16,18},{17,... | collective-permute-start | bytes 4325384 | tf_op jit(solution)/shard_map/ppermute | solution.py:731
  473.9 40.4 %collective-permute-start.47 = (bf16[256,2816]{1,0:T(8,128)(2,1)}, bf16[256,2816]{1,0:T(8,128)(2,1)}, u32[]{:S(2)}, u32[]{:S(2)}) collective-permute-start(bf16[256,2816]{1,0:T(8,128)(2,1)} %add_convert_fusion.8.refs_10_), channel_id=1, source_target_pairs={{2,4},{3,5},{4,2},{5,3},{10,12},{11,13},{12,10},{13,11},{18,20},{1... | collective-permute-start | bytes 4325384 | tf_op jit(solution)/shard_map/ppermute | solution.py:731
  476.1 40.4 %collective-permute-start.49 = (bf16[256,2816]{1,0:T(8,128)(2,1)}, bf16[256,2816]{1,0:T(8,128)(2,1)}, u32[]{:S(2)}, u32[]{:S(2)}) collective-permute-start(bf16[256,2816]{1,0:T(8,128)(2,1)} %get-tuple-element.323), channel_id=1, source_target_pairs={{0,24},{8,16},{16,8},{24,0},{1,25},{9,17},{17,9},{25,1},{2,26},{10... | collective-permute-start | bytes 4325384 | tf_op jit(solution)/shard_map/ppermute | solution.py:725
  521.1 38.1 %collective-permute-start.52 = (bf16[704,1024]{1,0:T(8,128)(2,1)}, bf16[704,1024]{1,0:T(8,128)(2,1)}, u32[]{:S(2)}, u32[]{:S(2)}) collective-permute-start(bf16[704,1024]{1,0:T(8,128)(2,1)} %broadcast_select_fusion.3.refs_8_.refs_1_), channel_id=1, source_target_pairs={{0,1},{1,0},{2,3},{3,2},{4,5},{5,4},{6,7},{7,6},{8,9},{9,8},{10,11... | collective-permute-start | bytes 4325384 | tf_op jit(solution)/shard_map/ppermute | solution.py:728
  521.1 38.1 %collective-permute-start.53 = (bf16[704,1024]{1,0:T(8,128)(2,1)}, bf16[704,1024]{1,0:T(8,128)(2,1)}, u32[]{:S(2)}, u32[]{:S(2)}) collective-permute-start(bf16[704,1024]{1,0:T(8,128)(2,1)} %broadcast_select_fusion.2.refs_3_), channel_id=1, source_target_pairs={{0,1},{1,0},{2,3},{3,2},{4,5},{5,4},{6,7},{7,6},{8,9},{9,8},{10,11... | collective-permute-start | bytes 4325384 | tf_op jit(solution)/shard_map/ppermute | solution.py:728
  576.0 63.5 %collective-permute-start.61 = (bf16[1024,2048]{1,0:T(8,128)(2,1)}, bf16[1024,2048]{1,0:T(8,128)(2,1)}, u32[]{:S(2)}, u32[]{:S(2)}) collective-permute-start(bf16[1024,2048]{1,0:T(8,128)(2,1)} %shard_map.219), channel_id=1, source_target_pairs={{0,1},{1,0},{2,3},{3,2},{4,5},{5,4},{6,7},{7,6},{8,9},{9,8},{10,11... | collective-permute-start | bytes 12582920 | tf_op jit(solution)/shard_map/ppermute | solution.py:728
  577.9 43.7 %collective-permute-start.54 = (bf16[256,2816]{1,0:T(8,128)(2,1)S(1)}, bf16[256,2816]{1,0:T(8,128)(2,1)S(1)}, u32[]{:S(2)}, u32[]{:S(2)}) collective-permute-start(bf16[256,2816]{1,0:T(8,128)(2,1)S(1)} %broadcast_select_fusion.5), channel_id=1, source_target_pairs={{0,2},{1,3},{2,0},{3,1},{4,6},{5,7},{6,4},{7,5},{8,10},{9,11},{10,... | collective-permute-start | bytes 4325384 | tf_op jit(solution)/shard_map/ppermute | solution.py:731
  580.0 45.7 %collective-permute-start.55 = (bf16[256,2816]{1,0:T(8,128)(2,1)S(1)}, bf16[256,2816]{1,0:T(8,128)(2,1)S(1)}, u32[]{:S(2)}, u32[]{:S(2)}) collective-permute-start(bf16[256,2816]{1,0:T(8,128)(2,1)S(1)} %copy-done.12), channel_id=1, source_target_pairs={{2,4},{3,5},{4,2},{5,3},{10,12},{11,13},{12,10},{13,11},{18,20},{1... | collective-permute-start | bytes 4325384 | tf_op jit(solution)/shard_map/ppermute | solution.py:731
  581.5 36.3 %collective-permute-start.57 = (bf16[256,512]{1,0:T(8,128)(2,1)S(1)}, bf16[256,512]{1,0:T(8,128)(2,1)S(1)}, u32[]{:S(2)}, u32[]{:S(2)}) collective-permute-start(bf16[256,512]{1,0:T(8,128)(2,1)S(1)} %get-tuple-element.362), channel_id=1, source_target_pairs={{0,6},{1,7},{2,0},{3,1},{4,2},{5,3},{6,4},{7,5},{8,14},{9,15},{10,... | collective-permute-start | bytes 786440 | tf_op jit(solution)/shard_map/ppermute | solution.py:731
  653.1 35.6 %collective-permute-start.62 = (bf16[256,2816]{1,0:T(8,128)(2,1)}, bf16[256,2816]{1,0:T(8,128)(2,1)}, u32[]{:S(2)}, u32[]{:S(2)}) collective-permute-start(bf16[256,2816]{1,0:T(8,128)(2,1)} %add_convert_fusion.3.refs_6_), channel_id=1, source_target_pairs={{2,0},{3,1},{4,6},{5,7},{10,8},{11,9},{12,14},{13,15},{18,16},{19,... | collective-permute-start | bytes 4325384 | tf_op jit(solution)/shard_map/ppermute | solution.py:731
  (148 other events, 2155.0 us)

commit v3 on v2

--- a/solution.py
+++ b/solution.py
@@ -123,6 +123,9 @@
             side = lax.rem(where[3] + self.levels - step, self.levels) * 2 + side
         return pl.multiple_of(side * self.cell, self.cell)
 
+    def row(self, where, row, bit):
+        return row if row is not None else pl.multiple_of((where[0] ^ bit) * self.cell, self.cell)
+
     def moves(self, where, refs, bit, first, size):
         own, sources = refs[: len(self.own)], refs[len(self.own) :]
         step = self.width // len(self.own)
@@ -138,7 +141,10 @@
                 continue
             spot = self.spot(where, step_, flip)
             for number in range(len(own)):
-                place = sources[source].at[pl.ds(row, self.cell), pl.ds(number * step + first, size)]
+                row_ = self.row(where, row, bit)
+                place = sources[source].at[
+                    pl.ds(row_, self.cell), pl.ds(number * step + first, size)
+                ]
                 moves.append((place, spot, self.cell, number))
         return moves
 
@@ -156,7 +162,13 @@
             if flag == bit:
                 spot = self.spot(where, step_, flip)
                 moves.append(
-                    (sources[source].at[pl.ds(row, self.cell), :], spot, self.cell, 0, self.width)
+                    (
+                        sources[source].at[pl.ds(self.row(where, row, bit), self.cell), :],
+                        spot,
+                        self.cell,
+                        0,
+                        self.width,
+                    )
                 )
         return moves
 
@@ -357,24 +369,41 @@
     )
 
 
-def grad_body(more, where, left_ref, right_ref, *refs):
+def grad_body(parts, gots, outs, where, left_ref, right_ref, *refs):
     total = dot_rows(left_ref[...], right_ref[...])
-    if more:
-        total = total.astype(BF).astype(F32) + refs[0][...].astype(F32)
-    refs[-1][...] = total.astype(BF)
-
-
-def grad_mm(where, left, right, side, parts, got=None, after=()):
+    half = left_ref.shape[1]
+    for number in range(parts):
+
+        @pl.when(pl.program_id(0) == number)
+        def _(number=number):
+            value = total
+            if gots:
+                value = value.astype(BF).astype(F32)
+                value = value + refs[number * gots // parts][...].astype(F32)
+            per = parts // outs
+            out_ref = refs[gots + number // per]
+            row = number % per * half
+            out_ref[row : row + half, :] = value.astype(BF)
+
+
+def grad_mm(where, left, right, side, parts, got=(), after=(), outs=1):
     rows, depth = left.shape
     width = right.shape[1]
     half = depth // parts // 2
-    more = got is not None
+    gots = len(got)
     column = lambda b, w: (0, (w[0] ^ b) * 2 + (w[2] ^ side))
-    block = pl.BlockSpec((half, width), lambda b, w: (b, 0))
-    return call(
-        functools.partial(grad_body, more),
-        shape((parts * half, width), BF),
-        [where, left, right] + [got] * more,
+
+    def piece(number):
+        per = parts // gots
+        return pl.BlockSpec(
+            (half, width), lambda b, w: (jnp.clip(b - number * per, 0, per - 1), 0)
+        )
+
+    tall = parts // outs * half
+    made = call(
+        functools.partial(grad_body, parts, gots, outs),
+        [shape((tall, width), BF)] * outs,
+        [where, left, right, *got],
         flops=2 * rows * parts * half * width,
         nbytes=2 * (rows * parts * half + rows * width + parts * half * width),
         grid=(parts,),
@@ -382,57 +411,39 @@
             pl.BlockSpec((rows, half), column),
             pl.BlockSpec((rows, width), lambda b, w: (0, 0)),
         ]
-        + [block] * more,
-        out_specs=block,
+        + [piece(number) for number in range(gots)],
+        out_specs=[pl.BlockSpec((tall, width), lambda b, w: (0, 0))] * outs,
         after=after,
         prefetch=True,
     )
-
-
-def grad_columns(where, left, right, side, got=None, after=()):
-    rows, depth = left.shape
-    width = right.shape[1] // 2
-    steps = 2
-    more = got is not None
-    column = lambda n, w: (0, (w[2] ^ side) * steps + n)
-    block = pl.BlockSpec((depth, width // steps), lambda n, w: (0, n))
-    return call(
-        functools.partial(grad_body, more),
-        shape((depth, width), BF),
-        [where, left, right] + [got] * more,
-        flops=2 * rows * depth * width,
-        nbytes=2 * (rows * depth + rows * width + depth * width),
-        grid=(steps,),
-        in_specs=[
-            pl.BlockSpec((rows, depth), lambda n, w: (0, 0)),
-            pl.BlockSpec((rows, width // steps), column),
-        ]
-        + [block] * more,
-        out_specs=block,
-        after=after,
-        prefetch=True,
-    )
-
-
-def mix_body(left_ref, right_ref, out_ref):
-    out_ref[...] = dot(left_ref[...], right_ref[...]).astype(BF)
+    return made
+
+
+def mix_body(apart, left_ref, right_ref, *outs):
+    total = dot(left_ref[...], right_ref[...]).astype(BF)
+    for number in range(apart):
+
+        @pl.when(pl.program_id(0) == number)
+        def _(number=number):
+            outs[number][...] = total
 
 
 def mix(left, right, blocks, after=()):
     rows, depth = left.shape
     width = right.shape[1]
+    tall = rows // blocks
     return call(
-        mix_body,
-        shape((rows, width), BF),
+        functools.partial(mix_body, blocks),
+        [shape((tall, width), BF)] * blocks,
         [left, right],
         flops=2 * rows * depth * width,
         nbytes=2 * (rows * depth + depth * width + rows * width),
         grid=(blocks,),
         in_specs=[
-            pl.BlockSpec((rows // blocks, depth), lambda n: (n, 0)),
+            pl.BlockSpec((tall, depth), lambda n: (n, 0)),
             pl.BlockSpec((depth, width), lambda n: (0, 0)),
         ],
-        out_specs=pl.BlockSpec((rows // blocks, width), lambda n: (n, 0)),
+        out_specs=[pl.BlockSpec((tall, width), lambda n: (0, 0))] * blocks,
         after=after,
     )
 
@@ -758,6 +769,9 @@
                 bit += 1
         return Pieces(own, pieces + list(others), blocks, cell, width)
 
+    def swap_all(arrays):
+        return [swap_run(a, 1) for a in arrays]
+
     def hops(local):
         return [hop(local, bit) for bit in range(1, parts)]
 
@@ -867,6 +881,24 @@
         for climb, got in zip(climbs, results):
             climb.take(got)
 
+    def values(climbs):
+        return [c.value for c in climbs]
+
+    def sync(*groups):
+        flat = [a for group in groups for a in group]
+        flat = list(lax.optimization_barrier(tuple(flat)))
+        out = []
+        for group in groups:
+            out.append(flat[: len(group)])
+            flat = flat[len(group) :]
+        return out
+
+    def sync_climbs(climbs, *groups):
+        held, *rest = sync(values(climbs), *groups)
+        for climb, value in zip(climbs, held):
+            climb.value = value
+        return rest
+
     gains = jnp.stack([norm_gain, ffn_gain] + [jnp.zeros_like(norm_gain)] * (EXTRA - 2), 0)
     own_kv = jnp.concatenate([w_key, w_value], 1)
     wide = own_kv.shape[1] // shard
@@ -874,6 +906,7 @@
     sent_kv = jnp.concatenate([at(own_kv, core * half, half), tag_rows], 0)
     got_kv = [hop(sent_kv, bit) for bit in range(1, parts)]
     own_query = at(w_query, core * half, half)
+    got_kv[:1], (own_query,) = sync(got_kv[:1], [own_query])
     near_query = [hop(own_query, bit) for bit in range(1, min(3, parts))]
     got_kv = tie(got_kv)
     kv_pieces = [a[:half] for a in got_kv]
@@ -928,47 +961,49 @@
     query_w = halves([w_query], got_query, [other_query], w_query.shape[1])
     query_raw = forward_mm(where, normed_one, query_w, parts)
 
-    wide_hops = tie(wide_hops, query_raw)
+    own_out, own_dm = at(w_out, core * half, half), cotangent.reshape(row_count, model_width)
+    (own_out,), got_query = sync([own_out], got_query)
+    all_out = lax.all_gather(own_out, "fsdp", axis=0, tiled=True)
+    forward = [list(attend(0, query_raw, kv, tag, cosine, sine, tok_count))]
+    wide_hops, forward[0], (own_dm,) = sync(wide_hops, forward[0], [own_dm])
     rings = [jnp.concatenate(wide_hops, 0)]
     moving = turn(rings[0])
-    near_out = near_of(at(tie(w_out, *wide_hops), core * half, half))
-    forward = [
-        attend(0, query_raw, kv, tag, cosine, sine, tok_count, after=[rings[0]])
-    ]
-    moving, *near_out = tie([moving, *near_out], forward[0][1])
-    rings.append(moving)
-    moving = turn(rings[1])
-    far_out = far_of(near_out)
-    grad_y_low = cotangent.reshape(row_count, model_width)
-    near_dm = near_of(tie(grad_y_low, *near_out))
+    grad_y_low = own_dm
+    near_dm = near_of(own_dm)
     for seq in range(1, seq_count):
         forward.append(
-            attend(
-                seq, query_raw, kv, tag, cosine, sine, tok_count, after=[rings[-1], *near_out]
+            list(
+                attend(
+                    seq, query_raw, kv, tag, cosine, sine, tok_count,
+                    after=[rings[0], forward[-1][1]],
+                )
             )
         )
     rot, attended, logs = [list(a) for a in zip(*forward)]
-    moving, *far_out = tie([moving, *far_out], attended[-1])
+    (moving,), (attended[-1],), (all_out,) = sync([moving], [attended[-1]], [all_out])
     rings.append(moving)
-    far_out = [jnp.concatenate(far_out, 0)] if parts == 4 else far_out
-    got_out = near_out + far_out
-    other_out = [swap_run(jnp.concatenate(got_out, 0), 1)]
-    while len(rings) < levels - 1:
-        rings.append(turn(rings[-1]))
     moving = turn(rings[-1])
-    out_w = halves([w_out], got_out, other_out, w_out.shape[1])
+    other_out = swap_run(all_out, 1)
+    blocks = [(0, None, 0, 0, bit) for bit in range(1, parts)]
+    blocks += [(1, None, 0, 1, bit) for bit in range(1, parts)]
+    out_w = Pieces([w_out], [all_out, other_out], blocks, half, w_out.shape[1])
     attended = jnp.concatenate(attended, 0)
     inputs = x_low.astype(F32)
     residual = inputs + forward_mm(where, attended, out_w, parts)
     scale_two = rms_scale(residual)
     normed_two = (residual * scale_two * gain_two).astype(BF)
+    (moving,), (normed_two,), near_dm = sync([moving], [normed_two], near_dm)
     near_normed = near_of(normed_two)
-    far_dm = far_of(tie(near_dm, residual))
+    far_dm = far_of(near_dm)
+    all_dm = [grad_y_low] + near_dm + far_dm
+    while len(rings) < levels - 1:
+        rings.append(moving)
+        moving = turn(rings[-1])
+    near_normed, (moving,) = sync(near_normed, [moving])
     far_normed = far_of(near_normed)
     rings.append(moving)
     other_wide = swap_run(jnp.concatenate(rings, 0), 1)
     all_normed = [normed_two] + near_normed + far_normed
-    all_dm = [grad_y_low] + near_dm + far_dm
     cell = shard // runs
     blocks = []
     for back in range(levels):
@@ -983,7 +1018,8 @@
         )
     else:
         laid = lay_rows(wide_w)
-        stacked, stacked_dm = jnp.concatenate(all_normed, 0), jnp.concatenate(all_dm, 0)
+        stacked = jnp.concatenate(all_normed, 0)
+        stacked_dm = jnp.concatenate(all_dm, 0)
         gate_proj, up_proj = dot(stacked, laid[:, :ff_part]), dot(stacked, laid[:, ff_part:])
         sigmoid_gate = jax.nn.sigmoid(gate_proj)
         hidden_low = (gate_proj * sigmoid_gate * up_proj).astype(BF)
@@ -1004,9 +1040,6 @@
             both = both[count:]
         return [*out, both]
 
-    def values(climbs):
-        return [c.value for c in climbs]
-
     down_rows = ff_part // 2
     middle = model_width // 2
 
@@ -1018,12 +1051,12 @@
 
     def put(steps, outs):
         pieces, plan = [], []
-        for piece, column, cols, target, spot in steps:
+        for piece, column, cols, target, spot, *span in steps:
             if not any(piece is p for p in pieces):
                 pieces.append(piece)
             index = [piece is p for p in pieces].index(True)
-            rows = piece.shape[0]
-            plan.append((index, 0, column, rows, cols, target, spot))
+            first, rows = span or (0, piece.shape[0])
+            plan.append((index, first, column, rows, cols, target, spot))
         return place(where, pieces, plan, outs)
 
     full = (shard, parts * ff_part)
@@ -1072,63 +1105,9 @@
                 steps.append((down_done[number][side], 0, middle, 0, spot))
         return put(steps, [(ff_part, model_width)])[0]
 
-    def sync(*groups):
-        flat = [a for group in groups for a in group]
-        flat = list(lax.optimization_barrier(tuple(flat)))
-        out = []
-        for group in groups:
-            out.append(flat[: len(group)])
-            flat = flat[len(group) :]
-        return out
-
-    def sync_climbs(climbs, *groups):
-        held, *rest = sync(values(climbs), *groups)
-        for climb, value in zip(climbs, held):
-            climb.value = value
-        return rest
-
-    down_sent = dot_rows(hidden_low, at(stacked_dm, (1 - core) * middle, middle, 1)).astype(BF)
-    (down_sent,), (hidden_low,) = sync([down_sent], [hidden_low])
-    down_got = swap_run(down_sent, 1)
-    down_kept = dot_rows(hidden_low, at(stacked_dm, core * middle, middle, 1)).astype(BF)
-    down_pair = add(down_kept, down_got)
-    down = [Climb(down_pair[i * down_rows : (i + 1) * down_rows]) for i in range(2)]
-
-    moving = advance(down[:1])
-    if aligned:
-        back_blocks = back_mm(
-            where, grad_wide_in, wide_w, parts, BF, parts, after=values(down)
-        )
-    else:
-        back_rows = dot_cols(grad_wide_in, laid).astype(BF)
-        back_blocks = [back_rows[i * row_count : (i + 1) * row_count] for i in range(parts)]
-    back_got = sum_first(back_blocks)
-    wide_sent = grad_mm(where, stacked, grad_wide_in, 1, parts, after=back_blocks[:1])
-    take(down[:1], moving)
-    (wide_sent,), back_got = sync_climbs(down, [wide_sent], back_got)
-
-    moving = advance(down)
-    wide_got = swap_run(wide_sent, 1)
-    back_got = sum_second(back_blocks, back_got)
-    mixed = mix(hidden_low, w_down, parts, after=[wide_sent, *values(down)])
-    wide_pair = grad_mm(
-        where, stacked, grad_wide_in, 0, parts, got=wide_got, after=[mixed]
-    )
-    take(down, moving)
-    (wide_pair,), back_got, (mixed,) = sync_climbs(down, [wide_pair], back_got, [mixed])
-    wide_blocks = blocks_of(wide_pair)
-    mixed_blocks = [mixed[i * row_count : (i + 1) * row_count] for i in range(parts)]
-
-    climbs = [Climb(wide_blocks[0])]
-    moving = advance(down + climbs)
-    near_wide = [hop(a, bit + 1) for bit, a in enumerate(wide_blocks[1:3])]
-    grad_normed_two = sum_last(back_blocks, back_got)
-    grad_y = grad_y_low.astype(F32)
-    grad_res_norm, grad_gain_two = norm_back(grad_normed_two, residual, scale_two, gain_two)
-    grad_residual = grad_y + grad_res_norm
-    grad_proj = grad_residual.astype(BF)
-    (grad_attended,) = back_mm(where, grad_proj, out_w, parts, BF, after=values(down))
-    backward = []
+    def sum_apart(arrays, flip):
+        groups = [[2 * l + (k ^ flip) for l in range(levels)] for k in range(2)]
+        return list(lax.psum(tuple(arrays), "ctx", axis_index_groups=groups))
 
     def pull(seq, number, after=()):
         heads = range(number * KVH // 2, (number + 1) * KVH // 2)
@@ -1145,26 +1124,54 @@
         backward[-1] = pulled
         return rest
 
-    pull(0, 0, values(down))
-    take(down + climbs, moving)
-    (near_wide,) = sync_pulled(down + climbs, near_wide)
-
-    climbs += [Climb(a) for a in near_wide]
-    moving = advance(down[1:] + climbs[:2])
-    rest_wide = [hop(wide_blocks[b], b) for b in range(3, parts)]
-    pull(0, 1, values(down + climbs))
-    pull(1, 0)
-    take(down[1:] + climbs[:2], moving)
-    (rest_wide,) = sync_pulled(down + climbs, rest_wide)
-
-    climbs += [Climb(a) for a in rest_wide]
-    moving = advance(climbs[1:2])
-    merged = both_ways(climbs[2], climbs[0])
-    swap_down = [swap_run(complete(c).value, 1) for c in down]
-    pull(1, 1, values(climbs))
-    for seq in range(2, seq_count):
+    down_sent = dot_rows(hidden_low, at(stacked_dm, (1 - core) * middle, middle, 1)).astype(BF)
+    (down_sent,), (hidden_low,) = sync([down_sent], [hidden_low])
+    down_got = swap_run(down_sent, 1)
+    down_kept = dot_rows(hidden_low, at(stacked_dm, core * middle, middle, 1)).astype(BF)
+    down_pair = add(down_kept, down_got)
+    down = [Climb(down_pair[i * down_rows : (i + 1) * down_rows]) for i in range(2)]
+    moving = advance(down[:1])
+
+    if aligned:
+        back_blocks = back_mm(where, grad_wide_in, wide_w, parts, BF, parts, after=values(down))
+    else:
+        back_rows = dot_cols(grad_wide_in, laid).astype(BF)
+        back_blocks = [back_rows[i * row_count : (i + 1) * row_count] for i in range(parts)]
+    back_got = sum_first(back_blocks)
+    wide_sent = grad_mm(
+        where, stacked, grad_wide_in, 1, parts, after=back_blocks[:1]
+    )
+    wide_sent, back_got, moving = sync(wide_sent, back_got, moving)
+    take(down[:1], moving)
+
+    moving = advance(down)
+    wide_got = swap_all(wide_sent)
+    back_got = sum_second(back_blocks, back_got)
+    wide_blocks = grad_mm(
+        where, stacked, grad_wide_in, 0, parts, got=wide_got, after=values(down), outs=parts
+    )
+    back_got, wide_blocks, moving = sync(back_got, wide_blocks, moving)
+    take(down, moving)
+
+    moving = advance(down)
+    wide_moved = [hop(a, bit + 1) for bit, a in enumerate(wide_blocks[1:])]
+    grad_normed_two = sum_last(back_blocks, back_got)
+    grad_y = grad_y_low.astype(F32)
+    grad_res_norm, grad_gain_two = norm_back(grad_normed_two, residual, scale_two, gain_two)
+    grad_residual = grad_y + grad_res_norm
+    grad_proj = grad_residual.astype(BF)
+    (grad_attended,) = back_mm(where, grad_proj, out_w, parts, BF)
+    (grad_attended,), wide_moved[:1], moving = sync(
+        [grad_attended], wide_moved[:1], moving
+    )
+    take(down, moving)
+
+    wide_near = sum_apart(wide_blocks[:1] + wide_moved[:1], 1)
+    moving = advance(down[1:])
+    backward = []
+    for seq in range(seq_count):
         for number in range(2):
-            pull(seq, number)
+            pull(seq, number, values(down) if seq == 0 else ())
 
     def lay(index):
         rows = [
@@ -1178,56 +1185,63 @@
         rest = jnp.concatenate([jnp.concatenate([a[..., step:] for a in r], 2) for r in rows], 1)
         return jnp.concatenate([keys, rest], 2)
 
-    out_sent = grad_mm(where, attended, grad_proj, 1, parts, after=[backward[-1][0]])
+    out_sent = grad_mm(
+        where, attended, grad_proj, 1, parts, after=[backward[-1][0]], outs=2
+    )
     grad_query_low = lay(0)
-    query_sent = grad_mm(where, normed_one, grad_query_low, 1, parts, after=[out_sent])
-    take(climbs[1:2], moving)
-    take_both(climbs[2], climbs[0], merged)
-    (out_sent, query_sent), swap_down = sync_pulled(
-        climbs, [out_sent, query_sent], swap_down
-    )
-
-    moving = advance(climbs[2:3])
-    merged = both_ways(climbs[3], climbs[1])
+    query_sent = grad_mm(
+        where, normed_one, grad_query_low, 1, parts, after=out_sent[:1], outs=2
+    )
+    (grad_normed_one,) = back_mm(
+        where, grad_query_low, query_w, parts, F32, after=query_sent[:1]
+    )
+    mixed_blocks = mix(hidden_low, w_down, parts, after=[grad_normed_one])
+    (
+        out_sent, query_sent, wide_near, wide_moved[1:], (grad_normed_one,), moving, mixed_blocks
+    ) = sync_pulled(
+        [], out_sent, query_sent, wide_near, wide_moved[1:], [grad_normed_one], moving,
+        mixed_blocks,
+    )
+    take(down[1:], moving)
+
+    wide_far = sum_apart(wide_moved[1:], 0)
     other_dkv = swap_run(lay(2), 1)
-    out_got = swap_run(out_sent, 1)
+    out_got = swap_all(out_sent)
     by_level = add(lay(1), other_dkv)
-    ring_kv = by_level[levels - 1]
-    for step in reversed(range(1, levels)):
-        ring_kv = level_send(ring_kv, [(i, (i - 1) % levels) for i in range(levels)])
-        if step > 1:
-            ring_kv = add(ring_kv, by_level[step - 1])
-    out_pair = grad_mm(
-        where, attended, grad_proj, 0, parts, got=out_got, after=[by_level, *values(climbs)]
-    )
-    (out_pair,), (query_sent,) = sync([out_pair], [query_sent])
-    query_got = swap_run(query_sent, 1)
-    (grad_normed_one,) = back_mm(where, grad_query_low, query_w, parts, F32, after=[out_pair])
-    query_pair = grad_mm(
-        where, normed_one, grad_query_low, 0, parts, got=query_got, after=[grad_normed_one]
-    )
-    take(climbs[2:3], moving)
-    take_both(climbs[3], climbs[1], merged)
-    (ring_kv,), (out_pair, query_pair) = sync_climbs(climbs, [ring_kv], [out_pair, query_pair])
-    out_blocks, query_blocks = blocks_of(out_pair), blocks_of(query_pair)
-
-    moving = advance(climbs[2:])
-    out_got = sum_first(out_blocks)
+    kv_parts = []
+    for step in range(1, levels):
+        pairs = [(i, (i - step) % levels) for i in range(levels)]
+        kv_parts.append(level_send(by_level[step], pairs))
+    out_blocks = grad_mm(
+        where, attended, grad_proj, 0, parts, got=out_got, after=[by_level], outs=parts
+    )
+    out_mid = sum_first(out_blocks)
+    out_mid, kv_parts, query_sent = sync(out_mid, kv_parts, query_sent)
+
+    query_got = swap_all(query_sent)
+    out_end = sum_second(out_blocks, out_mid)
     grad_kv_low = call(
         kv_back_body,
         shape((row_count, 2 * KW), BF),
-        [by_level[0], ring_kv, cosine, sine],
+        [by_level[0], *kv_parts, cosine, sine],
         nbytes=row_count * KW * 4 * (levels + 1),
-        after=values(climbs),
-    )
-    kv_sent = grad_mm(where, normed_one, grad_kv_low, 1, parts)
-    out_got, (kv_sent,) = sync(out_got, [kv_sent])
-    out_got = sum_second(out_blocks, out_got)
+        after=out_blocks[:1],
+    )
+    (kv_sent,) = grad_mm(where, normed_one, grad_kv_low, 1, parts)
+    query_blocks = grad_mm(
+        where, normed_one, grad_query_low, 0, parts, got=query_got, after=[kv_sent], outs=parts
+    )
+    out_end, (kv_sent,), query_blocks = sync(out_end, [kv_sent], query_blocks)
+
+    out_sum = sum_last(out_blocks, out_end).astype(BF)
+    query_mid = sum_first(query_blocks)
     kv_got = swap_run(kv_sent, 1)
     (grad_normed_kv,) = back_mm(where, grad_kv_low, key_value_w, parts, F32, after=[kv_sent])
-    kv_pair = grad_mm(
-        where, normed_one, grad_kv_low, 0, parts, got=kv_got, after=[grad_normed_kv]
-    )
+    (kv_pair,) = grad_mm(
+        where, normed_one, grad_kv_low, 0, parts, got=[kv_got], after=[grad_normed_kv]
+    )
+    query_mid, (kv_pair,) = sync(query_mid, [kv_pair])
+    query_end = sum_second(query_blocks, query_mid)
     grad_normed_one = grad_normed_one + grad_normed_kv
     scale_one = rms_scale(inputs)
     grad_in_norm, grad_gain_one = norm_back(grad_normed_one, inputs, scale_one, gain_one)
@@ -1243,51 +1257,30 @@
     gain_cols = add(gain_kept, swap_run(gain_sent, 1)).T
     gain_cols = jnp.concatenate([gain_cols, jnp.zeros((parts * half, 126), BF)], 1)
     kv_blocks = blocks_of(jnp.concatenate([kv_pair, gain_cols], 1))
-    take(climbs[2:], moving)
-    out_got, kv_blocks, (grad_in,) = sync_climbs(climbs, out_got, kv_blocks, [grad_in])
-
-    out_climb = Climb(sum_last(out_blocks, out_got).astype(BF))
-    moving = advance([climbs[3], out_climb])
-    query_mid = sum_first(query_blocks)
-    swap_wide = [swap_run(complete(c).value, 1) for c in climbs[:2]]
-    query_mid, swap_wide = sync(query_mid, swap_wide)
-    query_end = sum_second(query_blocks, query_mid)
+    query_end, kv_blocks, (grad_in,) = sync(query_end, kv_blocks, [grad_in])
+
+    query_sum = sum_last(query_blocks, query_end).astype(BF)
     kv_mid = sum_first(kv_blocks)
-    take([climbs[3], out_climb], moving)
-    query_end, kv_mid = sync_climbs([climbs[3], out_climb], query_end, kv_mid)
-
-    query_climb = Climb(sum_last(query_blocks, query_end).astype(BF))
-    moving = advance([out_climb, query_climb])
+    mixed_mid = sum_first(mixed_blocks)
+    down_got = swap_all([complete(c).value for c in down])
+    kv_mid, (query_sum,), down_got, mixed_mid = sync(kv_mid, [query_sum], down_got, mixed_mid)
+    down_done = [[c.value, a] for c, a in zip(down, down_got)]
     kv_end = sum_second(kv_blocks, kv_mid)
-    swap_wide += [swap_run(complete(c).value, 1) for c in climbs[2:]]
-    down_done = [[c.value, s] for c, s in zip(down, swap_down)]
     grad_down = place_down(down_done)
-    take([out_climb, query_climb], moving)
-    kv_end, swap_wide, (grad_down,) = sync_climbs(
-        [out_climb, query_climb], kv_end, swap_wide, [grad_down]
-    )
-
-    kv_climb = Climb(sum_last(kv_blocks, kv_end).astype(BF))
-    moving = advance([kv_climb, out_climb, query_climb])
-    mixed_mid = sum_first(mixed_blocks)
-    wide_done = [[c.value, s] for c, s in zip(climbs, swap_wide)]
+    kv_end, (grad_down,) = sync(kv_end, [grad_down])
+    kv_sum = sum_last(kv_blocks, kv_end).astype(BF)
+
+    wide_far, last, mixed_mid = sync(wide_far, [out_sum, query_sum, kv_sum], mixed_mid)
+    last = sum_apart(last, 1)
+    wide_done = [[a, swap_run(a, 1)] for a in wide_near + wide_far]
+    mixed_end = sum_second(mixed_blocks, mixed_mid)
     grad_gate_w, grad_up_w = place_wide(wide_done)
-    take([kv_climb, out_climb, query_climb], moving)
-    mixed_mid, (grad_gate_w, grad_up_w) = sync_climbs(
-        [kv_climb, out_climb, query_climb], mixed_mid, [grad_gate_w, grad_up_w]
-    )
-
-    moving = advance([query_climb, kv_climb])
-    mixed_end = sum_second(mixed_blocks, mixed_mid)
-    out_done = [complete(out_climb).value, swap_run(out_climb.value, 1)]
+    mixed_end, (grad_gate_w, grad_up_w) = sync(mixed_end, [grad_gate_w, grad_up_w])
+    output = (residual + sum_last(mixed_blocks, mixed_end)).astype(BF)
+    output = output.reshape(seq_count, tok_count, model_width)
+    last, (output,) = sync(last, [output])
+    out_done, query_done, kv_done = [[a, swap_run(a, 1)] for a in last]
     (grad_out_w,) = put(both_rows(out_done, 0, model_width, 0), [(shard, model_width)])
-    take([query_climb, kv_climb], moving)
-    mixed_end, (grad_out_w,) = sync_climbs([query_climb, kv_climb], mixed_end, [grad_out_w])
-    mixed_sum = sum_last(mixed_blocks, mixed_end)
-    output = (residual + mixed_sum).astype(BF).reshape(seq_count, tok_count, model_width)
-    query_done, kv_done = [
-        [c.value, swap_run(c.value, 1)] for c in [complete(c) for c in (query_climb, kv_climb)]
-    ]
     grad_query_w, grad_key_w, grad_value_w, gain_out = put(
         both_rows(query_done, 0, model_width, 0)
         + both_rows(kv_done, 0, KW, 1)

time: 908 us -> 872 us (0.960)
  starting transfers between devices: 138 us -> 68.8 us
  other arithmetic: 119 us -> 76.6 us
  waiting for transfers between devices: 259 us -> 301 us
  Pallas kernels: 309 us -> 322 us
  between operations: 2.75 us -> 15.2 us
  local copies, waits for them, and re-layouts: 56 us -> 65.4 us
    psum x0 -> x3, waiting for transfers between devices: none -> 103 us  [sum_apart(): return list(lax.psum(tuple(arrays), 'ctx', axis_index_groups=groups))]
    ppermute x34 -> x15, waiting for transfers between devices: 150 us -> 58 us  [level_send(): lax.ppermute(array, 'ctx', [(2 * a + k, 2 * b + k) for a, b in pairs for...]
    ppermute x34 -> x15, starting transfers between devices: 83.4 us -> 18.7 us  [level_send(): lax.ppermute(array, 'ctx', [(2 * a + k, 2 * b + k) for a, b in pairs for...]
    ppermute x44 -> x40, waiting for transfers between devices: 95.3 us -> 121 us  [hop(): return lax.ppermute(array, 'fsdp', [(i, i ^ bit) for i in range(parts)])]
    convert_element_type x27 -> x16, other arithmetic: 49.1 us -> 23.2 us  [add(): return (a.astype(F32) + b.astype(F32)).astype(BF)]
    select_n x4 -> x0, other arithmetic: 13.7 us -> none  [the longest x2 9.38 us: take_both(): new.value = jnp.where(inner, add(new.value, got[0]), new.value)]
    pallas_call x8, Pallas kernels: 58.3 us -> 68.6 us  [call(): pl.pallas_call(run, out_shape=outs, grid_spec=pltpu.PrefetchScalarGridSpe...]
    ppermute x44 -> x40, starting transfers between devices: 51.5 us -> 46.5 us  [hop(): return lax.ppermute(array, 'fsdp', [(i, i ^ bit) for i in range(parts)])]
  transfers between devices with their start and end apart: 99 -> 82, of which waited for: 33 -> 39; matrix products, arithmetic and copies ran while one was open for 16% -> 14% of each run, Pallas kernels for 29% -> 32%
where the time goes in v3:
time: 872 us; the launch traced here: 862 us
  Pallas kernels  322 us (37%)
  waiting for transfers between devices  301 us (35%)
  other arithmetic  76.6 us (9%)
  starting transfers between devices  68.8 us (8%)
  local copies, waits for them, and re-layouts  65.4 us (8%)
  between operations  15.2 us (2%)
  matrix products  13.7 us (2%)
    pallas_call x20, Pallas kernels, call(): pl.pallas_call(run, out_shape=outs, in_specs=in_specs, out_specs=out_spec...  253 us
    ppermute x40, waiting for transfers between devices, hop(): return lax.ppermute(array, 'fsdp', [(i, i ^ bit) for i in range(parts)])  121 us
    psum x3, waiting for transfers between devices, sum_apart(): return list(lax.psum(tuple(arrays), 'ctx', axis_index_groups=groups))  103 us
    pallas_call x8, Pallas kernels, call(): pl.pallas_call(run, out_shape=outs, grid_spec=pltpu.PrefetchScalarGridSpe...  68.6 us
    ppermute x15, waiting for transfers between devices, level_send(): lax.ppermute(array, 'ctx', [(2 * a + k, 2 * b + k) for a, b in pairs for...  58 us
    ppermute x40, starting transfers between devices, hop(): return lax.ppermute(array, 'fsdp', [(i, i ^ bit) for i in range(parts)])  46.5 us
    convert_element_type x16, other arithmetic, add(): return (a.astype(F32) + b.astype(F32)).astype(BF)  23.2 us
    ppermute x15, starting transfers between devices, level_send(): lax.ppermute(array, 'ctx', [(2 * a + k, 2 * b + k) for a, b in pairs for...  18.7 us
  transfers between devices with their start and end apart: 82, of which 39 were waited for; matrix products, arithmetic and copies ran while one was open for 14% of the time, Pallas kernels for 32%

profile of v3, /device:TPU:0, one launch (start us, length us, event | category | flops | bytes accessed | tf_op | source)
XLA Modules:
  0.0 862.2 jit_solution(5028935366307884267)
XLA Ops:
  47.0 8.7 %collective-permute-done.7 = bf16[272,512]{1,0:T(8,128)(2,1)S(1)} collective-permute-done((bf16[272,512]{1,0:T(8,128)(2,1)}, bf16[272,512]{1,0:T(8,128)(2,1)S(1)}, u32[]{:S(2)}, u32[]{:S(2)}) %collective-permute-start.7) | collective-permute-done | bytes 278560 | tf_op jit(solution)/shard_map/ppermute | solution.py:742
  55.7 9.2 %collective-permute-done.8 = bf16[272,512]{1,0:T(8,128)(2,1)S(1)} collective-permute-done((bf16[272,512]{1,0:T(8,128)(2,1)S(1)}, bf16[272,512]{1,0:T(8,128)(2,1)S(1)}, u32[]{:S(2)}, u32[]{:S(2)}) %collective-permute-start.8) | collective-permute-done | bytes 278560 | tf_op jit(solution)/shard_map/ppermute | solution.py:742
  64.9 16.8 %collective-permute-done.5.refs_4_ = bf16[256,2048]{1,0:T(8,128)(2,1)S(1)} collective-permute-done((bf16[256,2048]{1,0:T(8,128)(2,1)}, bf16[256,2048]{1,0:T(8,128)(2,1)S(1)}, u32[]{:S(2)}, u32[]{:S(2)}) %collective-permute-start.5) | collective-permute-done | bytes 1048608 | tf_op jit(solution)/shard_map/ppermute | solution.py:736
  97.9 9.2 %shard_map.204.refs_0_ = f32[256,2048]{1,0:T(8,128)} custom-call(s32[4]{0:T(128)} %pad_add_fusion.refs_0_, bf16[256,2048]{1,0:T(8,128)(2,1)} %get-tuple-element.182.refs_1_, bf16[512,2048]{1,0:T(8,128)(2,1)} %refs_2_.9, bf16[256,2048]{1,0:T(8,128)(2,1)} %copy-done.9, bf16[256,2048]{1,0:T(8,128)(2,1)} %copy-done.10, bf16[256,2048]{1,0:T(8,128)(2,1)} %copy-done.11, ...), custom_call_target="tpu_custom_call" | custom-call | flops 2147483648 | bytes 11534336 | tf_op jit(solution)/shard_map/pallas_call | solution.py:92
  107.1 22.5 %shard_map.205 = (bf16[128,2048]{1,0:T(8,128)(2,1)}, bf16[128,2048]{1,0:T(8,128)(2,1)}, f32[1,32,128]{2,1,0:T(8,128)}) custom-call(f32[256,2048]{1,0:T(8,128)} %shard_map.204.refs_0_, bf16[4,272,512]{2,1,0:T(8,128)(2,1)} %pad_maximum_fusion.1.refs_1_, bf16[4,272,512]{2,1,0:T(8,128)(2,1)} %collective-permute-done.11.refs_2_, ...), custom_call_target="tpu_custom_call" | custom-call | flops 4294967296 | bytes 2097152 | tf_op jit(solution)/shard_map/pallas_call | solution.py:92
  135.0 22.5 %shard_map.206 = (bf16[128,2048]{1,0:T(8,128)(2,1)}, bf16[128,2048]{1,0:T(8,128)(2,1)}, f32[1,32,128]{2,1,0:T(8,128)}) custom-call(f32[256,2048]{1,0:T(8,128)} %shard_map.204.refs_0_, bf16[4,272,512]{2,1,0:T(8,128)(2,1)} %pad_maximum_fusion.1.refs_1_, bf16[4,272,512]{2,1,0:T(8,128)(2,1)} %collective-permute-done.11.refs_2_, ...), custom_call_target="tpu_custom_call" | custom-call | flops 4294967296 | bytes 2097152 | tf_op jit(solution)/shard_map/pallas_call | solution.py:92
  167.9 9.2 %shard_map.207 = f32[256,2048]{1,0:T(8,128)} custom-call(s32[4]{0:T(128)} %pad_add_fusion.refs_0_, bf16[256,2048]{1,0:T(8,128)(2,1)} %copy-done.13, bf16[512,2048]{1,0:T(8,128)(2,1)} %refs_2_.8, bf16[1024,2048]{1,0:T(8,128)(2,1)} %all-gather.2.cloned.1.call-done.refs_3_, bf16[1024,2048]{1,0:T(8,128)(2,1)} %collective-permute-done.16.refs_4_), custom_call_target="tpu_custom_call" | custom-call | flops 2147483648 | bytes 11534336 | tf_op jit(solution)/shard_map/pallas_call | solution.py:92
  197.3 18.1 %collective-permute-done.20.refs_2_ = bf16[256,2048]{1,0:T(8,128)(2,1)S(1)} collective-permute-done((bf16[256,2048]{1,0:T(8,128)(2,1)S(1)}, bf16[256,2048]{1,0:T(8,128)(2,1)S(1)}, u32[]{:S(2)}, u32[]{:S(2)}) %collective-permute-start.20) | collective-permute-done | bytes 1048608 | tf_op jit(solution)/shard_map/ppermute | solution.py:736
  249.1 34.3 %shard_map.208 = (bf16[1024,1408]{1,0:T(8,128)(2,1)}, bf16[1024,2816]{1,0:T(8,128)(2,1)}, bf16[1024,2048]{1,0:T(8,128)(2,1)}, bf16[1024,2048]{1,0:T(8,128)(2,1)}) custom-call(s32[4]{0:T(128)} %pad_add_fusion.refs_0_, bf16[256,2048]{1,0:T(8,128)(2,1)} %copy-done.35, bf16[256,2048]{1,0:T(8,128)(2,1)} %copy-done.52, bf16[256,2048]{1,0:T(8,128)(2,1)} %copy-done.53, ...), custom_call_target="tpu_custom_call" | custom-call | flops 17716740096 | bytes 34340864 | tf_op jit(solution)/shard_map/pallas_call | solution.py:92
  307.7 19.9 %shard_map.209 = (bf16[256,2048]{1,0:T(8,128)(2,1)}, bf16[256,2048]{1,0:T(8,128)(2,1)}, bf16[256,2048]{1,0:T(8,128)(2,1)}, bf16[256,2048]{1,0:T(8,128)(2,1)}) custom-call(s32[4]{0:T(128)} %pad_add_fusion.refs_0_, bf16[1024,2816]{1,0:T(8,128)(2,1)} %get-tuple-element.214.refs_1_.refs_2_, bf16[512,5632]{1,0:T(8,128)(2,1)} %refs_2_.7, ...), custom_call_target="tpu_custom_call" | custom-call | flops 11811160064 | bytes 21495808 | tf_op jit(solution)/shard_map/pallas_call | solution.py:92
  331.9 13.5 %shard_map.210 = bf16[1024,2816]{1,0:T(8,128)(2,1)} custom-call(s32[4]{0:T(128)} %pad_add_fusion.refs_0_, bf16[1024,2048]{1,0:T(8,128)(2,1)} %get-tuple-element.221.refs_1_, bf16[1024,2816]{1,0:T(8,128)(2,1)} %get-tuple-element.214.refs_1_.refs_2_, bf16[256,2048]{1,0:T(8,128)(2,1)} %get-tuple-element.219.refs_3_), custom_call_target="tpu_custom_call" | custom-call | flops 5905580032 | bytes 13631488 | tf_op jit(solution)/shard_map/pallas_call | solution.py:83
  360.8 15.0 %shard_map.211 = (bf16[256,2816]{1,0:T(8,128)(2,1)}, bf16[256,2816]{1,0:T(8,128)(2,1)}, bf16[256,2816]{1,0:T(8,128)(2,1)}, bf16[256,2816]{1,0:T(8,128)(2,1)}) custom-call(s32[4]{0:T(128)} %pad_add_fusion.refs_0_, bf16[1024,2048]{1,0:T(8,128)(2,1)} %get-tuple-element.221.refs_1_, bf16[1024,2816]{1,0:T(8,128)(2,1)} %get-tuple-element.214.refs_1_.refs_2_, ...), custom_call_target="tpu_custom_call" | custom-call | flops 5905580032 | bytes 13631488 | tf_op jit(solution)/shard_map/pallas_call | solution.py:83
  436.4 15.3 %shard_map.213 = (bf16[128,1024]{1,0:T(8,128)(2,1)}, bf16[4,128,256]{2,1,0:T(8,128)(2,1)}, bf16[4,128,256]{2,1,0:T(8,128)(2,1)}) custom-call(bf16[128,2048]{1,0:T(8,128)(2,1)} %get-tuple-element.238.refs_0_, bf16[4,272,512]{2,1,0:T(8,128)(2,1)} %pad_maximum_fusion.1.refs_1_, bf16[4,272,512]{2,1,0:T(8,128)(2,1)} %collective-permute-done.11.refs_2_, ...), custom_call_target="tpu_custom_call" | custom-call | flops 1342177280 | bytes 1048576 | tf_op jit(solution)/shard_map/pallas_call | solution.py:92
  451.6 15.2 %shard_map.214 = (bf16[128,1024]{1,0:T(8,128)(2,1)}, bf16[4,128,256]{2,1,0:T(8,128)(2,1)}, bf16[4,128,256]{2,1,0:T(8,128)(2,1)}) custom-call(bf16[128,2048]{1,0:T(8,128)(2,1)} %get-tuple-element.238.refs_0_, bf16[4,272,512]{2,1,0:T(8,128)(2,1)} %pad_maximum_fusion.1.refs_1_, bf16[4,272,512]{2,1,0:T(8,128)(2,1)} %collective-permute-done.11.refs_2_, ...), custom_call_target="tpu_custom_call" | custom-call | flops 1342177280 | bytes 1048576 | tf_op jit(solution)/shard_map/pallas_call | solution.py:92
  466.9 15.3 %shard_map.215 = (bf16[128,1024]{1,0:T(8,128)(2,1)}, bf16[4,128,256]{2,1,0:T(8,128)(2,1)}, bf16[4,128,256]{2,1,0:T(8,128)(2,1)}) custom-call(bf16[128,2048]{1,0:T(8,128)(2,1)} %get-tuple-element.199.refs_0_, bf16[4,272,512]{2,1,0:T(8,128)(2,1)} %pad_maximum_fusion.1.refs_1_, bf16[4,272,512]{2,1,0:T(8,128)(2,1)} %collective-permute-done.11.refs_2_, ...), custom_call_target="tpu_custom_call" | custom-call | flops 1342177280 | bytes 1048576 | tf_op jit(solution)/shard_map/pallas_call | solution.py:92
  482.1 15.7 %shard_map.216 = (bf16[128,1024]{1,0:T(8,128)(2,1)}, bf16[4,128,256]{2,1,0:T(8,128)(2,1)}, bf16[4,128,256]{2,1,0:T(8,128)(2,1)}) custom-call(bf16[128,2048]{1,0:T(8,128)(2,1)} %get-tuple-element.199.refs_0_, bf16[4,272,512]{2,1,0:T(8,128)(2,1)} %pad_maximum_fusion.1.refs_1_, bf16[4,272,512]{2,1,0:T(8,128)(2,1)} %collective-permute-done.11.refs_2_, ...), custom_call_target="tpu_custom_call" | custom-call | flops 1342177280 | bytes 1048576 | tf_op jit(solution)/shard_map/pallas_call | solution.py:92
  521.6 12.6 %shard_map.220 = (bf16[256,2048]{1,0:T(8,128)(2,1)}, bf16[256,2048]{1,0:T(8,128)(2,1)}, bf16[256,2048]{1,0:T(8,128)(2,1)}, bf16[256,2048]{1,0:T(8,128)(2,1)}) custom-call(bf16[1024,1408]{1,0:T(8,128)(2,1)} %get-tuple-element.217.refs_0_, bf16[1408,2048]{1,0:T(8,128)(2,1)} %refs_1_.1, f32[256,2048]{1,0:T(8,128)} %shard_map.219.refs_2_), custom_call_target="tpu_custom_call" | custom-call | flops 5905580032 | bytes 12845056 | tf_op jit(solution)/shard_map/pallas_call | solution.py:92
  534.2 31.3 %all-reduce.12.cloned.1.call-done = (bf16[256,2816]{1,0:T(8,128)(2,1)}, bf16[256,2816]{1,0:T(8,128)(2,1)}) async-done(((bf16[256,2816]{1,0:T(8,128)(2,1)}, bf16[256,2816]{1,0:T(8,128)(2,1)}), (bf16[256,2816]{1,0:T(8,128)(2,1)}, bf16[256,2816]{1,0:T(8,128)(2,1)})) %all-reduce.12.cloned.1.call-update) | async-done | bytes 2883600 | tf_op jit(solution)/shard_map/psum | solution.py:1110
  575.5 8.6 shard_map.221
  597.9 15.8 %collective-permute-done.49.refs_2_ = bf16[256,512]{1,0:T(8,128)(2,1)S(1)} collective-permute-done((bf16[256,512]{1,0:T(8,128)(2,1)S(1)}, bf16[256,512]{1,0:T(8,128)(2,1)S(1)}, u32[]{:S(2)}, u32[]{:S(2)}) %collective-permute-start.49) | collective-permute-done | bytes 262176 | tf_op jit(solution)/shard_map/ppermute | solution.py:742
  633.2 8.5 shard_map.224
  678.5 15.6 %collective-permute-done.58 = bf16[256,2048]{1,0:T(8,128)(2,1)} collective-permute-done((bf16[256,2048]{1,0:T(8,128)(2,1)}, bf16[256,2048]{1,0:T(8,128)(2,1)}, u32[]{:S(2)}, u32[]{:S(2)}) %collective-permute-start.58) | collective-permute-done | bytes 1048608 | tf_op jit(solution)/shard_map/ppermute | solution.py:736
  746.0 15.2 %shard_map.228 = (f32[512,5632]{1,0:T(8,128)}, f32[512,5632]{1,0:T(8,128)}) custom-call(s32[4]{0:T(128)} %pad_add_fusion.refs_0_, bf16[256,2816]{1,0:T(8,128)(2,1)} %get-tuple-element.325.refs_1_, bf16[256,2816]{1,0:T(8,128)(2,1)} %collective-permute-done.71.refs_2_, bf16[256,2816]{1,0:T(8,128)(2,1)} %get-tuple-element.326.refs_3_, ...), custom_call_target="tpu_custom_call" | custom-call | bytes 34603008 | tf_op jit(solution)/shard_map/pallas_call | solution.py:92
  771.7 63.5 %all-reduce.10.cloned.1.call-done = (bf16[256,2048]{1,0:T(8,128)(2,1)}, bf16[256,2048]{1,0:T(8,128)(2,1)}, bf16[256,640]{1,0:T(8,128)(2,1)}) async-done(((bf16[256,2048]{1,0:T(8,128)(2,1)}, bf16[256,2048]{1,0:T(8,128)(2,1)}, bf16[256,640]{1,0:T(8,128)(2,1)}), (bf16[256,2048]{1,0:T(8,128)(2,1)}, bf16[256,2048]{1,0:T(8,128)(2,1)}, bf16[256,640]{1,0:T(8,128)(2,1)})) %all-reduce.10.cloned.1.call-update) | async-done | bytes 2424848 | tf_op jit(solution)/shard_map/psum | solution.py:1110
  (433 shorter events, 415.5 us)
Async XLA Ops:
  7.2 153.2 %all-gather.2.cloned.1.call-start = ((), (), s32[]{:S(2)}) async-start(), calls=%async_computation | async-start | bytes 5242880 | tf_op jit(solution)/shard_map/all_gather | solution.py:966
  34.1 30.8 %collective-permute-start.4 = (bf16[256,2048]{1,0:T(8,128)(2,1)}, bf16[256,2048]{1,0:T(8,128)(2,1)S(1)}, u32[]{:S(2)}, u32[]{:S(2)}) collective-permute-start(bf16[256,2048]{1,0:T(8,128)(2,1)} %get-tuple-element.184), channel_id=1, source_target_pairs={{0,8},{8,0},{16,24},{24,16},{1,9},{9,1},{17,25},{25,17},{2,10},{10... | collective-permute-start | bytes 3145736 | tf_op jit(solution)/shard_map/ppermute | solution.py:736
  35.3 46.4 %collective-permute-start.5 = (bf16[256,2048]{1,0:T(8,128)(2,1)}, bf16[256,2048]{1,0:T(8,128)(2,1)S(1)}, u32[]{:S(2)}, u32[]{:S(2)}) collective-permute-start(bf16[256,2048]{1,0:T(8,128)(2,1)} %get-tuple-element.184), channel_id=1, source_target_pairs={{0,16},{8,24},{16,0},{24,8},{1,17},{9,25},{17,1},{25,9},{2,18},{10... | collective-permute-start | bytes 3145736 | tf_op jit(solution)/shard_map/ppermute | solution.py:736
  36.1 47.1 %collective-permute-start.6 = (bf16[256,2048]{1,0:T(8,128)(2,1)}, bf16[256,2048]{1,0:T(8,128)(2,1)S(1)}, u32[]{:S(2)}, u32[]{:S(2)}) collective-permute-start(bf16[256,2048]{1,0:T(8,128)(2,1)} %get-tuple-element.184), channel_id=1, source_target_pairs={{0,24},{8,16},{16,8},{24,0},{1,25},{9,17},{17,9},{25,1},{2,26},{10... | collective-permute-start | bytes 3145736 | tf_op jit(solution)/shard_map/ppermute | solution.py:736
  84.1 481.4 %all-reduce.12.cloned.1.call-start = ((), (), s32[]{:S(2)}) async-start(), calls=%async_computation.3 | async-start | bytes 5767168 | tf_op jit(solution)/shard_map/psum | solution.py:1110
  92.8 36.9 %collective-permute-start.12 = (bf16[64,2816]{1,0:T(8,128)(2,1)}, bf16[64,2816]{1,0:T(8,128)(2,1)}, u32[]{:S(2)}, u32[]{:S(2)}) collective-permute-start(bf16[64,2816]{1,0:T(8,128)(2,1)} %pad_maximum_fusion.11), channel_id=1, source_target_pairs={{0,8},{8,0},{16,24},{24,16},{1,9},{9,1},{17,25},{25,17},{2,10},{10... | collective-permute-start | bytes 1081352 | tf_op jit(solution)/shard_map/ppermute | solution.py:736
  93.9 35.8 %collective-permute-start.13 = (bf16[64,2816]{1,0:T(8,128)(2,1)}, bf16[64,2816]{1,0:T(8,128)(2,1)S(1)}, u32[]{:S(2)}, u32[]{:S(2)}) collective-permute-start(bf16[64,2816]{1,0:T(8,128)(2,1)} %pad_maximum_fusion.12), channel_id=1, source_target_pairs={{0,16},{8,24},{16,0},{24,8},{1,17},{9,25},{17,1},{25,9},{2,18},{10... | collective-permute-start | bytes 1081352 | tf_op jit(solution)/shard_map/ppermute | solution.py:736
  95.4 34.2 %collective-permute-start.14 = (bf16[64,2816]{1,0:T(8,128)(2,1)}, bf16[64,2816]{1,0:T(8,128)(2,1)S(1)}, u32[]{:S(2)}, u32[]{:S(2)}) collective-permute-start(bf16[64,2816]{1,0:T(8,128)(2,1)} %pad_maximum_fusion.13), channel_id=1, source_target_pairs={{0,24},{8,16},{16,8},{24,0},{1,25},{9,17},{17,9},{25,1},{2,26},{10... | collective-permute-start | bytes 1081352 | tf_op jit(solution)/shard_map/ppermute | solution.py:736
  219.2 29.9 %collective-permute-start.27 = (bf16[768,2816]{1,0:T(8,128)(2,1)}, bf16[768,2816]{1,0:T(8,128)(2,1)}, u32[]{:S(2)}, u32[]{:S(2)}) collective-permute-start(bf16[768,2816]{1,0:T(8,128)(2,1)} %constant_dynamic-update-slice_fusion.7), channel_id=1, source_target_pairs={{0,1},{1,0},{2,3},{3,2},{4,5},{5,4},{6,7},{7,6},{8,9},{9,8},{10,11... | collective-permute-start | bytes 12976136 | tf_op jit(solution)/shard_map/ppermute | solution.py:739
  305.3 40.1 %collective-permute-start.31 = (bf16[704,1024]{1,0:T(8,128)(2,1)}, bf16[704,1024]{1,0:T(8,128)(2,1)}, u32[]{:S(2)}, u32[]{:S(2)}) collective-permute-start(bf16[704,1024]{1,0:T(8,128)(2,1)} %get-tuple-element.369.refs_9_), channel_id=1, source_target_pairs={{0,2},{1,3},{6,4},{7,5},{8,10},{9,11},{14,12},{15,13},{16,18},{17,... | collective-permute-start | bytes 4325384 | tf_op jit(solution)/shard_map/ppermute | solution.py:742
  345.5 33.4 %collective-permute-start.36 = (bf16[704,1024]{1,0:T(8,128)(2,1)}, bf16[704,1024]{1,0:T(8,128)(2,1)}, u32[]{:S(2)}, u32[]{:S(2)}) collective-permute-start(bf16[704,1024]{1,0:T(8,128)(2,1)} %get-tuple-element.368.refs_10_.refs_5_), channel_id=1, source_target_pairs={{0,2},{1,3},{6,4},{7,5},{8,10},{9,11},{14,12},{15,13},{16,18},{17,... | collective-permute-start | bytes 4325384 | tf_op jit(solution)/shard_map/ppermute | solution.py:742
  385.7 33.0 %collective-permute-start.37 = (bf16[256,2816]{1,0:T(8,128)(2,1)}, bf16[256,2816]{1,0:T(8,128)(2,1)}, u32[]{:S(2)}, u32[]{:S(2)}) collective-permute-start(bf16[256,2816]{1,0:T(8,128)(2,1)} %get-tuple-element.234), channel_id=1, source_target_pairs={{0,8},{8,0},{16,24},{24,16},{1,9},{9,1},{17,25},{25,17},{2,10},{10... | collective-permute-start | bytes 4325384 | tf_op jit(solution)/shard_map/ppermute | solution.py:736
  390.1 36.0 %collective-permute-start.38 = (bf16[704,1024]{1,0:T(8,128)(2,1)}, bf16[704,1024]{1,0:T(8,128)(2,1)}, u32[]{:S(2)}, u32[]{:S(2)}) collective-permute-start(bf16[704,1024]{1,0:T(8,128)(2,1)} %add_convert_fusion.3), channel_id=1, source_target_pairs={{2,0},{3,1},{4,6},{5,7},{10,8},{11,9},{12,14},{13,15},{18,16},{19,... | collective-permute-start | bytes 4325384 | tf_op jit(solution)/shard_map/ppermute | solution.py:742
  394.6 31.5 %collective-permute-start.39 = (bf16[704,1024]{1,0:T(8,128)(2,1)}, bf16[704,1024]{1,0:T(8,128)(2,1)}, u32[]{:S(2)}, u32[]{:S(2)}) collective-permute-start(bf16[704,1024]{1,0:T(8,128)(2,1)} %add_convert_fusion.2), channel_id=1, source_target_pairs={{2,4},{3,5},{4,2},{5,3},{10,12},{11,13},{12,10},{13,11},{18,20},{1... | collective-permute-start | bytes 4325384 | tf_op jit(solution)/shard_map/ppermute | solution.py:742
  426.2 309.1 %all-reduce.8.cloned.1.call-start = ((), (), s32[]{:S(2)}) async-start(), calls=%async_computation.1 | async-start | bytes 5767168 | tf_op jit(solution)/shard_map/psum | solution.py:1110
  426.2 107.9 %collective-permute-start.40 = (bf16[256,2816]{1,0:T(8,128)(2,1)}, bf16[256,2816]{1,0:T(8,128)(2,1)}, u32[]{:S(2)}, u32[]{:S(2)}) collective-permute-start(bf16[256,2816]{1,0:T(8,128)(2,1)} %get-tuple-element.254), channel_id=1, source_target_pairs={{0,16},{8,24},{16,0},{24,8},{1,17},{9,25},{17,1},{25,9},{2,18},{10... | collective-permute-start | bytes 4325384 | tf_op jit(solution)/shard_map/ppermute | solution.py:736
  427.0 107.1 %collective-permute-start.41 = (bf16[256,2816]{1,0:T(8,128)(2,1)}, bf16[256,2816]{1,0:T(8,128)(2,1)}, u32[]{:S(2)}, u32[]{:S(2)}) collective-permute-start(bf16[256,2816]{1,0:T(8,128)(2,1)} %get-tuple-element.255), channel_id=1, source_target_pairs={{0,24},{8,16},{16,8},{24,0},{1,25},{9,17},{17,9},{25,1},{2,26},{10... | collective-permute-start | bytes 4325384 | tf_op jit(solution)/shard_map/ppermute | solution.py:736
  432.4 101.8 %collective-permute-start.42 = (bf16[704,1024]{1,0:T(8,128)(2,1)}, bf16[704,1024]{1,0:T(8,128)(2,1)}, u32[]{:S(2)}, u32[]{:S(2)}) collective-permute-start(bf16[704,1024]{1,0:T(8,128)(2,1)} %add_convert_fusion.1.refs_9_), channel_id=1, source_target_pairs={{2,0},{3,1},{4,6},{5,7},{10,8},{11,9},{12,14},{13,15},{18,16},{19,... | collective-permute-start | bytes 4325384 | tf_op jit(solution)/shard_map/ppermute | solution.py:742
  618.1 80.7 %collective-permute-start.63 = (bf16[704,1024]{1,0:T(8,128)(2,1)}, bf16[704,1024]{1,0:T(8,128)(2,1)}, u32[]{:S(2)}, u32[]{:S(2)}) collective-permute-start(bf16[704,1024]{1,0:T(8,128)(2,1)} %broadcast_select_fusion.1.refs_8_.refs_1_), channel_id=1, source_target_pairs={{0,1},{1,0},{2,3},{3,2},{4,5},{5,4},{6,7},{7,6},{8,9},{9,8},{10,11... | collective-permute-start | bytes 4325384 | tf_op jit(solution)/shard_map/ppermute | solution.py:739
  621.9 213.3 %all-reduce.10.cloned.1.call-start = ((), (), s32[]{:S(2)}) async-start(), calls=%async_computation.2 | async-start | bytes 4849664 | tf_op jit(solution)/shard_map/psum | solution.py:1110
  632.7 76.4 %collective-permute-start.64 = (bf16[704,1024]{1,0:T(8,128)(2,1)}, bf16[704,1024]{1,0:T(8,128)(2,1)}, u32[]{:S(2)}, u32[]{:S(2)}) collective-permute-start(bf16[704,1024]{1,0:T(8,128)(2,1)} %broadcast_select_fusion.refs_3_), channel_id=1, source_target_pairs={{0,1},{1,0},{2,3},{3,2},{4,5},{5,4},{6,7},{7,6},{8,9},{9,8},{10,11... | collective-permute-start | bytes 4325384 | tf_op jit(solution)/shard_map/ppermute | solution.py:739
  675.6 29.7 %collective-permute-start.65 = (bf16[128,2048]{1,0:T(8,128)(2,1)}, bf16[128,2048]{1,0:T(8,128)(2,1)S(1)}, u32[]{:S(2)}, u32[]{:S(2)}) collective-permute-start(bf16[128,2048]{1,0:T(8,128)(2,1)} %get-tuple-element.375), channel_id=1, source_target_pairs={{0,8},{8,0},{16,24},{24,16},{1,9},{9,1},{17,25},{25,17},{2,10},{10... | collective-permute-start | bytes 1572872 | tf_op jit(solution)/shard_map/ppermute | solution.py:736
  705.3 37.8 %collective-permute-start.71 = (bf16[256,2816]{1,0:T(8,128)(2,1)}, bf16[256,2816]{1,0:T(8,128)(2,1)}, u32[]{:S(2)}, u32[]{:S(2)}) collective-permute-start(bf16[256,2816]{1,0:T(8,128)(2,1)} %get-tuple-element.325.refs_1_), channel_id=1, source_target_pairs={{0,1},{1,0},{2,3},{3,2},{4,5},{5,4},{6,7},{7,6},{8,9},{9,8},{10,11... | collective-permute-start | bytes 4325384 | tf_op jit(solution)/shard_map/ppermute | solution.py:739
  709.0 35.5 %collective-permute-start.72 = (bf16[256,2816]{1,0:T(8,128)(2,1)}, bf16[256,2816]{1,0:T(8,128)(2,1)}, u32[]{:S(2)}, u32[]{:S(2)}) collective-permute-start(bf16[256,2816]{1,0:T(8,128)(2,1)} %get-tuple-element.326.refs_3_), channel_id=1, source_target_pairs={{0,1},{1,0},{2,3},{3,2},{4,5},{5,4},{6,7},{7,6},{8,9},{9,8},{10,11... | collective-permute-start | bytes 4325384 | tf_op jit(solution)/shard_map/ppermute | solution.py:739
  (121 other events, 1486.3 us)
Sparse Core Ops, SparseCore 0:
  84.2 68.7 all-gather.1
  426.3 139.1 all-reduce.11
  622.0 113.1 all-reduce.7
  737.7 97.4 all-reduce.9
